TPU v7x, 256 devices: a whole 4x4x8 slice. The times are simulated.
256 devices in a mesh: con: 8 (over x, core), tile: 32 (over y, z).
Axes of the slice: x: 4, y: 4, z: 8, core: 2. Of those that a mesh axis runs over, the one named last changes fastest.
Arguments:
- first_guess: float32 [8, 2, 512, 2048], P('con', None, 'tile'), may hold values from -4 to 4
- misfit: float32 [8, 2, 512, 2048], P('con', None, 'tile'), may hold values from -6 to 6
- innovations: float32 [8, 2, 8192], P('con', None, 'tile'), may hold values from -6 to 6
- obs_cells: int32 [8192], P('tile'), may hold values from 0 to 32767
- depth: float32 [512, 2048], P('tile'), may hold values from 1 to 8
- base_speed: float32 [512, 2048], P('tile'), may hold values from 0.1 to 1
- frequency: float32 [8], P('con'), may hold values from 0.5 to 3
Outputs:
- adjoint: float32 [8, 2, 512, 2048], P('con', None, 'tile')
Inputs may be any that keep to these rules, and one draw needn't show every extreme that they name: `obs_cells`: an observation's cell lies in the tile that holds it; several observations may share a cell.
All inputs are finite; a program needn't handle non-finite values.
Results may differ from a plain program's by a relative error of at most 0.00002.
Values sent between devices are 32-bit elements; how exact they have to be, the bound alone decides.
No kernel may reach another device: no remote copies, remote signals or barrier semaphores. Data moves between devices by JAX's collectives and lax.ppermute only.
A program may use at most 64 MiB of HBM per device.

v0:
```python
import jax
import jax.numpy as jnp
from jax import lax
from jax.sharding import PartitionSpec as P

SWEEPS = 16


DRAG_COEF = 0.5
SHIFT_SIGMA = 0.1


def extended_2(cells, sides, width):
    for axis, dim in sides:
        count = lax.axis_size(axis)
        ends = count - 1
        head = lax.slice_in_dim(cells, 0, width, axis=dim)
        tail = lax.slice_in_dim(cells, cells.shape[dim] - width, cells.shape[dim], axis=dim)
        cells = jnp.concatenate(
            [
                lax.ppermute(tail, axis, [(i, (i + 1) % count) for i in range(ends)]),
                cells,
                lax.ppermute(head, axis, [((i + 1) % count, i) for i in range(ends)]),
            ],
            axis=dim,
        )
    return cells


def spread(value, axis, source):
    kept = jnp.where(lax.axis_index(axis) == source, value, 0).astype(value.dtype)
    return lax.psum(kept, axis)


def coefficients(speed_sq, depth_cells, angular):
    drag = DRAG_COEF * jnp.sqrt(speed_sq)
    modulus = drag * drag + angular * angular
    gain_real = depth_cells * drag / modulus
    gain_imag = depth_cells * angular / modulus
    diag_real = SHIFT_SIGMA + 4.0 * gain_real
    diag_imag = angular + 4.0 * gain_imag
    norm_sq = diag_real * diag_real + diag_imag * diag_imag
    return (gain_real, gain_imag, diag_real / norm_sq, -diag_imag / norm_sq)


def neighbours(extended):
    middle = extended[:, 1:-1]
    along = extended[:, 2:] + extended[:, :-2]
    padded = jnp.pad(middle, ((0, 0), (0, 0), (1, 1)))
    across = padded[:, :, 2:] + padded[:, :, :-2]
    return along + across


def relax(neighbour_sum, forcing, coefficient):
    gain_real, gain_imag, inv_real, inv_imag = coefficient
    numer_real = forcing[0] + gain_real * neighbour_sum[0] - gain_imag * neighbour_sum[1]
    numer_imag = forcing[1] + gain_real * neighbour_sum[1] + gain_imag * neighbour_sum[0]
    return jnp.stack(
        [
            numer_real * inv_real - numer_imag * inv_imag,
            numer_real * inv_imag + numer_imag * inv_real,
        ]
    )


def squared(field):
    return field[0] * field[0] + field[1] * field[1]


def settle(start_field, forcing, speed_sq, depth, angular):
    coefficient = coefficients(speed_sq, depth, angular)

    def edge_step(sweep, current):
        extended = extended_2(current, (("tile", 1),), 1)
        return relax(neighbours(extended), forcing, coefficient)

    return lax.fori_loop(0, SWEEPS, edge_step, start_field)


def body(first_guess, misfit, innovations, obs_cells, depth, base_speed, frequency):
    count = lax.axis_size("con")
    con_index = lax.axis_index("con")
    start_field = first_guess[0]
    tile_rows = start_field.shape[1]
    lane_count = start_field.shape[2]
    forcing = (
        misfit[0]
        .reshape(2, -1)
        .at[:, obs_cells]
        .add(innovations[0])
        .reshape(2, tile_rows, lane_count)
    )
    angular = frequency[0]
    speed_total = base_speed + lax.psum(squared(start_field), "con")
    current = start_field
    for section in range(count):
        own_square = squared(current)
        speed_sq = speed_total - own_square
        solved = settle(current, forcing, speed_sq, depth, angular)
        current = jnp.where(con_index == section, solved, current)
        if section + 1 < count:
            change = squared(current) - own_square
            speed_total = speed_total + spread(change, "con", section)
    return current[None]


def solution(mesh):
    placed = (
        P("con", None, "tile", None),
        P("con", None, "tile", None),
        P("con", None, "tile"),
        P("tile"),
        P("tile", None),
        P("tile", None),
        P("con"),
    )
    return jax.shard_map(
        body, mesh=mesh, in_specs=placed, out_specs=P("con", None, "tile", None), check_vma=False
    )
```

profile of v0, /device:TPU:7, one launch (start us, length us, event | category | flops | bytes accessed | tf_op | source)
XLA Modules:
  0.0 1796.3 jit_solution(3342870284634371277)
XLA Ops:
  9.9 9.5 copy.8
  19.5 13.3 scatter_fusion
  32.9 10.0 copy.10
  43.5 32.0 %all-reduce.17.cloned.1.call-done = f32[16,2048]{1,0:T(8,128)} async-done(((f32[16,2048]{1,0:T(8,128)}), f32[16,2048]{1,0:T(8,128)}) %all-reduce.17.cloned.1.call-update) | async-done | bytes 131088 | tf_op jit(solution)/shard_map/psum | solution.py:94
  76.6 138.8 %while.96 = (s32[]{:T(128)}, f32[2,16,2048]{2,1,0:T(8,128)S(1)}, f32[2,16,2048]{2,1,0:T(8,128)S(1)}, f32[16,2048]{1,0:T(8,128)S(1)}, f32[16,2048]{1,0:T(8,128)S(...) while((s32[]{:T(128)}, f32[2,16,2048]{2,1,0:T(8,128)S(1)}, ...), condition=%wide.region_3.4_spmd, body=%wide.region_2.3_spmd.sunk | while | flops 851970 | bytes 3375269 | solution.py:77
  89.2 4.0 collective-permute-done.1
  93.7 4.6 collective-permute-start
  152.6 4.1 collective-permute-start
  161.6 4.0 collective-permute-start
  179.4 4.5 collective-permute-start
  197.7 4.0 collective-permute-start
  206.6 4.0 collective-permute-start
  216.3 84.0 %all-reduce.19.cloned.1.call-done = f32[16,2048]{1,0:T(8,128)} async-done(((f32[16,2048]{1,0:T(8,128)}), f32[16,2048]{1,0:T(8,128)}) %all-reduce.19.cloned.1.call-update) | async-done | bytes 131088 | tf_op jit(solution)/shard_map/psum | solution.py:32
  301.4 138.8 %while.97 = (s32[]{:T(128)}, f32[2,16,2048]{2,1,0:T(8,128)S(1)}, f32[2,16,2048]{2,1,0:T(8,128)S(1)}, f32[16,2048]{1,0:T(8,128)S(1)}, f32[16,2048]{1,0:T(8,128)S(...) while((s32[]{:T(128)}, f32[2,16,2048]{2,1,0:T(8,128)S(1)}, ...), condition=%wide.region_6.7_spmd, body=%wide.region_5.6_spmd.sunk | while | flops 851970 | bytes 3375269 | solution.py:77
  314.0 4.0 collective-permute-done.3
  318.4 4.6 collective-permute-start.2
  377.4 4.1 collective-permute-start.2
  386.3 4.0 collective-permute-start.2
  404.1 4.5 collective-permute-start.2
  431.4 4.0 collective-permute-start.2
  441.1 84.0 %all-reduce.21.cloned.1.call-done = f32[16,2048]{1,0:T(8,128)} async-done(((f32[16,2048]{1,0:T(8,128)}), f32[16,2048]{1,0:T(8,128)}) %all-reduce.21.cloned.1.call-update) | async-done | bytes 131088 | tf_op jit(solution)/shard_map/psum | solution.py:32
  526.1 138.8 %while.98 = (s32[]{:T(128)}, f32[2,16,2048]{2,1,0:T(8,128)S(1)}, f32[2,16,2048]{2,1,0:T(8,128)S(1)}, f32[16,2048]{1,0:T(8,128)S(1)}, f32[16,2048]{1,0:T(8,128)S(...) while((s32[]{:T(128)}, f32[2,16,2048]{2,1,0:T(8,128)S(1)}, ...), condition=%wide.region_9.10_spmd, body=%wide.region_8.9_spmd.sunk | while | flops 851970 | bytes 3375269 | solution.py:77
  538.8 4.0 collective-permute-done.5
  543.2 4.6 collective-permute-start.4
  602.1 4.1 collective-permute-start.4
  611.1 4.0 collective-permute-start.4
  628.9 4.5 collective-permute-start.4
  647.2 4.0 collective-permute-start.4
  656.1 4.0 collective-permute-start.4
  665.8 84.0 %all-reduce.23.cloned.1.call-done = f32[16,2048]{1,0:T(8,128)} async-done(((f32[16,2048]{1,0:T(8,128)}), f32[16,2048]{1,0:T(8,128)}) %all-reduce.23.cloned.1.call-update) | async-done | bytes 131088 | tf_op jit(solution)/shard_map/psum | solution.py:32
  750.9 138.8 %while.99 = (s32[]{:T(128)}, f32[2,16,2048]{2,1,0:T(8,128)S(1)}, f32[2,16,2048]{2,1,0:T(8,128)S(1)}, f32[16,2048]{1,0:T(8,128)S(1)}, f32[16,2048]{1,0:T(8,128)S(...) while((s32[]{:T(128)}, f32[2,16,2048]{2,1,0:T(8,128)S(1)}, ...), condition=%wide.region_12.13_spmd, body=%wide.region_11.12_spmd.sunk | while | flops 851970 | bytes 3375269 | solution.py:77
  763.5 4.0 collective-permute-done.7
  767.9 4.6 collective-permute-start.6
  826.9 4.1 collective-permute-start.6
  835.8 4.0 collective-permute-start.6
  853.6 4.5 collective-permute-start.6
  871.9 4.0 collective-permute-start.6
  880.8 4.0 collective-permute-start.6
  890.5 84.0 %all-reduce.25.cloned.1.call-done = f32[16,2048]{1,0:T(8,128)} async-done(((f32[16,2048]{1,0:T(8,128)}), f32[16,2048]{1,0:T(8,128)}) %all-reduce.25.cloned.1.call-update) | async-done | bytes 131088 | tf_op jit(solution)/shard_map/psum | solution.py:32
  975.6 138.8 %while.100 = (s32[]{:T(128)}, f32[2,16,2048]{2,1,0:T(8,128)S(1)}, f32[2,16,2048]{2,1,0:T(8,128)S(1)}, f32[16,2048]{1,0:T(8,128)S(1)}, f32[16,2048]{1,0:T(8,128)S...) while((s32[]{:T(128)}, f32[2,16,2048]{2,1,0:T(8,128)S(1)}, ...), condition=%wide.region_15.16_spmd, body=%wide.region_14.15_spmd.sunk | while | flops 851970 | bytes 3375269 | solution.py:77
  988.2 4.0 collective-permute-done.9
  992.7 4.6 collective-permute-start.8
  1051.6 4.1 collective-permute-start.8
  1078.4 4.5 collective-permute-start.8
  1096.7 4.0 collective-permute-start.8
  1115.3 84.0 %all-reduce.27.cloned.1.call-done = f32[16,2048]{1,0:T(8,128)} async-done(((f32[16,2048]{1,0:T(8,128)}), f32[16,2048]{1,0:T(8,128)}) %all-reduce.27.cloned.1.call-update) | async-done | bytes 131088 | tf_op jit(solution)/shard_map/psum | solution.py:32
  1200.4 138.8 %while.101 = (s32[]{:T(128)}, f32[2,16,2048]{2,1,0:T(8,128)S(1)}, f32[2,16,2048]{2,1,0:T(8,128)S(1)}, f32[16,2048]{1,0:T(8,128)S(1)}, f32[16,2048]{1,0:T(8,128)S...) while((s32[]{:T(128)}, f32[2,16,2048]{2,1,0:T(8,128)S(1)}, ...), condition=%wide.region_18.19_spmd, body=%wide.region_17.18_spmd.sunk | while | flops 851970 | bytes 3375269 | solution.py:77
  1213.0 4.0 collective-permute-done.11
  1217.4 4.6 collective-permute-start.10
  1276.4 4.1 collective-permute-start.10
  1285.3 4.0 collective-permute-start.10
  1303.1 4.5 collective-permute-start.10
  1340.0 84.0 %all-reduce.29.cloned.1.call-done = f32[16,2048]{1,0:T(8,128)} async-done(((f32[16,2048]{1,0:T(8,128)}), f32[16,2048]{1,0:T(8,128)}) %all-reduce.29.cloned.1.call-update) | async-done | bytes 131088 | tf_op jit(solution)/shard_map/psum | solution.py:32
  1425.1 138.8 %while.102 = (s32[]{:T(128)}, f32[2,16,2048]{2,1,0:T(8,128)S(1)}, f32[2,16,2048]{2,1,0:T(8,128)S(1)}, f32[16,2048]{1,0:T(8,128)S(1)}, f32[16,2048]{1,0:T(8,128)S...) while((s32[]{:T(128)}, f32[2,16,2048]{2,1,0:T(8,128)S(1)}, ...), condition=%wide.region_21.22_spmd, body=%wide.region_20.21_spmd.sunk | while | flops 851970 | bytes 3375269 | solution.py:77
  1437.7 4.0 collective-permute-done.13
  1442.2 4.6 collective-permute-start.12
  1501.1 4.1 collective-permute-start.12
  1527.9 4.5 collective-permute-start.12
  1564.7 84.0 %all-reduce.31.cloned.1.call-done = f32[16,2048]{1,0:T(8,128)} async-done(((f32[16,2048]{1,0:T(8,128)}), f32[16,2048]{1,0:T(8,128)}) %all-reduce.31.cloned.1.call-update) | async-done | bytes 131088 | tf_op jit(solution)/shard_map/psum | solution.py:32
  1649.9 138.8 %while.103 = (s32[]{:T(128)}, f32[2,16,2048]{2,1,0:T(8,128)S(1)}, f32[2,16,2048]{2,1,0:T(8,128)S(1)}, f32[16,2048]{1,0:T(8,128)S(1)}, f32[16,2048]{1,0:T(8,128)S...) while((s32[]{:T(128)}, f32[2,16,2048]{2,1,0:T(8,128)S(1)}, ...), condition=%wide.region_24.25_spmd, body=%wide.region_23.24_spmd.sunk | while | flops 851970 | bytes 3375269 | solution.py:77
  1662.5 4.0 collective-permute-done.15
  1666.9 4.6 collective-permute-start.14
  1725.9 4.1 collective-permute-start.14
  1752.6 4.5 collective-permute-start.14
  (1173 shorter events, 931.7 us)
Async XLA Ops:
  6.5 69.0 %all-reduce.17.cloned.1.call-start = ((), (), s32[]{:S(2)}) async-start(), calls=%async_computation | async-start | bytes 262144 | tf_op jit(solution)/shard_map/psum | solution.py:94
  8.2 292.1 %all-reduce.19.cloned.1.call-start = ((), (), s32[]{:S(2)}) async-start(), calls=%async_computation.1 | async-start | bytes 262144 | tf_op jit(solution)/shard_map/psum | solution.py:32
  87.9 5.3 collective-permute-start.1
  93.7 5.9 collective-permute-start
  152.6 5.4 collective-permute-start
  161.6 5.3 collective-permute-start
  179.4 5.8 collective-permute-start
  197.7 5.3 collective-permute-start
  206.6 5.3 collective-permute-start
  216.2 308.8 %all-reduce.21.cloned.1.call-start = ((), (), s32[]{:S(2)}) async-start(), calls=%async_computation.2 | async-start | bytes 262144 | tf_op jit(solution)/shard_map/psum | solution.py:32
  312.7 5.3 collective-permute-start.3
  318.4 5.9 collective-permute-start.2
  377.4 5.4 collective-permute-start.2
  386.3 5.3 collective-permute-start.2
  404.1 5.8 collective-permute-start.2
  422.4 5.3 collective-permute-start.2
  431.4 5.3 collective-permute-start.2
  441.0 308.8 %all-reduce.23.cloned.1.call-start = ((), (), s32[]{:S(2)}) async-start(), calls=%async_computation.3 | async-start | bytes 262144 | tf_op jit(solution)/shard_map/psum | solution.py:32
  537.4 5.3 collective-permute-start.5
  543.2 5.9 collective-permute-start.4
  602.1 5.4 collective-permute-start.4
  611.1 5.3 collective-permute-start.4
  628.9 5.8 collective-permute-start.4
  647.2 5.3 collective-permute-start.4
  656.1 5.3 collective-permute-start.4
  665.7 308.8 %all-reduce.25.cloned.1.call-start = ((), (), s32[]{:S(2)}) async-start(), calls=%async_computation.4 | async-start | bytes 262144 | tf_op jit(solution)/shard_map/psum | solution.py:32
  762.2 5.3 collective-permute-start.7
  767.9 5.9 collective-permute-start.6
  826.9 5.4 collective-permute-start.6
  835.8 5.3 collective-permute-start.6
  853.6 5.8 collective-permute-start.6
  871.9 5.3 collective-permute-start.6
  880.8 5.3 collective-permute-start.6
  890.5 308.8 %all-reduce.27.cloned.1.call-start = ((), (), s32[]{:S(2)}) async-start(), calls=%async_computation.5 | async-start | bytes 262144 | tf_op jit(solution)/shard_map/psum | solution.py:32
  986.9 5.3 collective-permute-start.9
  992.7 5.9 collective-permute-start.8
  1051.6 5.4 collective-permute-start.8
  1060.6 5.3 collective-permute-start.8
  1078.4 5.8 collective-permute-start.8
  1096.7 5.3 collective-permute-start.8
  1105.6 5.3 collective-permute-start.8
  1115.2 308.8 %all-reduce.29.cloned.1.call-start = ((), (), s32[]{:S(2)}) async-start(), calls=%async_computation.6 | async-start | bytes 262144 | tf_op jit(solution)/shard_map/psum | solution.py:32
  1211.7 5.3 collective-permute-start.11
  1217.4 5.9 collective-permute-start.10
  1276.4 5.4 collective-permute-start.10
  1285.3 5.3 collective-permute-start.10
  1303.1 5.8 collective-permute-start.10
  1321.4 5.3 collective-permute-start.10
  1330.3 5.3 collective-permute-start.10
  1340.0 308.8 %all-reduce.31.cloned.1.call-start = ((), (), s32[]{:S(2)}) async-start(), calls=%async_computation.7 | async-start | bytes 262144 | tf_op jit(solution)/shard_map/psum | solution.py:32
  1436.4 5.3 collective-permute-start.13
  1442.2 5.9 collective-permute-start.12
  1501.1 5.4 collective-permute-start.12
  1510.1 5.3 collective-permute-start.12
  1527.9 5.8 collective-permute-start.12
  1546.2 5.3 collective-permute-start.12
  1555.1 5.3 collective-permute-start.12
  1661.2 5.3 collective-permute-start.15
  1666.9 5.9 collective-permute-start.14
  1725.9 5.4 collective-permute-start.14
  1734.8 5.3 collective-permute-start.14
  1752.6 5.8 collective-permute-start.14
  1770.9 5.3 collective-permute-start.14
  1779.8 5.3 collective-permute-start.14
  (204 other events, 1129.2 us)
Sparse Core Ops, SparseCore 0:
  9.7 65.8 all-reduce.16
  216.3 83.9 all-reduce.18
  441.1 83.9 all-reduce.20
  665.8 83.9 all-reduce.22
  890.6 83.9 all-reduce.24
  1115.3 83.9 all-reduce.26
  1340.1 83.9 all-reduce.28
  1564.8 83.9 all-reduce.30
where the time goes:
time: 1830 us; the launch traced here: 1800 us
  waiting for transfers between devices  1040 us (57%)
  starting transfers between devices  641 us (35%)
  other arithmetic  72.8 us (4%)
  local copies, waits for them, and re-layouts  24 us (1%)
    psum x7, waiting for transfers between devices, spread(): return lax.psum(kept, axis)  588 us
    ppermute x128, starting transfers between devices, extended_2(): lax.ppermute(tail, axis, [(i, (i + 1) % count) for i in range(ends)])  476 us
    ppermute x128, waiting for transfers between devices, extended_2(): lax.ppermute(head, axis, [((i + 1) % count, i) for i in range(ends)])  415 us
    ppermute x128, starting transfers between devices, extended_2(): lax.ppermute(head, axis, [((i + 1) % count, i) for i in range(ends)])  165 us
  transfers between devices with their start and end apart: 264, of which 136 were waited for; matrix products, arithmetic and copies ran while one was open for 2% of the time, Pallas kernels for 0%

commit v1 on v0

v1 whole, which is shorter than its diff:
```python
import functools

import jax
import jax.numpy as jnp
from jax import lax
from jax.experimental import pallas as pl
from jax.experimental.pallas import tpu as pltpu
from jax.sharding import PartitionSpec as P

SWEEPS = 16
DRAG_COEF = 0.5
SHIFT_SIGMA = 0.1
ROWS = 16
LANES = 2048
WINDOW = 1152
COLS = WINDOW // 128
SPAN = 3 * ROWS
BOTH = ("con", "tile")


def ring(axis, shift):
    count = lax.axis_size(axis)
    return [(i, (i + shift) % count) for i in range(count)]


def hop_pairs(chip, shift):
    tiles = lax.axis_size("tile")
    return [
        (con * tiles + tile, (con + 2) * tiles + tile + shift)
        for con in (2 * chip, 2 * chip + 1)
        for tile in range(tiles)
        if 0 <= tile + shift < tiles
    ]


def sweep(source, target, gain, offset, lane, first, last):
    for block in range(first, last):
        row = 8 + 8 * block
        inside = pl.ds(8 * block, 8)
        cells = {}

        def rolled(plane, col, shift):
            key = (plane, col % COLS, shift)
            if key not in cells:
                value = source[plane, col % COLS, pl.ds(row, 8), :]
                cells[key] = pltpu.roll(value, shift, 1)
            return cells[key]

        for col in range(COLS):
            total = []
            for plane in range(2):
                up = source[plane, col, pl.ds(row - 1, 8), :]
                down = source[plane, col, pl.ds(row + 1, 8), :]
                left = jnp.where(lane == 0, rolled(plane, col - 1, 1), rolled(plane, col, 1))
                right = jnp.where(
                    lane == 127, rolled(plane, col + 1, 127), rolled(plane, col, 127)
                )
                total.append((up + down) + (left + right))
            gain_real = gain[0, col, inside, :]
            gain_imag = gain[1, col, inside, :]
            target[0, col, pl.ds(row, 8), :] = offset[0, col, inside, :] + (
                gain_real * total[0] - gain_imag * total[1]
            )
            target[1, col, pl.ds(row, 8), :] = offset[1, col, inside, :] + (
                gain_real * total[1] + gain_imag * total[0]
            )


def section_kernel(chip, speeds, carried, *refs):
    count = 3 * speeds + 9 + 1 + (2 if carried else 1)
    ins, (freq_ref,) = refs[: count - 1], refs[count - 1 : count]
    adjoint_ref, sum_ref = refs[count : count + 2]
    next_ref = refs[count + 2] if carried else None
    scratch = refs[count + (3 if carried else 2) :]
    speed_v, field_v, force_v, depth_v, own_v, gain, offset, here, there, out_v, sum_v, sem = scratch
    con = lax.axis_index("con")
    tile = lax.axis_index("tile")
    tiles = lax.axis_size("tile")

    @pl.when(con // 2 == chip)
    def _():
        copies = []
        place = 0
        for term in range(speeds):
            for piece in range(3):
                copies.append((ins[place], speed_v.at[term, piece]))
                place += 1
        for target in (field_v, force_v, depth_v):
            for piece in range(3):
                copies.append((ins[place], target.at[piece]))
                place += 1
        for extra in range(2 if carried else 1):
            copies.append((ins[place], own_v.at[extra]))
            place += 1
        copies = [
            pltpu.make_async_copy(source, target, sem.at[number])
            for number, (source, target) in enumerate(copies)
        ]
        for copy in copies:
            copy.start()
        for copy in copies:
            copy.wait()
        angular = freq_ref[0]
        core = con % 2
        lane = lax.broadcasted_iota(jnp.int32, (8, 128), 1)
        lane2 = lax.broadcasted_iota(jnp.int32, (ROWS, 128), 1)
        nothing = jnp.zeros((8, 128), jnp.float32)
        for col in range(COLS):
            lanes = pl.ds(128 * col, 128)
            for plane in range(2):
                for buffer in (here, there):
                    buffer[plane, col, pl.ds(0, 8), :] = nothing
                    buffer[plane, col, pl.ds(8 + SPAN, 8), :] = nothing
            for piece in range(3):
                speed_sq = speed_v[0, piece, :, lanes]
                if speeds == 2:
                    speed_sq = speed_sq + speed_v[1, piece, :, lanes]
                deep = depth_v[piece, :, lanes]
                drag = DRAG_COEF * jnp.sqrt(speed_sq)
                scaled = deep / (drag * drag + angular * angular)
                gain_real = scaled * drag
                gain_imag = scaled * angular
                diag_real = SHIFT_SIGMA + 4.0 * gain_real
                diag_imag = angular + 4.0 * gain_imag
                inverse = 1.0 / (diag_real * diag_real + diag_imag * diag_imag)
                inv_real = diag_real * inverse
                inv_imag = -diag_imag * inverse
                force_real = force_v[piece, 0, :, lanes]
                force_imag = force_v[piece, 1, :, lanes]
                values = [
                    gain_real * inv_real - gain_imag * inv_imag,
                    gain_real * inv_imag + gain_imag * inv_real,
                    force_real * inv_real - force_imag * inv_imag,
                    force_real * inv_imag + force_imag * inv_real,
                    field_v[piece, 0, :, lanes],
                    field_v[piece, 1, :, lanes],
                ]
                keep = None
                if piece == 0:
                    keep = jnp.broadcast_to(tile > 0, (ROWS, 128))
                if piece == 2:
                    keep = jnp.broadcast_to(tile < tiles - 1, (ROWS, 128))
                edge = None
                if col == 0:
                    edge = (lane2 != 0) | (core == 0)
                if col == COLS - 1:
                    edge = (lane2 != 127) | (core == 1)
                if edge is not None:
                    keep = edge if keep is None else keep & edge
                if keep is not None:
                    values = [jnp.where(keep, value, 0.0) for value in values]
                inside = pl.ds(ROWS * piece, ROWS)
                gain[0, col, inside, :] = values[0]
                gain[1, col, inside, :] = values[1]
                offset[0, col, inside, :] = values[2]
                offset[1, col, inside, :] = values[3]
                here[0, col, pl.ds(8 + ROWS * piece, ROWS), :] = values[4]
                here[1, col, pl.ds(8 + ROWS * piece, ROWS), :] = values[5]

        def both(first, last):
            def step(_, carry):
                sweep(here, there, gain, offset, lane, first, last)
                sweep(there, here, gain, offset, lane, first, last)
                return carry

            return step

        lax.fori_loop(0, SWEEPS // 4, both(0, 6), 0)
        lax.fori_loop(0, SWEEPS // 4, both(1, 5), 0)
        for col in range(COLS):
            lanes = pl.ds(128 * col, 128)
            real = here[0, col, pl.ds(8 + ROWS, ROWS), :]
            imag = here[1, col, pl.ds(8 + ROWS, ROWS), :]
            out_v[0, :, lanes] = real
            out_v[1, :, lanes] = imag
            solved = own_v[0, :, lanes] + (real * real + imag * imag)
            sum_v[0, :, lanes] = solved
            if carried:
                sum_v[1, :, lanes] = solved + own_v[1, :, lanes]
        outs = [(out_v, adjoint_ref), (sum_v.at[0], sum_ref)]
        if carried:
            outs.append((sum_v.at[1], next_ref))
        outs = [
            pltpu.make_async_copy(source, target, sem.at[number])
            for number, (source, target) in enumerate(outs)
        ]
        for copy in outs:
            copy.start()
        for copy in outs:
            copy.wait()


def section(chip, speeds, field, force, deep, own, angular):
    carried = len(own) == 2
    tile_shape = jax.ShapeDtypeStruct((ROWS, WINDOW), jnp.float32)
    pair_shape = jax.ShapeDtypeStruct((2, ROWS, WINDOW), jnp.float32)
    operands = [piece for term in speeds for piece in term] + [*field, *force, *deep, *own]
    anywhere = pl.BlockSpec(memory_space=pl.ANY)
    vmem = lambda *shape: pltpu.VMEM(shape, jnp.float32)
    return pl.pallas_call(
        functools.partial(section_kernel, chip, len(speeds), carried),
        out_shape=[pair_shape, tile_shape] + ([tile_shape] if carried else []),
        in_specs=[anywhere] * len(operands) + [pl.BlockSpec(memory_space=pltpu.SMEM)],
        out_specs=[anywhere] * (3 if carried else 2),
        scratch_shapes=[
            vmem(2, 3, ROWS, WINDOW),
            vmem(3, 2, ROWS, WINDOW),
            vmem(3, 2, ROWS, WINDOW),
            vmem(3, ROWS, WINDOW),
            vmem(2, ROWS, WINDOW),
            vmem(2, COLS, SPAN, 128),
            vmem(2, COLS, SPAN, 128),
            vmem(2, COLS, SPAN + 16, 128),
            vmem(2, COLS, SPAN + 16, 128),
            vmem(2, ROWS, WINDOW),
            vmem(2, ROWS, WINDOW),
            pltpu.SemaphoreType.DMA((len(operands),)),
        ],
        compiler_params=pltpu.CompilerParams(vmem_limit_bytes=16 * 1024 * 1024),
    )(*operands, angular)


def squared(field):
    return field[0] * field[0] + field[1] * field[1]


def beside(value):
    return (
        lax.ppermute(value, "tile", ring("tile", 1)),
        value,
        lax.ppermute(value, "tile", ring("tile", -1)),
    )


def body(first_guess, misfit, innovations, obs_cells, depth, base_speed, frequency):
    chips = lax.axis_size("con") // 2
    con = lax.axis_index("con")
    chip, core = con // 2, con % 2
    swap = [(i, i ^ 1) for i in range(2 * chips)]

    def window(value, side):
        return jnp.where(core == side, value[..., :WINDOW], value[..., -WINDOW:])

    def shared(value):
        mine = window(value, 0)
        got = lax.ppermute(window(value, 1), "con", swap)
        return jnp.where(core == 0, mine, got), jnp.where(core == 0, got, mine)

    field_even, field_odd = shared(first_guess[0])
    lanes = jnp.arange(LANES, dtype=jnp.int32)
    rows = jnp.arange(ROWS, dtype=jnp.int32)
    at_lane = (obs_cells[:, None] % LANES == lanes[None]).astype(jnp.float32)
    at_row = (obs_cells[None] // LANES == rows[:, None]).astype(jnp.float32)
    added = jnp.dot(
        (innovations[0][:, None] * at_row[None]).reshape(2 * ROWS, -1),
        at_lane,
        precision=lax.Precision.HIGHEST,
        preferred_element_type=jnp.float32,
    ).reshape(2, ROWS, LANES)
    force_even, force_odd = shared(misfit[0] + added)
    angular_even, angular_odd = (
        value.reshape(-1)[:1] for value in shared(jnp.broadcast_to(frequency, (8, WINDOW)))
    )
    deep = window(depth, 0)

    square_odd = squared(field_odd)
    square_pair = squared(field_even) + square_odd
    later = window(base_speed, 0)
    for shift in range(1, chips):
        got = lax.ppermute(square_pair, "con", ring("con", -2 * shift))
        later = later + jnp.where(chip + shift < chips, got, 0.0)
    starts = beside(later + square_odd)
    fields_even = beside(field_even)
    forces_even = beside(force_even)
    deeps = beside(deep)
    fields_odd = beside(field_odd)
    forces_odd = beside(force_odd)

    even = jnp.zeros((2, ROWS, WINDOW), jnp.float32)
    odd = even
    passed = None
    for now in range(chips):
        speeds = [starts]
        before = jnp.zeros((ROWS, WINDOW), jnp.float32)
        if passed is not None:
            pieces = [lax.ppermute(passed, BOTH, hop_pairs(now - 1, shift)) for shift in (1, 0, -1)]
            speeds.append(pieces)
            before = pieces[1]
        solved, passed, speed = section(
            now, speeds, fields_even, forces_even, deeps, [before, later], angular_even
        )
        even = jnp.where(chip == now, solved, even)
        solved, passed = section(
            now, [beside(speed)], fields_odd, forces_odd, deeps, [passed], angular_odd
        )
        odd = jnp.where(chip == now, solved, odd)

    own = LANES // 2
    sent = jnp.where(core == 0, odd[..., :own], even[..., -own:])
    got = lax.ppermute(sent, "con", swap)
    result = jnp.where(
        core == 0,
        jnp.concatenate([even[..., :own], got], axis=-1),
        jnp.concatenate([got, odd[..., -own:]], axis=-1),
    )
    return result[None]


def solution(mesh):
    placed = (
        P("con", None, "tile", None),
        P("con", None, "tile", None),
        P("con", None, "tile"),
        P("tile"),
        P("tile", None),
        P("tile", None),
        P("con"),
    )
    return jax.shard_map(
        body, mesh=mesh, in_specs=placed, out_specs=P("con", None, "tile", None), check_vma=False
    )
```

time: 1830 us -> 149 us (0.08); the launches traced: 1800 us -> 149 us
  waiting for transfers between devices: 1040 us -> 55 us
  starting transfers between devices: 641 us -> 68.6 us
  other arithmetic: 72.8 us -> 1.72 us
  local copies, waits for them, and re-layouts: 24 us -> 1.26 us
  Pallas kernels: 0 us -> 19.6 us
    psum x8 -> x0, waiting for transfers between devices: 620 us -> none  [the longest x7 588 us: spread(): return lax.psum(kept, axis)]
    ppermute x256 -> x36, starting transfers between devices: 641 us -> 68.6 us  [the longest x10 42 us: beside(): lax.ppermute(value, 'tile', ring('tile', -1))]
    ppermute x256 -> x36, waiting for transfers between devices: 416 us -> 55 us  [the longest x9 45.1 us: body(): lax.ppermute(passed, BOTH, hop_pairs(now - 1, shift))]
    add x257 -> x2, other arithmetic: 33 us -> 0.08 us  [the longest x1 0.05 us: body(): starts = beside(later + square_odd)]
    pallas_call x0 -> x8, Pallas kernels: none -> 19.6 us  [section(): pl.pallas_call(functools.partial(section_kernel, chip, len(speeds), carri...]
  transfers between devices with their start and end apart: 264 -> 36, of which waited for: 136 -> 7; matrix products, arithmetic and copies ran while one was open for 2% -> 1% of each run, Pallas kernels for 0% -> 1%
where the time goes in v1:
time: 149 us
  starting transfers between devices  68.6 us (46%)
  waiting for transfers between devices  55 us (37%)
  Pallas kernels  19.6 us (13%)
  matrix products  1.88 us (1%)
  other arithmetic  1.72 us (1%)
    ppermute x9, waiting for transfers between devices, body(): lax.ppermute(passed, BOTH, hop_pairs(now - 1, shift))  45.1 us
    ppermute x10, starting transfers between devices, beside(): lax.ppermute(value, 'tile', ring('tile', -1))  42 us
    pallas_call x8, Pallas kernels, section(): pl.pallas_call(functools.partial(section_kernel, chip, len(speeds), carri...  19.6 us
    ppermute x1, starting transfers between devices, body(): got = lax.ppermute(sent, 'con', swap)  11.2 us
    ppermute x10, waiting for transfers between devices, beside(): lax.ppermute(value, 'tile', ring('tile', 1))  8.84 us
    ppermute x9, starting transfers between devices, body(): lax.ppermute(passed, BOTH, hop_pairs(now - 1, shift))  7.24 us
    ppermute x3, starting transfers between devices, body(): got = lax.ppermute(square_pair, 'con', ring('con', -2 * shift))  3.27 us
  transfers between devices with their start and end apart: 36, of which 7 were waited for; matrix products, arithmetic and copies ran while one was open for 1% of the time, Pallas kernels for 1%

profile of v1, /device:TPU:7, one launch (start us, length us, event | category | flops | bytes accessed | tf_op | source)
XLA Modules:
  0.0 149.1 jit_solution(18259752181232465445)
XLA Ops:
  0.0 0.7 and_select_fusion.1
  0.7 1.9 %convolution_add_fusion = f32[2,16,2048]{2,1,0:T(8,128)S(1)} fusion(s32[256]{0:T(256)S(1)} %get-tuple-element.55, f32[1,2,16,2048]{3,2,1,0:T(8,128)} %param.8, f32[16,256]{1,0:T(8,128)S(1)} %fusion.11, f32[2,256]{1,0:T(2,128)} %bitcast.28), kind=kOutput, calls=%fused_computation | convolution fusion | flops 201924608 | bytes 543744 | tf_op jit(solution)/shard_map/dot_general | solution.py:254
  2.6 0.0 copy-start
  2.6 0.0 copy-start.1
  2.6 0.8 collective-permute-start.8
  3.4 0.1 copy-done
  3.6 0.8 collective-permute-start
  4.3 1.7 %collective-permute-start.11 = (f32[16,1152]{1,0:T(8,128)S(1)}, f32[16,1152]{1,0:T(8,128)S(1)}, u32[]{:S(2)}, u32[]{:S(2)}) collective-permute-start(f32[16,1152]{1,0:T(8,128)S(1)} %slice_select_fusion.5.refs_10_.refs_13_), channel_id=1, source_target_pairs={{0,1},{1,2},{2,3},{3,4},{4,5},{5,6},{6,7},{7,8},{8,9},{9,10},{10,1... | collective-permute-start | bytes 221192 | tf_op jit(solution)/shard_map/ppermute | solution.py:229
  6.7 0.4 collective-permute-start.13
  7.2 0.0 copy-start.2
  7.2 0.6 collective-permute-start.1
  7.8 0.8 collective-permute-start.2
  8.6 0.0 collective-permute-done.8
  8.7 1.8 %collective-permute-start.3 = (f32[16,1152]{1,0:T(8,128)S(1)}, f32[16,1152]{1,0:T(8,128)S(1)}, u32[]{:S(2)}, u32[]{:S(2)}) collective-permute-start(f32[16,1152]{1,0:T(8,128)S(1)} %fusion.7), channel_id=1, source_target_pairs={{0,64},{32,96},{64,128},{96,160},{128,192},{160,224},{192,0},{224,... | collective-permute-start | bytes 221192 | tf_op jit(solution)/shard_map/ppermute | solution.py:270
  10.5 0.0 collective-permute-done.13
  10.5 6.3 %collective-permute-start.12 = (f32[16,1152]{1,0:T(8,128)S(1)}, f32[16,1152]{1,0:T(8,128)S(1)}, u32[]{:S(2)}, u32[]{:S(2)}) collective-permute-start(f32[16,1152]{1,0:T(8,128)S(1)} %slice_select_fusion.5.refs_10_.refs_13_), channel_id=1, source_target_pairs={{0,31},{1,0},{2,1},{3,2},{4,3},{5,4},{6,5},{7,6},{8,7},{9,8},{10,9... | collective-permute-start | bytes 221192 | tf_op jit(solution)/shard_map/ppermute | solution.py:231
  16.8 1.6 %collective-permute-start.10 = (f32[2,16,1152]{2,1,0:T(8,128)S(1)}, f32[2,16,1152]{2,1,0:T(8,128)S(1)}, u32[]{:S(2)}, u32[]{:S(2)}) collective-permute-start(f32[2,16,1152]{2,1,0:T(8,128)S(1)} %get-tuple-element.46.refs_7_.refs_10_), channel_id=1, source_target_pairs={{0,31},{1,0},{2,1},{3,2},{4,3},{5,4},{6,5},{7,6},{8,7},{9,8},{10,9... | collective-permute-start | bytes 442376 | tf_op jit(solution)/shard_map/ppermute | solution.py:231
  18.5 0.1 collective-permute-start.6
  18.6 0.1 fusion.12
  18.6 0.0 collective-permute-done.11.refs_9_.refs_12_
  18.6 0.6 collective-permute-start.4
  19.2 0.0 collective-permute-done.12.refs_11_.refs_14_
  19.2 4.3 %collective-permute-start.5 = (f32[16,1152]{1,0:T(8,128)S(1)}, f32[16,1152]{1,0:T(8,128)S(1)}, u32[]{:S(2)}, u32[]{:S(2)}) collective-permute-start(f32[16,1152]{1,0:T(8,128)S(1)} %get-tuple-element.43.refs_1_), channel_id=1, source_target_pairs={{0,31},{1,0},{2,1},{3,2},{4,3},{5,4},{6,5},{7,6},{8,7},{9,8},{10,9... | collective-permute-start | bytes 221192 | tf_op jit(solution)/shard_map/ppermute | solution.py:231
  23.6 0.0 collective-permute-done.10.refs_8_.refs_11_
  23.6 3.0 %collective-permute-start.7 = (f32[2,16,1152]{2,1,0:T(8,128)S(1)}, f32[2,16,1152]{2,1,0:T(8,128)S(1)}, u32[]{:S(2)}, u32[]{:S(2)}) collective-permute-start(f32[2,16,1152]{2,1,0:T(8,128)S(1)} %get-tuple-element.47.refs_4_.refs_7_), channel_id=1, source_target_pairs={{0,31},{1,0},{2,1},{3,2},{4,3},{5,4},{6,5},{7,6},{8,7},{9,8},{10,9... | collective-permute-start | bytes 442376 | tf_op jit(solution)/shard_map/ppermute | solution.py:231
  26.5 0.0 collective-permute-done.9.refs_6_.refs_9_
  26.6 2.4 %collective-permute-done.4.refs_0_ = f32[16,1152]{1,0:T(8,128)S(1)} collective-permute-done((f32[16,1152]{1,0:T(8,128)S(1)}, f32[16,1152]{1,0:T(8,128)S(1)}, u32[]{:S(2)}, u32[]{:S(2)}) %collective-permute-start.4) | collective-permute-done | bytes 73760 | tf_op jit(solution)/shard_map/ppermute | solution.py:229
  29.0 2.3 %collective-permute-start.19 = (f32[2,16,1152]{2,1,0:T(8,128)S(1)}, f32[2,16,1152]{2,1,0:T(8,128)S(1)}, u32[]{:S(2)}, u32[]{:S(2)}) collective-permute-start(f32[2,16,1152]{2,1,0:T(8,128)S(1)} %get-tuple-element.45.refs_7_), channel_id=1, source_target_pairs={{0,31},{1,0},{2,1},{3,2},{4,3},{5,4},{6,5},{7,6},{8,7},{9,8},{10,9... | collective-permute-start | bytes 442376 | tf_op jit(solution)/shard_map/ppermute | solution.py:231
  31.4 4.8 %collective-permute-start.17 = (f32[2,16,1152]{2,1,0:T(8,128)S(1)}, f32[2,16,1152]{2,1,0:T(8,128)S(1)}, u32[]{:S(2)}, u32[]{:S(2)}) collective-permute-start(f32[2,16,1152]{2,1,0:T(8,128)S(1)} %get-tuple-element.48.refs_4_), channel_id=1, source_target_pairs={{0,31},{1,0},{2,1},{3,2},{4,3},{5,4},{6,5},{7,6},{8,7},{9,8},{10,9... | collective-permute-start | bytes 442376 | tf_op jit(solution)/shard_map/ppermute | solution.py:231
  36.2 0.5 slice.88.refs_14_.refs_17_
  36.7 0.8 shard_map.76
  37.5 0.1 collective-permute-start.14
  37.6 4.8 %collective-permute-start.15 = (f32[16,1152]{1,0:T(8,128)S(1)}, f32[16,1152]{1,0:T(8,128)S(1)}, u32[]{:S(2)}, u32[]{:S(2)}) collective-permute-start(f32[16,1152]{1,0:T(8,128)S(1)} %get-tuple-element.24.refs_1_), channel_id=1, source_target_pairs={{0,31},{1,0},{2,1},{3,2},{4,3},{5,4},{6,5},{7,6},{8,7},{9,8},{10,9... | collective-permute-start | bytes 221192 | tf_op jit(solution)/shard_map/ppermute | solution.py:231
  42.4 0.6 slice.89.refs_13_
  42.9 1.4 collective-permute-done.14.refs_0_
  44.3 0.8 shard_map.77
  45.1 0.7 collective-permute-start.20
  45.8 0.7 collective-permute-start.21
  46.4 0.7 collective-permute-start.22
  47.1 0.8 shard_map.78
  48.0 0.1 collective-permute-start.23
  48.1 5.2 %collective-permute-start.24 = (f32[16,1152]{1,0:T(8,128)S(1)}, f32[16,1152]{1,0:T(8,128)S(1)}, u32[]{:S(2)}, u32[]{:S(2)}) collective-permute-start(f32[16,1152]{1,0:T(8,128)S(1)} %get-tuple-element.27.refs_1_), channel_id=1, source_target_pairs={{0,31},{1,0},{2,1},{3,2},{4,3},{5,4},{6,5},{7,6},{8,7},{9,8},{10,9... | collective-permute-start | bytes 221192 | tf_op jit(solution)/shard_map/ppermute | solution.py:231
  53.2 1.7 %collective-permute-done.23.refs_0_ = f32[16,1152]{1,0:T(8,128)S(1)} collective-permute-done((f32[16,1152]{1,0:T(8,128)S(1)}, f32[16,1152]{1,0:T(8,128)S(1)}, u32[]{:S(2)}, u32[]{:S(2)}) %collective-permute-start.23) | collective-permute-done | bytes 73760 | tf_op jit(solution)/shard_map/ppermute | solution.py:229
  54.9 0.8 shard_map.79
  55.6 0.7 collective-permute-start.25
  56.3 0.7 collective-permute-start.26
  57.0 0.7 collective-permute-start.27
  57.7 0.8 shard_map.80
  58.5 0.3 collective-permute-start.28
  58.8 4.9 %collective-permute-start.29 = (f32[16,1152]{1,0:T(8,128)S(1)}, f32[16,1152]{1,0:T(8,128)S(1)}, u32[]{:S(2)}, u32[]{:S(2)}) collective-permute-start(f32[16,1152]{1,0:T(8,128)S(1)} %get-tuple-element.30.refs_1_), channel_id=1, source_target_pairs={{0,31},{1,0},{2,1},{3,2},{4,3},{5,4},{6,5},{7,6},{8,7},{9,8},{10,9... | collective-permute-start | bytes 221192 | tf_op jit(solution)/shard_map/ppermute | solution.py:231
  63.8 1.7 %collective-permute-done.28.refs_0_ = f32[16,1152]{1,0:T(8,128)S(1)} collective-permute-done((f32[16,1152]{1,0:T(8,128)S(1)}, f32[16,1152]{1,0:T(8,128)S(1)}, u32[]{:S(2)}, u32[]{:S(2)}) %collective-permute-start.28) | collective-permute-done | bytes 73760 | tf_op jit(solution)/shard_map/ppermute | solution.py:229
  65.4 0.8 shard_map.81
  66.2 0.7 collective-permute-start.30
  66.9 1.3 collective-permute-start.31
  68.2 1.3 collective-permute-start.32
  69.5 45.1 %collective-permute-done.31.refs_4_.refs_15_ = f32[16,1152]{1,0:T(8,128)S(1)} collective-permute-done((f32[16,1152]{1,0:T(8,128)S(1)}, f32[16,1152]{1,0:T(8,128)S(1)}, u32[]{:S(2)}, u32[]{:S(2)}) %collective-permute-start.31) | collective-permute-done | bytes 73760 | tf_op jit(solution)/shard_map/ppermute | solution.py:286
  114.6 7.5 %shard_map.82 = (f32[2,16,1152]{2,1,0:T(8,128)S(1)}, f32[16,1152]{1,0:T(8,128)S(1)}, f32[16,1152]{1,0:T(8,128)S(1)}) custom-call(f32[16,1152]{1,0:T(8,128)S(1)} %collective-permute-done.4.refs_0_, f32[16,1152]{1,0:T(8,128)S(1)} %get-tuple-element.43.refs_1_, f32[16,1152]{1,0:T(8,128)S(1)} %collective-permute-done.5.refs_2_, ...), custom_call_target="tpu_custom_call" | custom-call | tf_op jit(solution)/shard_map/pallas_call | solution.py:200
  122.1 0.1 collective-permute-start.33
  122.2 4.8 %collective-permute-start.34 = (f32[16,1152]{1,0:T(8,128)S(1)}, f32[16,1152]{1,0:T(8,128)S(1)}, u32[]{:S(2)}, u32[]{:S(2)}) collective-permute-start(f32[16,1152]{1,0:T(8,128)S(1)} %get-tuple-element.37.refs_1_), channel_id=1, source_target_pairs={{0,31},{1,0},{2,1},{3,2},{4,3},{5,4},{6,5},{7,6},{8,7},{9,8},{10,9... | collective-permute-start | bytes 221192 | tf_op jit(solution)/shard_map/ppermute | solution.py:231
  127.0 1.7 %collective-permute-done.33.refs_0_ = f32[16,1152]{1,0:T(8,128)S(1)} collective-permute-done((f32[16,1152]{1,0:T(8,128)S(1)}, f32[16,1152]{1,0:T(8,128)S(1)}, u32[]{:S(2)}, u32[]{:S(2)}) %collective-permute-start.33) | collective-permute-done | bytes 73760 | tf_op jit(solution)/shard_map/ppermute | solution.py:229
  128.7 7.4 %shard_map.83 = (f32[2,16,1152]{2,1,0:T(8,128)S(1)}, f32[16,1152]{1,0:T(8,128)}) custom-call(f32[16,1152]{1,0:T(8,128)S(1)} %collective-permute-done.33.refs_0_, f32[16,1152]{1,0:T(8,128)S(1)} %get-tuple-element.37.refs_1_, f32[16,1152]{1,0:T(8,128)S(1)} %collective-permute-done.34.refs_2_, f32[2,16,1152]{2,1,0:T(8,128)S(1)} %collective-permute-done.16.refs_3_, ...), custom_call_target="tpu_custom_call" | custom-call | tf_op jit(solution)/shard_map/pallas_call | solution.py:200
  136.1 11.2 %collective-permute-start.35 = (f32[2,16,1024]{2,1,0:T(8,128)S(1)}, f32[2,16,1024]{2,1,0:T(8,128)S(1)}, u32[]{:S(2)}, u32[]{:S(2)}) collective-permute-start(f32[2,16,1024]{2,1,0:T(8,128)S(1)} %get-tuple-element.50), channel_id=1, source_target_pairs={{0,32},{32,0},{64,96},{96,64},{128,160},{160,128},{192,224},{224,1... | collective-permute-start | bytes 393224 | tf_op jit(solution)/shard_map/ppermute | solution.py:300
  147.3 1.0 collective-permute-done.35
  148.3 0.7 maximum_select_fusion
  (43 shorter events, 0.3 us)
Async XLA Ops:
  2.6 1.0 copy-start
  2.6 1.7 %copy-start.1 = (f32[16,2048]{1,0:T(8,128)S(1)}, f32[16,2048]{1,0:T(8,128)}, u32[]{:S(2)}) copy-start(f32[16,2048]{1,0:T(8,128)} %param.11) | copy-start | bytes 393220
  2.6 6.0 %collective-permute-start.8 = (f32[2,16,1152]{2,1,0:T(8,128)S(1)}, f32[2,16,1152]{2,1,0:T(8,128)S(1)}, u32[]{:S(2)}, u32[]{:S(2)}) collective-permute-start(f32[2,16,1152]{2,1,0:T(8,128)S(1)} %slice_select_fusion), channel_id=1, source_target_pairs={{0,32},{32,0},{64,96},{96,64},{128,160},{160,128},{192,224},{224,1... | collective-permute-start | bytes 442376 | tf_op jit(solution)/shard_map/ppermute | solution.py:246
  3.6 3.6 %collective-permute-start = (f32[2,16,1152]{2,1,0:T(8,128)S(1)}, f32[2,16,1152]{2,1,0:T(8,128)S(1)}, u32[]{:S(2)}, u32[]{:S(2)}) collective-permute-start(f32[2,16,1152]{2,1,0:T(8,128)S(1)} %slice_select_fusion.2), channel_id=1, source_target_pairs={{0,32},{32,0},{64,96},{96,64},{128,160},{160,128},{192,224},{224,1... | collective-permute-start | bytes 442376 | tf_op jit(solution)/shard_map/ppermute | solution.py:246
  4.3 14.3 %collective-permute-start.11 = (f32[16,1152]{1,0:T(8,128)S(1)}, f32[16,1152]{1,0:T(8,128)S(1)}, u32[]{:S(2)}, u32[]{:S(2)}) collective-permute-start(f32[16,1152]{1,0:T(8,128)S(1)} %slice_select_fusion.5.refs_10_.refs_13_), channel_id=1, source_target_pairs={{0,1},{1,2},{2,3},{3,4},{4,5},{5,6},{6,7},{7,8},{8,9},{9,10},{10,1... | collective-permute-start | bytes 221192 | tf_op jit(solution)/shard_map/ppermute | solution.py:229
  6.7 3.8 %collective-permute-start.13 = (f32[8,1152]{1,0:T(8,128)S(1)}, f32[8,1152]{1,0:T(8,128)S(1)}, u32[]{:S(2)}, u32[]{:S(2)}) collective-permute-start(f32[8,1152]{1,0:T(8,128)S(1)} %broadcast_in_dim.10), channel_id=1, source_target_pairs={{0,32},{32,0},{64,96},{96,64},{128,160},{160,128},{192,224},{224,1... | collective-permute-start | bytes 110600 | tf_op jit(solution)/shard_map/ppermute | solution.py:246
  7.2 11.4 %copy-start.2 = (f32[16,2048]{1,0:T(8,128)S(1)}, f32[16,2048]{1,0:T(8,128)}, u32[]{:S(2)}) copy-start(f32[16,2048]{1,0:T(8,128)} %param.12) | copy-start | bytes 393220
  7.2 9.6 %collective-permute-start.1 = (f32[16,1152]{1,0:T(8,128)S(1)}, f32[16,1152]{1,0:T(8,128)S(1)}, u32[]{:S(2)}, u32[]{:S(2)}) collective-permute-start(f32[16,1152]{1,0:T(8,128)S(1)} %fusion.7), channel_id=1, source_target_pairs={{0,192},{32,224},{64,0},{96,32},{128,64},{160,96},{192,128},{224,1... | collective-permute-start | bytes 221192 | tf_op jit(solution)/shard_map/ppermute | solution.py:270
  7.8 10.6 %collective-permute-start.2 = (f32[16,1152]{1,0:T(8,128)S(1)}, f32[16,1152]{1,0:T(8,128)S(1)}, u32[]{:S(2)}, u32[]{:S(2)}) collective-permute-start(f32[16,1152]{1,0:T(8,128)S(1)} %fusion.7), channel_id=1, source_target_pairs={{0,128},{32,160},{64,192},{96,224},{128,0},{160,32},{192,64},{224,... | collective-permute-start | bytes 221192 | tf_op jit(solution)/shard_map/ppermute | solution.py:270
  8.7 9.8 %collective-permute-start.3 = (f32[16,1152]{1,0:T(8,128)S(1)}, f32[16,1152]{1,0:T(8,128)S(1)}, u32[]{:S(2)}, u32[]{:S(2)}) collective-permute-start(f32[16,1152]{1,0:T(8,128)S(1)} %fusion.7), channel_id=1, source_target_pairs={{0,64},{32,96},{64,128},{96,160},{128,192},{160,224},{192,0},{224,... | collective-permute-start | bytes 221192 | tf_op jit(solution)/shard_map/ppermute | solution.py:270
  10.5 8.7 %collective-permute-start.12 = (f32[16,1152]{1,0:T(8,128)S(1)}, f32[16,1152]{1,0:T(8,128)S(1)}, u32[]{:S(2)}, u32[]{:S(2)}) collective-permute-start(f32[16,1152]{1,0:T(8,128)S(1)} %slice_select_fusion.5.refs_10_.refs_13_), channel_id=1, source_target_pairs={{0,31},{1,0},{2,1},{3,2},{4,3},{5,4},{6,5},{7,6},{8,7},{9,8},{10,9... | collective-permute-start | bytes 221192 | tf_op jit(solution)/shard_map/ppermute | solution.py:231
  16.8 6.7 %collective-permute-start.10 = (f32[2,16,1152]{2,1,0:T(8,128)S(1)}, f32[2,16,1152]{2,1,0:T(8,128)S(1)}, u32[]{:S(2)}, u32[]{:S(2)}) collective-permute-start(f32[2,16,1152]{2,1,0:T(8,128)S(1)} %get-tuple-element.46.refs_7_.refs_10_), channel_id=1, source_target_pairs={{0,31},{1,0},{2,1},{3,2},{4,3},{5,4},{6,5},{7,6},{8,7},{9,8},{10,9... | collective-permute-start | bytes 442376 | tf_op jit(solution)/shard_map/ppermute | solution.py:231
  18.4 8.1 %collective-permute-start.9 = (f32[2,16,1152]{2,1,0:T(8,128)S(1)}, f32[2,16,1152]{2,1,0:T(8,128)S(1)}, u32[]{:S(2)}, u32[]{:S(2)}) collective-permute-start(f32[2,16,1152]{2,1,0:T(8,128)S(1)} %get-tuple-element.46.refs_7_.refs_10_), channel_id=1, source_target_pairs={{0,1},{1,2},{2,3},{3,4},{4,5},{5,6},{6,7},{7,8},{8,9},{9,10},{10,1... | collective-permute-start | bytes 442376 | tf_op jit(solution)/shard_map/ppermute | solution.py:229
  18.5 12.9 %collective-permute-start.6 = (f32[2,16,1152]{2,1,0:T(8,128)S(1)}, f32[2,16,1152]{2,1,0:T(8,128)S(1)}, u32[]{:S(2)}, u32[]{:S(2)}) collective-permute-start(f32[2,16,1152]{2,1,0:T(8,128)S(1)} %get-tuple-element.47.refs_4_.refs_7_), channel_id=1, source_target_pairs={{0,1},{1,2},{2,3},{3,4},{4,5},{5,6},{6,7},{7,8},{8,9},{9,10},{10,1... | collective-permute-start | bytes 442376 | tf_op jit(solution)/shard_map/ppermute | solution.py:229
  18.6 10.4 %collective-permute-start.4 = (f32[16,1152]{1,0:T(8,128)S(1)}, f32[16,1152]{1,0:T(8,128)S(1)}, u32[]{:S(2)}, u32[]{:S(2)}) collective-permute-start(f32[16,1152]{1,0:T(8,128)S(1)} %get-tuple-element.43.refs_1_), channel_id=1, source_target_pairs={{0,1},{1,2},{2,3},{3,4},{4,5},{5,6},{6,7},{7,8},{8,9},{9,10},{10,1... | collective-permute-start | bytes 221192 | tf_op jit(solution)/shard_map/ppermute | solution.py:229
  19.2 12.1 %collective-permute-start.5 = (f32[16,1152]{1,0:T(8,128)S(1)}, f32[16,1152]{1,0:T(8,128)S(1)}, u32[]{:S(2)}, u32[]{:S(2)}) collective-permute-start(f32[16,1152]{1,0:T(8,128)S(1)} %get-tuple-element.43.refs_1_), channel_id=1, source_target_pairs={{0,31},{1,0},{2,1},{3,2},{4,3},{5,4},{6,5},{7,6},{8,7},{9,8},{10,9... | collective-permute-start | bytes 221192 | tf_op jit(solution)/shard_map/ppermute | solution.py:231
  23.6 13.1 %collective-permute-start.7 = (f32[2,16,1152]{2,1,0:T(8,128)S(1)}, f32[2,16,1152]{2,1,0:T(8,128)S(1)}, u32[]{:S(2)}, u32[]{:S(2)}) collective-permute-start(f32[2,16,1152]{2,1,0:T(8,128)S(1)} %get-tuple-element.47.refs_4_.refs_7_), channel_id=1, source_target_pairs={{0,31},{1,0},{2,1},{3,2},{4,3},{5,4},{6,5},{7,6},{8,7},{9,8},{10,9... | collective-permute-start | bytes 442376 | tf_op jit(solution)/shard_map/ppermute | solution.py:231
  26.6 11.0 %collective-permute-start.18 = (f32[2,16,1152]{2,1,0:T(8,128)S(1)}, f32[2,16,1152]{2,1,0:T(8,128)S(1)}, u32[]{:S(2)}, u32[]{:S(2)}) collective-permute-start(f32[2,16,1152]{2,1,0:T(8,128)S(1)} %get-tuple-element.45.refs_7_), channel_id=1, source_target_pairs={{0,1},{1,2},{2,3},{3,4},{4,5},{5,6},{6,7},{7,8},{8,9},{9,10},{10,1... | collective-permute-start | bytes 442376 | tf_op jit(solution)/shard_map/ppermute | solution.py:229
  29.0 13.9 %collective-permute-start.19 = (f32[2,16,1152]{2,1,0:T(8,128)S(1)}, f32[2,16,1152]{2,1,0:T(8,128)S(1)}, u32[]{:S(2)}, u32[]{:S(2)}) collective-permute-start(f32[2,16,1152]{2,1,0:T(8,128)S(1)} %get-tuple-element.45.refs_7_), channel_id=1, source_target_pairs={{0,31},{1,0},{2,1},{3,2},{4,3},{5,4},{6,5},{7,6},{8,7},{9,8},{10,9... | collective-permute-start | bytes 442376 | tf_op jit(solution)/shard_map/ppermute | solution.py:231
  31.3 11.6 %collective-permute-start.16 = (f32[2,16,1152]{2,1,0:T(8,128)S(1)}, f32[2,16,1152]{2,1,0:T(8,128)S(1)}, u32[]{:S(2)}, u32[]{:S(2)}) collective-permute-start(f32[2,16,1152]{2,1,0:T(8,128)S(1)} %get-tuple-element.48.refs_4_), channel_id=1, source_target_pairs={{0,1},{1,2},{2,3},{3,4},{4,5},{5,6},{6,7},{7,8},{8,9},{9,10},{10,1... | collective-permute-start | bytes 442376 | tf_op jit(solution)/shard_map/ppermute | solution.py:229
  31.4 11.6 %collective-permute-start.17 = (f32[2,16,1152]{2,1,0:T(8,128)S(1)}, f32[2,16,1152]{2,1,0:T(8,128)S(1)}, u32[]{:S(2)}, u32[]{:S(2)}) collective-permute-start(f32[2,16,1152]{2,1,0:T(8,128)S(1)} %get-tuple-element.48.refs_4_), channel_id=1, source_target_pairs={{0,31},{1,0},{2,1},{3,2},{4,3},{5,4},{6,5},{7,6},{8,7},{9,8},{10,9... | collective-permute-start | bytes 442376 | tf_op jit(solution)/shard_map/ppermute | solution.py:231
  37.5 6.8 %collective-permute-start.14 = (f32[16,1152]{1,0:T(8,128)S(1)}, f32[16,1152]{1,0:T(8,128)S(1)}, u32[]{:S(2)}, u32[]{:S(2)}) collective-permute-start(f32[16,1152]{1,0:T(8,128)S(1)} %get-tuple-element.24.refs_1_), channel_id=1, source_target_pairs={{0,1},{1,2},{2,3},{3,4},{4,5},{5,6},{6,7},{7,8},{8,9},{9,10},{10,1... | collective-permute-start | bytes 221192 | tf_op jit(solution)/shard_map/ppermute | solution.py:229
  37.6 6.7 %collective-permute-start.15 = (f32[16,1152]{1,0:T(8,128)S(1)}, f32[16,1152]{1,0:T(8,128)S(1)}, u32[]{:S(2)}, u32[]{:S(2)}) collective-permute-start(f32[16,1152]{1,0:T(8,128)S(1)} %get-tuple-element.24.refs_1_), channel_id=1, source_target_pairs={{0,31},{1,0},{2,1},{3,2},{4,3},{5,4},{6,5},{7,6},{8,7},{9,8},{10,9... | collective-permute-start | bytes 221192 | tf_op jit(solution)/shard_map/ppermute | solution.py:231
  45.1 2.0 %collective-permute-start.20 = (f32[16,1152]{1,0:T(8,128)S(1)}, f32[16,1152]{1,0:T(8,128)S(1)}, u32[]{:S(2)}, u32[]{:S(2)}) collective-permute-start(f32[16,1152]{1,0:T(8,128)S(1)} %get-tuple-element.26), channel_id=1, source_target_pairs={{0,65},{1,66},{2,67},{3,68},{4,69},{5,70},{6,71},{7,72},{8,73},{9,... | collective-permute-start | bytes 221192 | tf_op jit(solution)/shard_map/ppermute | solution.py:286
  45.8 1.4 collective-permute-start.21
  46.4 0.7 collective-permute-start.22
  48.0 6.9 %collective-permute-start.23 = (f32[16,1152]{1,0:T(8,128)S(1)}, f32[16,1152]{1,0:T(8,128)S(1)}, u32[]{:S(2)}, u32[]{:S(2)}) collective-permute-start(f32[16,1152]{1,0:T(8,128)S(1)} %get-tuple-element.27.refs_1_), channel_id=1, source_target_pairs={{0,1},{1,2},{2,3},{3,4},{4,5},{5,6},{6,7},{7,8},{8,9},{9,10},{10,1... | collective-permute-start | bytes 221192 | tf_op jit(solution)/shard_map/ppermute | solution.py:229
  48.1 6.8 %collective-permute-start.24 = (f32[16,1152]{1,0:T(8,128)S(1)}, f32[16,1152]{1,0:T(8,128)S(1)}, u32[]{:S(2)}, u32[]{:S(2)}) collective-permute-start(f32[16,1152]{1,0:T(8,128)S(1)} %get-tuple-element.27.refs_1_), channel_id=1, source_target_pairs={{0,31},{1,0},{2,1},{3,2},{4,3},{5,4},{6,5},{7,6},{8,7},{9,8},{10,9... | collective-permute-start | bytes 221192 | tf_op jit(solution)/shard_map/ppermute | solution.py:231
  55.6 2.0 %collective-permute-start.25 = (f32[16,1152]{1,0:T(8,128)S(1)}, f32[16,1152]{1,0:T(8,128)S(1)}, u32[]{:S(2)}, u32[]{:S(2)}) collective-permute-start(f32[16,1152]{1,0:T(8,128)S(1)} %get-tuple-element.29), channel_id=1, source_target_pairs={{64,129},{65,130},{66,131},{67,132},{68,133},{69,134},{70,135},{71... | collective-permute-start | bytes 221192 | tf_op jit(solution)/shard_map/ppermute | solution.py:286
  56.3 1.4 collective-permute-start.26
  57.0 0.7 collective-permute-start.27
  58.5 6.9 %collective-permute-start.28 = (f32[16,1152]{1,0:T(8,128)S(1)}, f32[16,1152]{1,0:T(8,128)S(1)}, u32[]{:S(2)}, u32[]{:S(2)}) collective-permute-start(f32[16,1152]{1,0:T(8,128)S(1)} %get-tuple-element.30.refs_1_), channel_id=1, source_target_pairs={{0,1},{1,2},{2,3},{3,4},{4,5},{5,6},{6,7},{7,8},{8,9},{9,10},{10,1... | collective-permute-start | bytes 221192 | tf_op jit(solution)/shard_map/ppermute | solution.py:229
  58.8 6.6 %collective-permute-start.29 = (f32[16,1152]{1,0:T(8,128)S(1)}, f32[16,1152]{1,0:T(8,128)S(1)}, u32[]{:S(2)}, u32[]{:S(2)}) collective-permute-start(f32[16,1152]{1,0:T(8,128)S(1)} %get-tuple-element.30.refs_1_), channel_id=1, source_target_pairs={{0,31},{1,0},{2,1},{3,2},{4,3},{5,4},{6,5},{7,6},{8,7},{9,8},{10,9... | collective-permute-start | bytes 221192 | tf_op jit(solution)/shard_map/ppermute | solution.py:231
  66.2 3.3 %collective-permute-start.30 = (f32[16,1152]{1,0:T(8,128)S(1)}, f32[16,1152]{1,0:T(8,128)S(1)}, u32[]{:S(2)}, u32[]{:S(2)}) collective-permute-start(f32[16,1152]{1,0:T(8,128)S(1)} %get-tuple-element.32), channel_id=1, source_target_pairs={{128,193},{129,194},{130,195},{131,196},{132,197},{133,198},{134,1... | collective-permute-start | bytes 221192 | tf_op jit(solution)/shard_map/ppermute | solution.py:286
  66.9 47.7 %collective-permute-start.31 = (f32[16,1152]{1,0:T(8,128)S(1)}, f32[16,1152]{1,0:T(8,128)S(1)}, u32[]{:S(2)}, u32[]{:S(2)}) collective-permute-start(f32[16,1152]{1,0:T(8,128)S(1)} %get-tuple-element.32), channel_id=1, source_target_pairs={{128,192},{129,193},{130,194},{131,195},{132,196},{133,197},{134,1... | collective-permute-start | bytes 221192 | tf_op jit(solution)/shard_map/ppermute | solution.py:286
  68.2 46.4 %collective-permute-start.32 = (f32[16,1152]{1,0:T(8,128)S(1)}, f32[16,1152]{1,0:T(8,128)S(1)}, u32[]{:S(2)}, u32[]{:S(2)}) collective-permute-start(f32[16,1152]{1,0:T(8,128)S(1)} %get-tuple-element.32), channel_id=1, source_target_pairs={{129,192},{130,193},{131,194},{132,195},{133,196},{134,197},{135,1... | collective-permute-start | bytes 221192 | tf_op jit(solution)/shard_map/ppermute | solution.py:286
  122.1 6.6 %collective-permute-start.33 = (f32[16,1152]{1,0:T(8,128)S(1)}, f32[16,1152]{1,0:T(8,128)S(1)}, u32[]{:S(2)}, u32[]{:S(2)}) collective-permute-start(f32[16,1152]{1,0:T(8,128)S(1)} %get-tuple-element.37.refs_1_), channel_id=1, source_target_pairs={{0,1},{1,2},{2,3},{3,4},{4,5},{5,6},{6,7},{7,8},{8,9},{9,10},{10,1... | collective-permute-start | bytes 221192 | tf_op jit(solution)/shard_map/ppermute | solution.py:229
  122.2 6.5 %collective-permute-start.34 = (f32[16,1152]{1,0:T(8,128)S(1)}, f32[16,1152]{1,0:T(8,128)S(1)}, u32[]{:S(2)}, u32[]{:S(2)}) collective-permute-start(f32[16,1152]{1,0:T(8,128)S(1)} %get-tuple-element.37.refs_1_), channel_id=1, source_target_pairs={{0,31},{1,0},{2,1},{3,2},{4,3},{5,4},{6,5},{7,6},{8,7},{9,8},{10,9... | collective-permute-start | bytes 221192 | tf_op jit(solution)/shard_map/ppermute | solution.py:231
  136.1 12.2 %collective-permute-start.35 = (f32[2,16,1024]{2,1,0:T(8,128)S(1)}, f32[2,16,1024]{2,1,0:T(8,128)S(1)}, u32[]{:S(2)}, u32[]{:S(2)}) collective-permute-start(f32[2,16,1024]{2,1,0:T(8,128)S(1)} %get-tuple-element.50), channel_id=1, source_target_pairs={{0,32},{32,0},{64,96},{96,64},{128,160},{160,128},{192,224},{224,1... | collective-permute-start | bytes 393224 | tf_op jit(solution)/shard_map/ppermute | solution.py:300

commit v2 on v1

v2 whole, which is shorter than its diff:
```python
import functools

import jax
import jax.numpy as jnp
from jax import lax
from jax.experimental import pallas as pl
from jax.experimental.pallas import tpu as pltpu
from jax.sharding import PartitionSpec as P

SWEEPS = 16
DRAG_COEF = 0.5
SHIFT_SIGMA = 0.1
ROWS = 16
LANES = 2048
WINDOW = 1152
COLS = WINDOW // 128
SPAN = 3 * ROWS
BOTH = ("con", "tile")


def ring(axis, shift):
    count = lax.axis_size(axis)
    return [(i, (i + shift) % count) for i in range(count)]


def hop_pairs(chip, shift):
    tiles = lax.axis_size("tile")
    return [
        (con * tiles + tile, (con + 2) * tiles + tile + shift)
        for con in (2 * chip, 2 * chip + 1)
        for tile in range(tiles)
        if 0 <= tile + shift < tiles
    ]


def sweep(source, target, gain, offset, lane, base, blocks):
    for block in range(blocks):
        inside = pl.ds(base + 8 * block, 8)
        middle = pl.ds(8 + base + 8 * block, 8)
        above = pl.ds(7 + base + 8 * block, 8)
        below = pl.ds(9 + base + 8 * block, 8)
        cells = {}

        def rolled(plane, col, shift):
            key = (plane, col % COLS, shift)
            if key not in cells:
                cells[key] = pltpu.roll(source[plane, col % COLS, middle, :], shift, 1)
            return cells[key]

        for col in range(COLS):
            total = []
            for plane in range(2):
                along = source[plane, col, above, :] + source[plane, col, below, :]
                left = jnp.where(lane == 0, rolled(plane, col - 1, 1), rolled(plane, col, 1))
                right = jnp.where(
                    lane == 127, rolled(plane, col + 1, 127), rolled(plane, col, 127)
                )
                total.append(along + (left + right))
            gain_real = gain[0, col, inside, :]
            gain_imag = gain[1, col, inside, :]
            target[0, col, middle, :] = offset[0, col, inside, :] + (
                gain_real * total[0] - gain_imag * total[1]
            )
            target[1, col, middle, :] = offset[1, col, inside, :] + (
                gain_real * total[1] + gain_imag * total[0]
            )


def section_kernel(chip, speeds, carried, more, *refs):
    refs = list(refs)
    take = lambda count: [refs.pop(0) for _ in range(count)]
    speed_refs = [take(3) for _ in range(speeds)]
    field_refs, deep_refs = take(3), take(3)
    (tone_ref,) = take(1)
    passed_ref = take(1)[0] if carried else None
    later_ref = take(1)[0] if more else None
    adjoint_out, passed_out = take(2)
    speed_out = take(1)[0] if more else None
    gain, offset, here, there = refs
    con = lax.axis_index("con")
    tile = lax.axis_index("tile")
    tiles = lax.axis_size("tile")
    core = con % 2

    @pl.when(con // 2 == chip)
    def _():
        lane = lax.broadcasted_iota(jnp.int32, (8, 128), 1)
        lane2 = lax.broadcasted_iota(jnp.int32, (ROWS, 128), 1)
        nothing = jnp.zeros((8, 128), jnp.float32)
        angular = jnp.broadcast_to(tone_ref[0:1, 0:128], (ROWS, 128))
        for col in range(COLS):
            lanes = pl.ds(128 * col, 128)
            for buffer in (here, there):
                for plane in range(2):
                    buffer[plane, col, pl.ds(0, 8), :] = nothing
                    buffer[plane, col, pl.ds(8 + SPAN, 8), :] = nothing
            for piece in range(3):
                speed_sq = speed_refs[0][piece][:, lanes]
                if speeds == 2:
                    speed_sq = speed_sq + speed_refs[1][piece][:, lanes]
                deep = deep_refs[piece][pl.ds(4 * ROWS, ROWS), lanes]
                drag = DRAG_COEF * jnp.sqrt(speed_sq)
                scaled = deep / (drag * drag + angular * angular)
                gain_real = scaled * drag
                gain_imag = scaled * angular
                diag_real = SHIFT_SIGMA + 4.0 * gain_real
                diag_imag = angular + 4.0 * gain_imag
                inverse = 1.0 / (diag_real * diag_real + diag_imag * diag_imag)
                inv_real = diag_real * inverse
                inv_imag = -diag_imag * inverse
                field_real, field_imag, force_real, force_imag = (
                    field_refs[piece][pl.ds(ROWS * part, ROWS), lanes] for part in range(4)
                )
                values = [
                    gain_real * inv_real - gain_imag * inv_imag,
                    gain_real * inv_imag + gain_imag * inv_real,
                    force_real * inv_real - force_imag * inv_imag,
                    force_real * inv_imag + force_imag * inv_real,
                    field_real,
                    field_imag,
                ]
                keep = None
                if piece == 0:
                    keep = jnp.broadcast_to(tile > 0, (ROWS, 128))
                if piece == 2:
                    keep = jnp.broadcast_to(tile < tiles - 1, (ROWS, 128))
                edge = None
                if col == 0:
                    edge = (lane2 != 0) | (core == 0)
                if col == COLS - 1:
                    edge = (lane2 != 127) | (core == 1)
                if edge is not None:
                    keep = edge if keep is None else keep & edge
                if keep is not None:
                    values = [jnp.where(keep, value, 0.0) for value in values]
                inside = pl.ds(ROWS * piece, ROWS)
                shifted = pl.ds(8 + ROWS * piece, ROWS)
                gain[0, col, inside, :] = values[0]
                gain[1, col, inside, :] = values[1]
                offset[0, col, inside, :] = values[2]
                offset[1, col, inside, :] = values[3]
                here[0, col, shifted, :] = values[4]
                here[1, col, shifted, :] = values[5]

        for phase in range(4):

            def step(_, carry):
                sweep(here, there, gain, offset, lane, 4 * phase, 6 - phase)
                sweep(there, here, gain, offset, lane, 4 * phase, 6 - phase)
                return carry

            lax.fori_loop(0, SWEEPS // 8, step, 0)
        for col in range(COLS):
            lanes = pl.ds(128 * col, 128)
            real = here[0, col, pl.ds(8 + ROWS, ROWS), :]
            imag = here[1, col, pl.ds(8 + ROWS, ROWS), :]
            adjoint_out[0, :, lanes] = real
            adjoint_out[1, :, lanes] = imag
            total = real * real + imag * imag
            if carried:
                total = total + passed_ref[:, lanes]
            passed_out[:, lanes] = total
            if more:
                speed_out[:, lanes] = total + later_ref[:, lanes]


def section(chip, speeds, fields, deeps, tone, passed=None, later=None):
    tile_shape = jax.ShapeDtypeStruct((ROWS, WINDOW), jnp.float32)
    pair_shape = jax.ShapeDtypeStruct((2, ROWS, WINDOW), jnp.float32)
    operands = [piece for term in speeds for piece in term] + [*fields, *deeps, tone]
    operands += [value for value in (passed, later) if value is not None]
    outs = [pair_shape, tile_shape] + ([tile_shape] if later is not None else [])
    whole = pl.BlockSpec(memory_space=pltpu.VMEM)
    vmem = lambda rows: pltpu.VMEM((2, COLS, rows, 128), jnp.float32)
    return pl.pallas_call(
        functools.partial(
            section_kernel, chip, len(speeds), passed is not None, later is not None
        ),
        out_shape=outs,
        in_specs=[whole] * len(operands),
        out_specs=[whole] * len(outs),
        scratch_shapes=[vmem(SPAN), vmem(SPAN), vmem(SPAN + 16), vmem(SPAN + 16)],
        compiler_params=pltpu.CompilerParams(vmem_limit_bytes=24 * 1024 * 1024),
    )(*operands)


def squared(field):
    return field[0] * field[0] + field[1] * field[1]


def beside(value):
    return (
        lax.ppermute(value, "tile", ring("tile", 1)),
        value,
        lax.ppermute(value, "tile", ring("tile", -1)),
    )


def after(value, *others):
    return lax.optimization_barrier((value, *others))[0]


def body(first_guess, misfit, innovations, obs_cells, depth, base_speed, frequency):
    chips = lax.axis_size("con") // 2
    con = lax.axis_index("con")
    chip, core = con // 2, con % 2
    swap = [(i, i ^ 1) for i in range(2 * chips)]

    def window(value, side):
        return jnp.where(core == side, value[..., :WINDOW], value[..., -WINDOW:])

    def shared(value):
        mine, sent = window(value, 0), window(value, 1)
        got = lax.ppermute(sent, "con", swap)
        return jnp.where(core == 0, mine, got), jnp.where(core == 0, got, mine), sent

    field_even, field_odd, sent = shared(first_guess[0])
    square_odd = squared(field_odd)
    square_pair = squared(field_even) + square_odd
    later = window(base_speed, 0)
    for shift in range(1, chips):
        got = lax.ppermute(square_pair, "con", ring("con", -2 * shift))
        later = later + jnp.where(chip + shift < chips, got, 0.0)
    starts = beside(later + square_odd)

    innovations = after(innovations, sent)
    lanes = jnp.arange(LANES, dtype=jnp.int32)
    rows = jnp.arange(ROWS, dtype=jnp.int32)
    at_lane = (obs_cells[:, None] % LANES == lanes[None]).astype(jnp.float32)
    at_row = (obs_cells[None] // LANES == rows[:, None]).astype(jnp.float32)
    added = jnp.dot(
        (innovations[0][:, None] * at_row[None]).reshape(2 * ROWS, -1),
        at_lane,
        precision=lax.Precision.HIGHEST,
        preferred_element_type=jnp.float32,
    )
    forcing = misfit[0].reshape(2 * ROWS, LANES) + added
    tones = jnp.broadcast_to(frequency, (8, LANES))
    force_even, force_odd, _ = shared(jnp.concatenate([forcing, tones]))
    tone_even, tone_odd = force_even[2 * ROWS :], force_odd[2 * ROWS :]
    flat = lambda field: field.reshape(2 * ROWS, WINDOW)
    evens = beside(
        jnp.concatenate([flat(field_even), force_even[: 2 * ROWS], window(depth, 0)])
    )
    odds = beside(jnp.concatenate([flat(after(field_odd, starts[0], starts[2], evens[0], evens[2])), force_odd[: 2 * ROWS]]))

    even = odd = passed = None
    for now in range(chips):
        speeds = [starts]
        if now:
            up, down, passed = [
                lax.ppermute(passed, BOTH, hop_pairs(now - 1, shift)) for shift in (1, -1, 0)
            ]
            speeds.append([up, passed, down])
        solved, passed, speed = section(now, speeds, evens, evens, tone_even, passed, later)
        even = solved if even is None else jnp.where(chip == now, solved, even)
        solved, passed = section(now, [beside(speed)], odds, evens, tone_odd, passed)
        odd = solved if odd is None else jnp.where(chip == now, solved, odd)

    own = LANES // 2
    sent = jnp.where(core == 0, odd[..., :own], even[..., -own:])
    got = lax.ppermute(sent, "con", swap)
    result = jnp.where(
        core == 0,
        jnp.concatenate([even[..., :own], got], axis=-1),
        jnp.concatenate([got, odd[..., -own:]], axis=-1),
    )
    return result[None]


def solution(mesh):
    placed = (
        P("con", None, "tile", None),
        P("con", None, "tile", None),
        P("con", None, "tile"),
        P("tile"),
        P("tile", None),
        P("tile", None),
        P("con"),
    )
    return jax.shard_map(
        body, mesh=mesh, in_specs=placed, out_specs=P("con", None, "tile", None), check_vma=False
    )
```

time: 149 us -> 115 us (0.77)
  starting transfers between devices: 68.6 us -> 55.3 us
  Pallas kernels: 19.6 us -> 8 us
  waiting for transfers between devices: 55 us -> 46.1 us
    ppermute x9, waiting for transfers between devices: 45.1 us -> 28.7 us  [body(): lax.ppermute(passed, BOTH, hop_pairs(now - 1, shift))]
    pallas_call x8, Pallas kernels: 19.6 us -> 8 us  [section(): pl.pallas_call(functools.partial(section_kernel, chip, len(speeds), passe...]
    ppermute x10 -> x7, starting transfers between devices: 42 us -> 31.6 us  [beside(): lax.ppermute(value, 'tile', ring('tile', -1))]
    ppermute x10 -> x7, waiting for transfers between devices: 0.03 us -> 4.69 us  [beside(): lax.ppermute(value, 'tile', ring('tile', -1))]
    ppermute x10 -> x7, waiting for transfers between devices: 8.84 us -> 11.6 us  [beside(): lax.ppermute(value, 'tile', ring('tile', 1))]
  transfers between devices with their start and end apart: 36 -> 29, of which waited for: 7 -> 8; matrix products, arithmetic and copies ran while one was open for 1% -> 1% of each run, Pallas kernels for 1% -> 0%
where the time goes in v2:
time: 115 us; the launch traced here: 114 us
  starting transfers between devices  55.3 us (48%)
  waiting for transfers between devices  46.1 us (40%)
  Pallas kernels  8 us (7%)
  other arithmetic  2.11 us (2%)
    ppermute x7, starting transfers between devices, beside(): lax.ppermute(value, 'tile', ring('tile', -1))  31.6 us
    ppermute x9, waiting for transfers between devices, body(): lax.ppermute(passed, BOTH, hop_pairs(now - 1, shift))  28.7 us
    ppermute x7, waiting for transfers between devices, beside(): lax.ppermute(value, 'tile', ring('tile', 1))  11.6 us
    ppermute x1, starting transfers between devices, body(): got = lax.ppermute(sent, 'con', swap)  9.9 us
    pallas_call x8, Pallas kernels, section(): pl.pallas_call(functools.partial(section_kernel, chip, len(speeds), passe...  8 us
    ppermute x9, starting transfers between devices, body(): lax.ppermute(passed, BOTH, hop_pairs(now - 1, shift))  7.22 us
    ppermute x7, waiting for transfers between devices, beside(): lax.ppermute(value, 'tile', ring('tile', -1))  4.69 us
    ppermute x3, starting transfers between devices, body(): got = lax.ppermute(square_pair, 'con', ring('con', -2 * shift))  3.27 us
  transfers between devices with their start and end apart: 29, of which 8 were waited for; matrix products, arithmetic and copies ran while one was open for 1% of the time, Pallas kernels for 0%

profile of v2, /device:TPU:7, one launch (start us, length us, event | category | flops | bytes accessed | tf_op | source)
XLA Modules:
  0.0 114.3 jit_solution(12320949013888565220)
XLA Ops:
  0.0 1.0 slice_select_fusion
  1.1 0.8 collective-permute-start
  2.5 0.9 convolution_add_fusion
  3.5 0.0 copy-start.1
  3.5 0.0 copy-start
  3.5 0.1 collective-permute-start.6
  3.6 0.7 copy-done.1
  4.4 0.0 collective-permute-done
  4.4 0.1 copy-done
  4.6 0.6 collective-permute-start.1
  5.2 2.5 %collective-permute-start.2 = (f32[16,1152]{1,0:T(8,128)S(1)}, f32[16,1152]{1,0:T(8,128)S(1)}, u32[]{:S(2)}, u32[]{:S(2)}) collective-permute-start(f32[16,1152]{1,0:T(8,128)S(1)} %fusion.5), channel_id=1, source_target_pairs={{0,128},{32,160},{64,192},{96,224},{128,0},{160,32},{192,64},{224,... | collective-permute-start | bytes 221192 | tf_op jit(solution)/shard_map/ppermute | solution.py:222
  7.7 0.1 collective-permute-start.3
  7.8 0.0 collective-permute-done.6
  7.9 0.0 copy-start.2
  7.9 1.7 %collective-permute-start.7 = (f32[80,1152]{1,0:T(8,128)S(1)}, f32[80,1152]{1,0:T(8,128)S(1)}, u32[]{:S(2)}, u32[]{:S(2)}) collective-permute-start(f32[80,1152]{1,0:T(8,128)S(1)} %pad_maximum_fusion.refs_4_.refs_7_.refs_10_), channel_id=1, source_target_pairs={{0,1},{1,2},{2,3},{3,4},{4,5},{5,6},{6,7},{7,8},{8,9},{9,10},{10,1... | collective-permute-start | bytes 1105928 | tf_op jit(solution)/shard_map/ppermute | solution.py:193
  9.7 6.5 %collective-permute-start.8 = (f32[80,1152]{1,0:T(8,128)S(1)}, f32[80,1152]{1,0:T(8,128)S(1)}, u32[]{:S(2)}, u32[]{:S(2)}) collective-permute-start(f32[80,1152]{1,0:T(8,128)S(1)} %pad_maximum_fusion.refs_4_.refs_7_.refs_10_), channel_id=1, source_target_pairs={{0,31},{1,0},{2,1},{3,2},{4,3},{5,4},{6,5},{7,6},{8,7},{9,8},{10,9... | collective-permute-start | bytes 1105928 | tf_op jit(solution)/shard_map/ppermute | solution.py:195
  16.1 0.0 collective-permute-done.1
  16.1 0.0 collective-permute-done.2
  16.1 0.0 collective-permute-done.3
  16.2 0.1 collective-permute-start.4
  16.3 4.8 %collective-permute-start.5 = (f32[16,1152]{1,0:T(8,128)S(1)}, f32[16,1152]{1,0:T(8,128)S(1)}, u32[]{:S(2)}, u32[]{:S(2)}) collective-permute-start(f32[16,1152]{1,0:T(8,128)S(1)} %get-tuple-element.47.refs_1_), channel_id=1, source_target_pairs={{0,31},{1,0},{2,1},{3,2},{4,3},{5,4},{6,5},{7,6},{8,7},{9,8},{10,9... | collective-permute-start | bytes 221192 | tf_op jit(solution)/shard_map/ppermute | solution.py:195
  21.1 4.6 %collective-permute-done.4.refs_0_ = f32[16,1152]{1,0:T(8,128)S(1)} collective-permute-done((f32[16,1152]{1,0:T(8,128)S(1)}, f32[16,1152]{1,0:T(8,128)S(1)}, u32[]{:S(2)}, u32[]{:S(2)}) %collective-permute-start.4) | collective-permute-done | bytes 73760 | tf_op jit(solution)/shard_map/ppermute | solution.py:193
  25.7 0.0 collective-permute-done.5.refs_2_
  25.7 0.0 collective-permute-done.8.refs_5_.refs_8_.refs_11_
  25.8 0.1 collective-permute-start.11
  25.8 4.8 %collective-permute-start.12 = (f32[64,1152]{1,0:T(8,128)S(1)}, f32[64,1152]{1,0:T(8,128)S(1)}, u32[]{:S(2)}, u32[]{:S(2)}) collective-permute-start(f32[64,1152]{1,0:T(8,128)S(1)} %pad_maximum_fusion.1.refs_4_), channel_id=1, source_target_pairs={{0,31},{1,0},{2,1},{3,2},{4,3},{5,4},{6,5},{7,6},{8,7},{9,8},{10,9... | collective-permute-start | bytes 884744 | tf_op jit(solution)/shard_map/ppermute | solution.py:195
  30.6 1.2 %collective-permute-start.10 = (f32[16,1152]{1,0:T(8,128)S(1)}, f32[16,1152]{1,0:T(8,128)S(1)}, u32[]{:S(2)}, u32[]{:S(2)}) collective-permute-start(f32[16,1152]{1,0:T(8,128)S(1)} %get-tuple-element.27.refs_1_), channel_id=1, source_target_pairs={{0,31},{1,0},{2,1},{3,2},{4,3},{5,4},{6,5},{7,6},{8,7},{9,8},{10,9... | collective-permute-start | bytes 221192 | tf_op jit(solution)/shard_map/ppermute | solution.py:195
  31.8 0.2 collective-permute-start.9
  32.1 4.7 %collective-permute-done.10.refs_2_ = f32[16,1152]{1,0:T(8,128)S(1)} collective-permute-done((f32[16,1152]{1,0:T(8,128)S(1)}, f32[16,1152]{1,0:T(8,128)S(1)}, u32[]{:S(2)}, u32[]{:S(2)}) %collective-permute-start.10) | collective-permute-done | bytes 73760 | tf_op jit(solution)/shard_map/ppermute | solution.py:195
  36.8 1.9 %collective-permute-done.9.refs_0_ = f32[16,1152]{1,0:T(8,128)S(1)} collective-permute-done((f32[16,1152]{1,0:T(8,128)S(1)}, f32[16,1152]{1,0:T(8,128)S(1)}, u32[]{:S(2)}, u32[]{:S(2)}) %collective-permute-start.9) | collective-permute-done | bytes 73760 | tf_op jit(solution)/shard_map/ppermute | solution.py:193
  38.7 0.0 collective-permute-done.11.refs_3_
  38.7 0.0 collective-permute-done.12.refs_5_
  38.7 0.7 collective-permute-start.13
  39.4 0.7 collective-permute-start.14
  40.0 0.7 collective-permute-start.15
  40.7 0.0 collective-permute-done.13.refs_3_
  40.7 0.0 collective-permute-done.15.refs_5_
  40.8 0.1 collective-permute-start.16
  40.9 4.8 %collective-permute-start.17 = (f32[16,1152]{1,0:T(8,128)S(1)}, f32[16,1152]{1,0:T(8,128)S(1)}, u32[]{:S(2)}, u32[]{:S(2)}) collective-permute-start(f32[16,1152]{1,0:T(8,128)S(1)} %get-tuple-element.31.refs_1_), channel_id=1, source_target_pairs={{0,31},{1,0},{2,1},{3,2},{4,3},{5,4},{6,5},{7,6},{8,7},{9,8},{10,9... | collective-permute-start | bytes 221192 | tf_op jit(solution)/shard_map/ppermute | solution.py:195
  45.6 1.7 %collective-permute-done.16.refs_0_ = f32[16,1152]{1,0:T(8,128)S(1)} collective-permute-done((f32[16,1152]{1,0:T(8,128)S(1)}, f32[16,1152]{1,0:T(8,128)S(1)}, u32[]{:S(2)}, u32[]{:S(2)}) %collective-permute-start.16) | collective-permute-done | bytes 73760 | tf_op jit(solution)/shard_map/ppermute | solution.py:193
  47.4 0.0 collective-permute-done.17.refs_2_
  47.4 0.7 collective-permute-start.18
  48.0 0.7 collective-permute-start.19
  48.7 0.7 collective-permute-start.20
  49.4 0.0 collective-permute-done.18.refs_3_
  49.4 0.0 collective-permute-done.19.refs_4_.refs_13_
  49.4 0.1 collective-permute-start.21
  49.5 4.9 %collective-permute-start.22 = (f32[16,1152]{1,0:T(8,128)S(1)}, f32[16,1152]{1,0:T(8,128)S(1)}, u32[]{:S(2)}, u32[]{:S(2)}) collective-permute-start(f32[16,1152]{1,0:T(8,128)S(1)} %get-tuple-element.34.refs_1_), channel_id=1, source_target_pairs={{0,31},{1,0},{2,1},{3,2},{4,3},{5,4},{6,5},{7,6},{8,7},{9,8},{10,9... | collective-permute-start | bytes 221192 | tf_op jit(solution)/shard_map/ppermute | solution.py:195
  54.4 1.7 %collective-permute-done.21.refs_0_ = f32[16,1152]{1,0:T(8,128)S(1)} collective-permute-done((f32[16,1152]{1,0:T(8,128)S(1)}, f32[16,1152]{1,0:T(8,128)S(1)}, u32[]{:S(2)}, u32[]{:S(2)}) %collective-permute-start.21) | collective-permute-done | bytes 73760 | tf_op jit(solution)/shard_map/ppermute | solution.py:193
  56.1 0.0 collective-permute-done.22.refs_2_
  56.1 0.7 collective-permute-start.23
  56.7 1.3 %collective-permute-start.24 = (f32[16,1152]{1,0:T(8,128)S(1)}, f32[16,1152]{1,0:T(8,128)S(1)}, u32[]{:S(2)}, u32[]{:S(2)}) collective-permute-start(f32[16,1152]{1,0:T(8,128)S(1)} %get-tuple-element.36), channel_id=1, source_target_pairs={{128,192},{129,193},{130,194},{131,195},{132,196},{133,197},{134,1... | collective-permute-start | bytes 221192 | tf_op jit(solution)/shard_map/ppermute | solution.py:252
  58.0 1.3 %collective-permute-start.25 = (f32[16,1152]{1,0:T(8,128)S(1)}, f32[16,1152]{1,0:T(8,128)S(1)}, u32[]{:S(2)}, u32[]{:S(2)}) collective-permute-start(f32[16,1152]{1,0:T(8,128)S(1)} %get-tuple-element.36), channel_id=1, source_target_pairs={{129,192},{130,193},{131,194},{132,195},{133,196},{134,197},{135,1... | collective-permute-start | bytes 221192 | tf_op jit(solution)/shard_map/ppermute | solution.py:252
  59.3 0.0 collective-permute-done.23.refs_3_
  59.3 28.7 %collective-permute-done.24.refs_4_.refs_13_ = f32[16,1152]{1,0:T(8,128)S(1)} collective-permute-done((f32[16,1152]{1,0:T(8,128)S(1)}, f32[16,1152]{1,0:T(8,128)S(1)}, u32[]{:S(2)}, u32[]{:S(2)}) %collective-permute-start.24) | collective-permute-done | bytes 73760 | tf_op jit(solution)/shard_map/ppermute | solution.py:252
  88.1 3.7 %shard_map.82 = (f32[2,16,1152]{2,1,0:T(8,128)S(1)}, f32[16,1152]{1,0:T(8,128)S(1)}, f32[16,1152]{1,0:T(8,128)S(1)}) custom-call(f32[16,1152]{1,0:T(8,128)S(1)} %collective-permute-done.4.refs_0_, f32[16,1152]{1,0:T(8,128)S(1)} %get-tuple-element.47.refs_1_, f32[16,1152]{1,0:T(8,128)S(1)} %collective-permute-done.5.refs_2_, ...), custom_call_target="tpu_custom_call" | custom-call | tf_op jit(solution)/shard_map/pallas_call | solution.py:175
  91.7 0.1 collective-permute-start.26
  91.8 4.8 %collective-permute-start.27 = (f32[16,1152]{1,0:T(8,128)S(1)}, f32[16,1152]{1,0:T(8,128)S(1)}, u32[]{:S(2)}, u32[]{:S(2)}) collective-permute-start(f32[16,1152]{1,0:T(8,128)S(1)} %get-tuple-element.41.refs_1_), channel_id=1, source_target_pairs={{0,31},{1,0},{2,1},{3,2},{4,3},{5,4},{6,5},{7,6},{8,7},{9,8},{10,9... | collective-permute-start | bytes 221192 | tf_op jit(solution)/shard_map/ppermute | solution.py:195
  96.6 1.7 %collective-permute-done.26.refs_0_ = f32[16,1152]{1,0:T(8,128)S(1)} collective-permute-done((f32[16,1152]{1,0:T(8,128)S(1)}, f32[16,1152]{1,0:T(8,128)S(1)}, u32[]{:S(2)}, u32[]{:S(2)}) %collective-permute-start.26) | collective-permute-done | bytes 73760 | tf_op jit(solution)/shard_map/ppermute | solution.py:193
  98.3 0.0 collective-permute-done.27.refs_2_
  98.3 4.3 %shard_map.83 = (f32[2,16,1152]{2,1,0:T(8,128)S(1)}, f32[16,1152]{1,0:T(8,128)}) custom-call(f32[16,1152]{1,0:T(8,128)S(1)} %collective-permute-done.26.refs_0_, f32[16,1152]{1,0:T(8,128)S(1)} %get-tuple-element.41.refs_1_, f32[16,1152]{1,0:T(8,128)S(1)} %collective-permute-done.27.refs_2_, f32[64,1152]{1,0:T(8,128)S(1)} %collective-permute-done.11.refs_3_, ...), custom_call_target="tpu_custom_call" | custom-call | tf_op jit(solution)/shard_map/pallas_call | solution.py:175
  102.7 9.9 %collective-permute-start.28 = (f32[2,16,1024]{2,1,0:T(8,128)S(1)}, f32[2,16,1024]{2,1,0:T(8,128)S(1)}, u32[]{:S(2)}, u32[]{:S(2)}) collective-permute-start(f32[2,16,1024]{2,1,0:T(8,128)S(1)} %get-tuple-element.54), channel_id=1, source_target_pairs={{0,32},{32,0},{64,96},{96,64},{128,160},{160,128},{192,224},{224,1... | collective-permute-start | bytes 393224 | tf_op jit(solution)/shard_map/ppermute | solution.py:262
  112.6 1.0 collective-permute-done.28
  113.6 0.7 maximum_select_fusion
  (35 shorter events, 0.4 us)
Async XLA Ops:
  0.0 2.5 %copy-start.3 = (f32[1,2,256]{2,1,0:T(2,128)S(1)}, f32[1,2,256]{2,1,0:T(2,128)}, u32[]{:S(2)}) copy-start(f32[1,2,256]{2,1,0:T(2,128)} %param.9) | copy-start | bytes 6148
  0.0 1.8 %copy-start.4 = (s32[256]{0:T(256)S(1)}, s32[256]{0:T(256)}, u32[]{:S(2)}) copy-start(s32[256]{0:T(256)} %param.10) | copy-start | bytes 3076
  0.0 2.5 %copy-start.5 = (f32[1,2,16,2048]{3,2,1,0:T(8,128)S(1)}, f32[1,2,16,2048]{3,2,1,0:T(8,128)}, u32[]{:S(2)}) copy-start(f32[1,2,16,2048]{3,2,1,0:T(8,128)} %param.8) | copy-start | bytes 786436
  1.1 3.3 %collective-permute-start = (f32[2,16,1152]{2,1,0:T(8,128)S(1)}, f32[2,16,1152]{2,1,0:T(8,128)S(1)}, u32[]{:S(2)}, u32[]{:S(2)}) collective-permute-start(f32[2,16,1152]{2,1,0:T(8,128)S(1)} %slice_select_fusion), channel_id=1, source_target_pairs={{0,32},{32,0},{64,96},{96,64},{128,160},{160,128},{192,224},{224,1... | collective-permute-start | bytes 442376 | tf_op jit(solution)/shard_map/ppermute | solution.py:214
  3.5 0.9 copy-start.1
  3.5 1.0 copy-start
  3.5 4.3 %collective-permute-start.6 = (f32[40,1152]{1,0:T(8,128)S(1)}, f32[40,1152]{1,0:T(8,128)S(1)}, u32[]{:S(2)}, u32[]{:S(2)}) collective-permute-start(f32[40,1152]{1,0:T(8,128)S(1)} %broadcast_select_fusion), channel_id=1, source_target_pairs={{0,32},{32,0},{64,96},{96,64},{128,160},{160,128},{192,224},{224,1... | collective-permute-start | bytes 552968 | tf_op jit(solution)/shard_map/ppermute | solution.py:214
  4.6 11.6 %collective-permute-start.1 = (f32[16,1152]{1,0:T(8,128)S(1)}, f32[16,1152]{1,0:T(8,128)S(1)}, u32[]{:S(2)}, u32[]{:S(2)}) collective-permute-start(f32[16,1152]{1,0:T(8,128)S(1)} %fusion.5), channel_id=1, source_target_pairs={{0,192},{32,224},{64,0},{96,32},{128,64},{160,96},{192,128},{224,1... | collective-permute-start | bytes 221192 | tf_op jit(solution)/shard_map/ppermute | solution.py:222
  5.2 11.0 %collective-permute-start.2 = (f32[16,1152]{1,0:T(8,128)S(1)}, f32[16,1152]{1,0:T(8,128)S(1)}, u32[]{:S(2)}, u32[]{:S(2)}) collective-permute-start(f32[16,1152]{1,0:T(8,128)S(1)} %fusion.5), channel_id=1, source_target_pairs={{0,128},{32,160},{64,192},{96,224},{128,0},{160,32},{192,64},{224,... | collective-permute-start | bytes 221192 | tf_op jit(solution)/shard_map/ppermute | solution.py:222
  7.7 8.4 %collective-permute-start.3 = (f32[16,1152]{1,0:T(8,128)S(1)}, f32[16,1152]{1,0:T(8,128)S(1)}, u32[]{:S(2)}, u32[]{:S(2)}) collective-permute-start(f32[16,1152]{1,0:T(8,128)S(1)} %fusion.5), channel_id=1, source_target_pairs={{0,64},{32,96},{64,128},{96,160},{128,192},{160,224},{192,0},{224,... | collective-permute-start | bytes 221192 | tf_op jit(solution)/shard_map/ppermute | solution.py:222
  7.9 8.3 %copy-start.2 = (f32[16,2048]{1,0:T(8,128)S(1)}, f32[16,2048]{1,0:T(8,128)}, u32[]{:S(2)}) copy-start(f32[16,2048]{1,0:T(8,128)} %param.12) | copy-start | bytes 393220
  7.9 17.8 %collective-permute-start.7 = (f32[80,1152]{1,0:T(8,128)S(1)}, f32[80,1152]{1,0:T(8,128)S(1)}, u32[]{:S(2)}, u32[]{:S(2)}) collective-permute-start(f32[80,1152]{1,0:T(8,128)S(1)} %pad_maximum_fusion.refs_4_.refs_7_.refs_10_), channel_id=1, source_target_pairs={{0,1},{1,2},{2,3},{3,4},{4,5},{5,6},{6,7},{7,8},{8,9},{9,10},{10,1... | collective-permute-start | bytes 1105928 | tf_op jit(solution)/shard_map/ppermute | solution.py:193
  9.7 16.1 %collective-permute-start.8 = (f32[80,1152]{1,0:T(8,128)S(1)}, f32[80,1152]{1,0:T(8,128)S(1)}, u32[]{:S(2)}, u32[]{:S(2)}) collective-permute-start(f32[80,1152]{1,0:T(8,128)S(1)} %pad_maximum_fusion.refs_4_.refs_7_.refs_10_), channel_id=1, source_target_pairs={{0,31},{1,0},{2,1},{3,2},{4,3},{5,4},{6,5},{7,6},{8,7},{9,8},{10,9... | collective-permute-start | bytes 1105928 | tf_op jit(solution)/shard_map/ppermute | solution.py:195
  16.2 9.5 %collective-permute-start.4 = (f32[16,1152]{1,0:T(8,128)S(1)}, f32[16,1152]{1,0:T(8,128)S(1)}, u32[]{:S(2)}, u32[]{:S(2)}) collective-permute-start(f32[16,1152]{1,0:T(8,128)S(1)} %get-tuple-element.47.refs_1_), channel_id=1, source_target_pairs={{0,1},{1,2},{2,3},{3,4},{4,5},{5,6},{6,7},{7,8},{8,9},{9,10},{10,1... | collective-permute-start | bytes 221192 | tf_op jit(solution)/shard_map/ppermute | solution.py:193
  16.3 9.4 %collective-permute-start.5 = (f32[16,1152]{1,0:T(8,128)S(1)}, f32[16,1152]{1,0:T(8,128)S(1)}, u32[]{:S(2)}, u32[]{:S(2)}) collective-permute-start(f32[16,1152]{1,0:T(8,128)S(1)} %get-tuple-element.47.refs_1_), channel_id=1, source_target_pairs={{0,31},{1,0},{2,1},{3,2},{4,3},{5,4},{6,5},{7,6},{8,7},{9,8},{10,9... | collective-permute-start | bytes 221192 | tf_op jit(solution)/shard_map/ppermute | solution.py:195
  25.8 12.9 %collective-permute-start.11 = (f32[64,1152]{1,0:T(8,128)S(1)}, f32[64,1152]{1,0:T(8,128)S(1)}, u32[]{:S(2)}, u32[]{:S(2)}) collective-permute-start(f32[64,1152]{1,0:T(8,128)S(1)} %pad_maximum_fusion.1.refs_4_), channel_id=1, source_target_pairs={{0,1},{1,2},{2,3},{3,4},{4,5},{5,6},{6,7},{7,8},{8,9},{9,10},{10,1... | collective-permute-start | bytes 884744 | tf_op jit(solution)/shard_map/ppermute | solution.py:193
  25.8 12.8 %collective-permute-start.12 = (f32[64,1152]{1,0:T(8,128)S(1)}, f32[64,1152]{1,0:T(8,128)S(1)}, u32[]{:S(2)}, u32[]{:S(2)}) collective-permute-start(f32[64,1152]{1,0:T(8,128)S(1)} %pad_maximum_fusion.1.refs_4_), channel_id=1, source_target_pairs={{0,31},{1,0},{2,1},{3,2},{4,3},{5,4},{6,5},{7,6},{8,7},{9,8},{10,9... | collective-permute-start | bytes 884744 | tf_op jit(solution)/shard_map/ppermute | solution.py:195
  30.6 6.1 %collective-permute-start.10 = (f32[16,1152]{1,0:T(8,128)S(1)}, f32[16,1152]{1,0:T(8,128)S(1)}, u32[]{:S(2)}, u32[]{:S(2)}) collective-permute-start(f32[16,1152]{1,0:T(8,128)S(1)} %get-tuple-element.27.refs_1_), channel_id=1, source_target_pairs={{0,31},{1,0},{2,1},{3,2},{4,3},{5,4},{6,5},{7,6},{8,7},{9,8},{10,9... | collective-permute-start | bytes 221192 | tf_op jit(solution)/shard_map/ppermute | solution.py:195
  31.8 6.8 %collective-permute-start.9 = (f32[16,1152]{1,0:T(8,128)S(1)}, f32[16,1152]{1,0:T(8,128)S(1)}, u32[]{:S(2)}, u32[]{:S(2)}) collective-permute-start(f32[16,1152]{1,0:T(8,128)S(1)} %get-tuple-element.27.refs_1_), channel_id=1, source_target_pairs={{0,1},{1,2},{2,3},{3,4},{4,5},{5,6},{6,7},{7,8},{8,9},{9,10},{10,1... | collective-permute-start | bytes 221192 | tf_op jit(solution)/shard_map/ppermute | solution.py:193
  38.7 2.0 %collective-permute-start.13 = (f32[16,1152]{1,0:T(8,128)S(1)}, f32[16,1152]{1,0:T(8,128)S(1)}, u32[]{:S(2)}, u32[]{:S(2)}) collective-permute-start(f32[16,1152]{1,0:T(8,128)S(1)} %get-tuple-element.30), channel_id=1, source_target_pairs={{0,65},{1,66},{2,67},{3,68},{4,69},{5,70},{6,71},{7,72},{8,73},{9,... | collective-permute-start | bytes 221192 | tf_op jit(solution)/shard_map/ppermute | solution.py:252
  39.4 1.4 %collective-permute-start.14 = (f32[16,1152]{1,0:T(8,128)S(1)}, f32[16,1152]{1,0:T(8,128)S(1)}, u32[]{:S(2)}, u32[]{:S(2)}) collective-permute-start(f32[16,1152]{1,0:T(8,128)S(1)} %get-tuple-element.30), channel_id=1, source_target_pairs={{0,64},{1,65},{2,66},{3,67},{4,68},{5,69},{6,70},{7,71},{8,72},{9,... | collective-permute-start | bytes 221192 | tf_op jit(solution)/shard_map/ppermute | solution.py:252
  40.0 0.7 collective-permute-start.15
  40.8 6.6 %collective-permute-start.16 = (f32[16,1152]{1,0:T(8,128)S(1)}, f32[16,1152]{1,0:T(8,128)S(1)}, u32[]{:S(2)}, u32[]{:S(2)}) collective-permute-start(f32[16,1152]{1,0:T(8,128)S(1)} %get-tuple-element.31.refs_1_), channel_id=1, source_target_pairs={{0,1},{1,2},{2,3},{3,4},{4,5},{5,6},{6,7},{7,8},{8,9},{9,10},{10,1... | collective-permute-start | bytes 221192 | tf_op jit(solution)/shard_map/ppermute | solution.py:193
  40.9 6.5 %collective-permute-start.17 = (f32[16,1152]{1,0:T(8,128)S(1)}, f32[16,1152]{1,0:T(8,128)S(1)}, u32[]{:S(2)}, u32[]{:S(2)}) collective-permute-start(f32[16,1152]{1,0:T(8,128)S(1)} %get-tuple-element.31.refs_1_), channel_id=1, source_target_pairs={{0,31},{1,0},{2,1},{3,2},{4,3},{5,4},{6,5},{7,6},{8,7},{9,8},{10,9... | collective-permute-start | bytes 221192 | tf_op jit(solution)/shard_map/ppermute | solution.py:195
  47.4 2.0 %collective-permute-start.18 = (f32[16,1152]{1,0:T(8,128)S(1)}, f32[16,1152]{1,0:T(8,128)S(1)}, u32[]{:S(2)}, u32[]{:S(2)}) collective-permute-start(f32[16,1152]{1,0:T(8,128)S(1)} %get-tuple-element.33), channel_id=1, source_target_pairs={{64,129},{65,130},{66,131},{67,132},{68,133},{69,134},{70,135},{71... | collective-permute-start | bytes 221192 | tf_op jit(solution)/shard_map/ppermute | solution.py:252
  48.0 1.4 %collective-permute-start.19 = (f32[16,1152]{1,0:T(8,128)S(1)}, f32[16,1152]{1,0:T(8,128)S(1)}, u32[]{:S(2)}, u32[]{:S(2)}) collective-permute-start(f32[16,1152]{1,0:T(8,128)S(1)} %get-tuple-element.33), channel_id=1, source_target_pairs={{64,128},{65,129},{66,130},{67,131},{68,132},{69,133},{70,134},{71... | collective-permute-start | bytes 221192 | tf_op jit(solution)/shard_map/ppermute | solution.py:252
  48.7 0.7 collective-permute-start.20
  49.4 6.6 %collective-permute-start.21 = (f32[16,1152]{1,0:T(8,128)S(1)}, f32[16,1152]{1,0:T(8,128)S(1)}, u32[]{:S(2)}, u32[]{:S(2)}) collective-permute-start(f32[16,1152]{1,0:T(8,128)S(1)} %get-tuple-element.34.refs_1_), channel_id=1, source_target_pairs={{0,1},{1,2},{2,3},{3,4},{4,5},{5,6},{6,7},{7,8},{8,9},{9,10},{10,1... | collective-permute-start | bytes 221192 | tf_op jit(solution)/shard_map/ppermute | solution.py:193
  49.5 6.5 %collective-permute-start.22 = (f32[16,1152]{1,0:T(8,128)S(1)}, f32[16,1152]{1,0:T(8,128)S(1)}, u32[]{:S(2)}, u32[]{:S(2)}) collective-permute-start(f32[16,1152]{1,0:T(8,128)S(1)} %get-tuple-element.34.refs_1_), channel_id=1, source_target_pairs={{0,31},{1,0},{2,1},{3,2},{4,3},{5,4},{6,5},{7,6},{8,7},{9,8},{10,9... | collective-permute-start | bytes 221192 | tf_op jit(solution)/shard_map/ppermute | solution.py:195
  56.1 3.3 %collective-permute-start.23 = (f32[16,1152]{1,0:T(8,128)S(1)}, f32[16,1152]{1,0:T(8,128)S(1)}, u32[]{:S(2)}, u32[]{:S(2)}) collective-permute-start(f32[16,1152]{1,0:T(8,128)S(1)} %get-tuple-element.36), channel_id=1, source_target_pairs={{128,193},{129,194},{130,195},{131,196},{132,197},{133,198},{134,1... | collective-permute-start | bytes 221192 | tf_op jit(solution)/shard_map/ppermute | solution.py:252
  56.7 31.3 %collective-permute-start.24 = (f32[16,1152]{1,0:T(8,128)S(1)}, f32[16,1152]{1,0:T(8,128)S(1)}, u32[]{:S(2)}, u32[]{:S(2)}) collective-permute-start(f32[16,1152]{1,0:T(8,128)S(1)} %get-tuple-element.36), channel_id=1, source_target_pairs={{128,192},{129,193},{130,194},{131,195},{132,196},{133,197},{134,1... | collective-permute-start | bytes 221192 | tf_op jit(solution)/shard_map/ppermute | solution.py:252
  58.0 30.0 %collective-permute-start.25 = (f32[16,1152]{1,0:T(8,128)S(1)}, f32[16,1152]{1,0:T(8,128)S(1)}, u32[]{:S(2)}, u32[]{:S(2)}) collective-permute-start(f32[16,1152]{1,0:T(8,128)S(1)} %get-tuple-element.36), channel_id=1, source_target_pairs={{129,192},{130,193},{131,194},{132,195},{133,196},{134,197},{135,1... | collective-permute-start | bytes 221192 | tf_op jit(solution)/shard_map/ppermute | solution.py:252
  91.7 6.6 %collective-permute-start.26 = (f32[16,1152]{1,0:T(8,128)S(1)}, f32[16,1152]{1,0:T(8,128)S(1)}, u32[]{:S(2)}, u32[]{:S(2)}) collective-permute-start(f32[16,1152]{1,0:T(8,128)S(1)} %get-tuple-element.41.refs_1_), channel_id=1, source_target_pairs={{0,1},{1,2},{2,3},{3,4},{4,5},{5,6},{6,7},{7,8},{8,9},{9,10},{10,1... | collective-permute-start | bytes 221192 | tf_op jit(solution)/shard_map/ppermute | solution.py:193
  91.8 6.5 %collective-permute-start.27 = (f32[16,1152]{1,0:T(8,128)S(1)}, f32[16,1152]{1,0:T(8,128)S(1)}, u32[]{:S(2)}, u32[]{:S(2)}) collective-permute-start(f32[16,1152]{1,0:T(8,128)S(1)} %get-tuple-element.41.refs_1_), channel_id=1, source_target_pairs={{0,31},{1,0},{2,1},{3,2},{4,3},{5,4},{6,5},{7,6},{8,7},{9,8},{10,9... | collective-permute-start | bytes 221192 | tf_op jit(solution)/shard_map/ppermute | solution.py:195
  102.7 10.9 %collective-permute-start.28 = (f32[2,16,1024]{2,1,0:T(8,128)S(1)}, f32[2,16,1024]{2,1,0:T(8,128)S(1)}, u32[]{:S(2)}, u32[]{:S(2)}) collective-permute-start(f32[2,16,1024]{2,1,0:T(8,128)S(1)} %get-tuple-element.54), channel_id=1, source_target_pairs={{0,32},{32,0},{64,96},{96,64},{128,160},{160,128},{192,224},{224,1... | collective-permute-start | bytes 393224 | tf_op jit(solution)/shard_map/ppermute | solution.py:262

commit v3 on v2

--- a/solution.py
+++ b/solution.py
@@ -18,44 +18,35 @@
 BOTH = ("con", "tile")
 
 
-def ring(axis, shift):
-    count = lax.axis_size(axis)
-    return [(i, (i + shift) % count) for i in range(count)]
-
-
 def hop_pairs(chip, shift):
     tiles = lax.axis_size("tile")
     return [
-        (con * tiles + tile, (con + 2) * tiles + tile + shift)
-        for con in (2 * chip, 2 * chip + 1)
+        (con * tiles + tile, (con + 2) * tiles + tile + step)
+        for con, step in ((2 * chip, shift), (2 * chip + 1, -shift))
         for tile in range(tiles)
-        if 0 <= tile + shift < tiles
+        if 0 <= tile + step < tiles
     ]
 
 
-def sweep(source, target, gain, offset, lane, base, blocks):
+def sweep(source, target, gain, offset, base, blocks):
     for block in range(blocks):
         inside = pl.ds(base + 8 * block, 8)
         middle = pl.ds(8 + base + 8 * block, 8)
         above = pl.ds(7 + base + 8 * block, 8)
         below = pl.ds(9 + base + 8 * block, 8)
-        cells = {}
-
-        def rolled(plane, col, shift):
-            key = (plane, col % COLS, shift)
-            if key not in cells:
-                cells[key] = pltpu.roll(source[plane, col % COLS, middle, :], shift, 1)
-            return cells[key]
+        cells = {
+            (plane, col): source[plane, col, middle, :] for plane in range(2) for col in range(COLS)
+        }
+        for plane in range(2):
+            cells[plane, -1] = pltpu.roll(cells[plane, COLS - 1], 1, 1)
+            cells[plane, COLS] = pltpu.roll(cells[plane, 0], 127, 1)
 
         for col in range(COLS):
             total = []
             for plane in range(2):
                 along = source[plane, col, above, :] + source[plane, col, below, :]
-                left = jnp.where(lane == 0, rolled(plane, col - 1, 1), rolled(plane, col, 1))
-                right = jnp.where(
-                    lane == 127, rolled(plane, col + 1, 127), rolled(plane, col, 127)
-                )
-                total.append(along + (left + right))
+                across = cells[plane, col - 1] + cells[plane, col + 1]
+                total.append(along + across)
             gain_real = gain[0, col, inside, :]
             gain_imag = gain[1, col, inside, :]
             target[0, col, middle, :] = offset[0, col, inside, :] + (
@@ -84,10 +75,18 @@
 
     @pl.when(con // 2 == chip)
     def _():
-        lane = lax.broadcasted_iota(jnp.int32, (8, 128), 1)
         lane2 = lax.broadcasted_iota(jnp.int32, (ROWS, 128), 1)
         nothing = jnp.zeros((8, 128), jnp.float32)
         angular = jnp.broadcast_to(tone_ref[0:1, 0:128], (ROWS, 128))
+        first_row = pl.multiple_of(2 * ROWS * core, ROWS)
+        places = (first_row, ROWS, pl.multiple_of(2 * ROWS - first_row, ROWS))
+        above, below = tile > 0, tile < tiles - 1
+        inner = [
+            jnp.logical_or(
+                jnp.logical_and(core == turn, above), jnp.logical_and(core != turn, below)
+            )
+            for turn in range(2)
+        ]
         for col in range(COLS):
             lanes = pl.ds(128 * col, 128)
             for buffer in (here, there):
@@ -120,10 +119,8 @@
                     field_imag,
                 ]
                 keep = None
-                if piece == 0:
-                    keep = jnp.broadcast_to(tile > 0, (ROWS, 128))
-                if piece == 2:
-                    keep = jnp.broadcast_to(tile < tiles - 1, (ROWS, 128))
+                if piece != 1:
+                    keep = jnp.broadcast_to(inner[piece // 2], (ROWS, 128))
                 edge = None
                 if col == 0:
                     edge = (lane2 != 0) | (core == 0)
@@ -133,8 +130,8 @@
                     keep = edge if keep is None else keep & edge
                 if keep is not None:
                     values = [jnp.where(keep, value, 0.0) for value in values]
-                inside = pl.ds(ROWS * piece, ROWS)
-                shifted = pl.ds(8 + ROWS * piece, ROWS)
+                inside = pl.ds(places[piece], ROWS)
+                shifted = pl.ds(8 + places[piece], ROWS)
                 gain[0, col, inside, :] = values[0]
                 gain[1, col, inside, :] = values[1]
                 offset[0, col, inside, :] = values[2]
@@ -145,8 +142,8 @@
         for phase in range(4):
 
             def step(_, carry):
-                sweep(here, there, gain, offset, lane, 4 * phase, 6 - phase)
-                sweep(there, here, gain, offset, lane, 4 * phase, 6 - phase)
+                sweep(here, there, gain, offset, 4 * phase, 6 - phase)
+                sweep(there, here, gain, offset, 4 * phase, 6 - phase)
                 return carry
 
             lax.fori_loop(0, SWEEPS // 8, step, 0)
@@ -184,15 +181,108 @@
     )(*operands)
 
 
+def weave(blocks, store, turned):
+    rows = blocks[0].shape[0]
+    for col in range(COLS):
+        turned[pl.ds(128 * col, 128), pl.ds(0, rows)] = blocks[col].T
+    for col in range(COLS):
+        store(col, turned[pl.ds(col, 128, stride=COLS), pl.ds(0, rows)].T)
+
+
+def weave_kernel(groups, *refs):
+    refs = list(refs)
+    turned = refs.pop()
+    outs = refs[-len(groups) :]
+    for group, out in zip(groups, outs):
+        parts = [(refs.pop(0), rows) for rows in group]
+        blocks = [
+            jnp.concatenate(
+                [part[pl.ds(0, rows), pl.ds(128 * col, 128)] for part, rows in parts], axis=0
+            )
+            for col in range(COLS)
+        ]
+
+        def store(col, value):
+            out[:, pl.ds(128 * col, 128)] = value
+
+        weave(blocks, store, turned)
+
+
+def woven(*groups):
+    whole = pl.BlockSpec(memory_space=pltpu.VMEM)
+    sizes = [[rows for _, rows in group] for group in groups]
+    operands = [value for group in groups for value, _ in group]
+    return pl.pallas_call(
+        functools.partial(weave_kernel, sizes),
+        out_shape=[jax.ShapeDtypeStruct((sum(rows), WINDOW), jnp.float32) for rows in sizes],
+        in_specs=[whole] * len(operands),
+        out_specs=[whole] * len(groups),
+        scratch_shapes=[pltpu.VMEM((WINDOW, 128), jnp.float32)],
+        compiler_params=pltpu.CompilerParams(vmem_limit_bytes=24 * 1024 * 1024),
+    )(*operands)
+
+
+def unweave_kernel(*refs):
+    refs = list(refs)
+    kept_out, sent_out, even_turned, odd_turned = refs[-4:]
+    evens, odds = refs[:-4][0::2], refs[:-4][1::2]
+    con = lax.axis_index("con")
+    chip, core = con // 2, con % 2
+    for pieces, turned in ((evens, even_turned), (odds, odd_turned)):
+        for col in range(COLS):
+            lanes = pl.ds(128 * col, 128)
+            value = None
+            for place, piece in enumerate(pieces):
+                block = jnp.concatenate([piece[0, :, lanes], piece[1, :, lanes]], axis=0)
+                value = block if value is None else jnp.where(chip == place, block, value)
+            turned[pl.ds(col, 128, stride=COLS), pl.ds(0, 2 * ROWS)] = value.T
+    for col in range(COLS - 1):
+        lanes = pl.ds(128 * col, 128)
+
+        def straight(turned, at):
+            return turned[pl.ds(128 * at, 128), pl.ds(0, 2 * ROWS)]
+
+        kept = jnp.where(core == 0, straight(even_turned, col), straight(odd_turned, col + 1)).T
+        sent = jnp.where(core == 0, straight(odd_turned, col), straight(even_turned, col + 1)).T
+        for plane in range(2):
+            rows = slice(ROWS * plane, ROWS * (plane + 1))
+            kept_out[plane, :, lanes] = kept[rows]
+            sent_out[plane, :, lanes] = sent[rows]
+
+
+def unwoven(pieces):
+    whole = pl.BlockSpec(memory_space=pltpu.VMEM)
+    half = jax.ShapeDtypeStruct((2, ROWS, LANES // 2), jnp.float32)
+    return pl.pallas_call(
+        unweave_kernel,
+        out_shape=[half, half],
+        in_specs=[whole] * len(pieces),
+        out_specs=[whole, whole],
+        scratch_shapes=[pltpu.VMEM((WINDOW, 128), jnp.float32)] * 2,
+        compiler_params=pltpu.CompilerParams(vmem_limit_bytes=24 * 1024 * 1024),
+    )(*pieces)
+
+
 def squared(field):
     return field[0] * field[0] + field[1] * field[1]
 
 
+def snake(turn):
+    cons, tiles = lax.axis_size("con"), lax.axis_size("tile")
+    pairs = []
+    for con in range(cons):
+        for tile in range(tiles):
+            there = tile + (1 if con % 2 == turn else -1)
+            other = (con, there) if 0 <= there < tiles else (con ^ 1, tile)
+            pairs.append((con * tiles + tile, other[0] * tiles + other[1]))
+    return pairs
+
+
 def beside(value):
     return (
-        lax.ppermute(value, "tile", ring("tile", 1)),
+        lax.ppermute(value, BOTH, snake(0)),
         value,
-        lax.ppermute(value, "tile", ring("tile", -1)),
+        lax.ppermute(value, BOTH, snake(1)),
     )
 
 
@@ -218,10 +308,12 @@
     square_odd = squared(field_odd)
     square_pair = squared(field_even) + square_odd
     later = window(base_speed, 0)
-    for shift in range(1, chips):
-        got = lax.ppermute(square_pair, "con", ring("con", -2 * shift))
-        later = later + jnp.where(chip + shift < chips, got, 0.0)
-    starts = beside(later + square_odd)
+    for step in range(1, chips):
+        pairs = [(i, i ^ (2 * step)) for i in range(2 * chips)]
+        got = lax.ppermute(square_pair, "con", pairs)
+        later = later + jnp.where(chip ^ step > chip, got, 0.0)
+    start, later = woven([(later + square_odd, ROWS)], [(later, ROWS)])
+    starts = beside(start)
 
     innovations = after(innovations, sent)
     lanes = jnp.arange(LANES, dtype=jnp.int32)
@@ -239,12 +331,14 @@
     force_even, force_odd, _ = shared(jnp.concatenate([forcing, tones]))
     tone_even, tone_odd = force_even[2 * ROWS :], force_odd[2 * ROWS :]
     flat = lambda field: field.reshape(2 * ROWS, WINDOW)
-    evens = beside(
-        jnp.concatenate([flat(field_even), force_even[: 2 * ROWS], window(depth, 0)])
-    )
-    odds = beside(jnp.concatenate([flat(after(field_odd, starts[0], starts[2], evens[0], evens[2])), force_odd[: 2 * ROWS]]))
-
-    even = odd = passed = None
+    even_bundle, odd_bundle = woven(
+        [(flat(field_even), 2 * ROWS), (force_even, 2 * ROWS), (window(depth, 0), ROWS)],
+        [(flat(field_odd), 2 * ROWS), (force_odd, 2 * ROWS)],
+    )
+    evens = beside(even_bundle)
+    odds = beside(after(odd_bundle, starts[0], starts[2], evens[0], evens[2]))
+
+    passed, results = None, []
     for now in range(chips):
         speeds = [starts]
         if now:
@@ -253,17 +347,16 @@
             ]
             speeds.append([up, passed, down])
         solved, passed, speed = section(now, speeds, evens, evens, tone_even, passed, later)
-        even = solved if even is None else jnp.where(chip == now, solved, even)
+        results.append(solved)
         solved, passed = section(now, [beside(speed)], odds, evens, tone_odd, passed)
-        odd = solved if odd is None else jnp.where(chip == now, solved, odd)
-
-    own = LANES // 2
-    sent = jnp.where(core == 0, odd[..., :own], even[..., -own:])
+        results.append(solved)
+
+    kept, sent = unwoven(results)
     got = lax.ppermute(sent, "con", swap)
     result = jnp.where(
         core == 0,
-        jnp.concatenate([even[..., :own], got], axis=-1),
-        jnp.concatenate([got, odd[..., -own:]], axis=-1),
+        jnp.concatenate([kept, got], axis=-1),
+        jnp.concatenate([got, kept], axis=-1),
     )
     return result[None]
 

time: 115 us -> 105 us (0.913)
  the two profiles are of different devices: /device:TPU:7 before, /device:TPU:31 now
where the time goes in v3:
time: 105 us; the launch traced here: 104 us
  starting transfers between devices  54.9 us (52%)
  waiting for transfers between devices  37.6 us (36%)
  Pallas kernels  7.02 us (7%)
  other arithmetic  1.96 us (2%)
    ppermute x9, waiting for transfers between devices, body(): lax.ppermute(passed, BOTH, hop_pairs(now - 1, shift))  24.4 us
    ppermute x7, starting transfers between devices, beside(): lax.ppermute(value, BOTH, snake(0))  23.5 us
    ppermute x1, starting transfers between devices, body(): got = lax.ppermute(sent, 'con', swap)  13.3 us
    ppermute x7, waiting for transfers between devices, beside(): lax.ppermute(value, BOTH, snake(1))  9.43 us
    ppermute x9, starting transfers between devices, body(): lax.ppermute(passed, BOTH, hop_pairs(now - 1, shift))  7.84 us
    ppermute x7, starting transfers between devices, beside(): lax.ppermute(value, BOTH, snake(1))  6 us
    pallas_call x8, Pallas kernels, section(): pl.pallas_call(functools.partial(section_kernel, chip, len(speeds), passe...  4.76 us
    ppermute x3, starting transfers between devices, body(): got = lax.ppermute(square_pair, 'con', pairs)  3.34 us
  transfers between devices with their start and end apart: 29, of which 9 were waited for; matrix products, arithmetic and copies ran while one was open for 1% of the time, Pallas kernels for 2%

profile of v3, /device:TPU:31, one launch (start us, length us, event | category | flops | bytes accessed | tf_op | source)
XLA Modules:
  0.0 104.3 jit_solution(486824825607043226)
XLA Ops:
  0.0 1.0 %slice_select_fusion = f32[2,16,1152]{2,1,0:T(8,128)S(1)} fusion(f32[2,16,2048]{2,1,0:T(8,128)} %bitcast.25, pred[]{:T(512)S(6)} %eq.25), kind=kLoop, calls=%fused_computation.6 | loop fusion | flops 36864 | bytes 442369 | tf_op jit(solution)/shard_map/jit(_where)/select_n | solution.py:300
  1.1 0.8 collective-permute-start
  2.6 0.9 convolution_add_fusion
  3.5 0.0 copy-start.1
  3.5 0.0 copy-start
  3.5 0.1 collective-permute-start.6
  3.6 0.8 copy-done.1
  4.4 0.0 collective-permute-done
  4.4 0.1 copy-done
  4.6 0.3 collective-permute-start.3
  4.9 2.1 %collective-permute-start.2 = (f32[16,1152]{1,0:T(8,128)S(1)}, f32[16,1152]{1,0:T(8,128)S(1)}, u32[]{:S(2)}, u32[]{:S(2)}) collective-permute-start(f32[16,1152]{1,0:T(8,128)S(1)} %fusion.5), channel_id=1, source_target_pairs={{0,128},{32,160},{64,192},{96,224},{128,0},{160,32},{192,64},{224,... | collective-permute-start | bytes 221192 | tf_op jit(solution)/shard_map/ppermute | solution.py:313
  7.0 0.9 collective-permute-start.1
  7.9 0.0 collective-permute-done.6
  8.0 0.0 copy-start.2
  8.0 0.8 shard_map.77
  8.8 1.7 %collective-permute-start.8 = (f32[80,1152]{1,0:T(8,128)S(1)}, f32[80,1152]{1,0:T(8,128)S(1)}, u32[]{:S(2)}, u32[]{:S(2)}) collective-permute-start(f32[80,1152]{1,0:T(8,128)S(1)} %get-tuple-element.34.refs_4_.refs_7_.refs_10_), channel_id=1, source_target_pairs={{0,32},{1,0},{2,1},{3,2},{4,3},{5,4},{6,5},{7,6},{8,7},{9,8},{10,9... | collective-permute-start | bytes 1105928 | tf_op jit(solution)/shard_map/ppermute | solution.py:285
  10.5 4.2 %collective-permute-start.7 = (f32[80,1152]{1,0:T(8,128)S(1)}, f32[80,1152]{1,0:T(8,128)S(1)}, u32[]{:S(2)}, u32[]{:S(2)}) collective-permute-start(f32[80,1152]{1,0:T(8,128)S(1)} %get-tuple-element.34.refs_4_.refs_7_.refs_10_), channel_id=1, source_target_pairs={{0,1},{1,2},{2,3},{3,4},{4,5},{5,6},{6,7},{7,8},{8,9},{9,10},{10,1... | collective-permute-start | bytes 1105928 | tf_op jit(solution)/shard_map/ppermute | solution.py:283
  14.7 0.0 collective-permute-done.3
  14.7 0.0 collective-permute-done.2
  14.7 0.0 collective-permute-done.1
  14.7 0.1 fusion.7
  14.8 0.8 shard_map.76
  15.6 0.1 collective-permute-start.5
  15.6 3.6 %collective-permute-start.4 = (f32[16,1152]{1,0:T(8,128)S(1)}, f32[16,1152]{1,0:T(8,128)S(1)}, u32[]{:S(2)}, u32[]{:S(2)}) collective-permute-start(f32[16,1152]{1,0:T(8,128)S(1)} %get-tuple-element.32.refs_1_), channel_id=1, source_target_pairs={{0,1},{1,2},{2,3},{3,4},{4,5},{5,6},{6,7},{7,8},{8,9},{9,10},{10,1... | collective-permute-start | bytes 221192 | tf_op jit(solution)/shard_map/ppermute | solution.py:283
  19.2 2.3 %collective-permute-done.5.refs_2_ = f32[16,1152]{1,0:T(8,128)S(1)} collective-permute-done((f32[16,1152]{1,0:T(8,128)S(1)}, f32[16,1152]{1,0:T(8,128)S(1)}, u32[]{:S(2)}, u32[]{:S(2)}) %collective-permute-start.5) | collective-permute-done | bytes 73760 | tf_op jit(solution)/shard_map/ppermute | solution.py:285
  21.6 1.9 %collective-permute-done.4.refs_0_ = f32[16,1152]{1,0:T(8,128)S(1)} collective-permute-done((f32[16,1152]{1,0:T(8,128)S(1)}, f32[16,1152]{1,0:T(8,128)S(1)}, u32[]{:S(2)}, u32[]{:S(2)}) %collective-permute-start.4) | collective-permute-done | bytes 73760 | tf_op jit(solution)/shard_map/ppermute | solution.py:283
  23.5 0.0 collective-permute-done.7.refs_3_.refs_6_.refs_9_
  23.5 0.5 collective-permute-start.12
  24.0 3.9 %collective-permute-start.11 = (f32[64,1152]{1,0:T(8,128)S(1)}, f32[64,1152]{1,0:T(8,128)S(1)}, u32[]{:S(2)}, u32[]{:S(2)}) collective-permute-start(f32[64,1152]{1,0:T(8,128)S(1)} %get-tuple-element.39.refs_4_), channel_id=1, source_target_pairs={{0,1},{1,2},{2,3},{3,4},{4,5},{5,6},{6,7},{7,8},{8,9},{9,10},{10,1... | collective-permute-start | bytes 884744 | tf_op jit(solution)/shard_map/ppermute | solution.py:283
  27.9 0.0 collective-permute-start.10
  27.9 3.6 %collective-permute-start.9 = (f32[16,1152]{1,0:T(8,128)S(1)}, f32[16,1152]{1,0:T(8,128)S(1)}, u32[]{:S(2)}, u32[]{:S(2)}) collective-permute-start(f32[16,1152]{1,0:T(8,128)S(1)} %get-tuple-element.37.refs_1_), channel_id=1, source_target_pairs={{0,1},{1,2},{2,3},{3,4},{4,5},{5,6},{6,7},{7,8},{8,9},{9,10},{10,1... | collective-permute-start | bytes 221192 | tf_op jit(solution)/shard_map/ppermute | solution.py:283
  31.4 1.7 %collective-permute-done.10.refs_2_ = f32[16,1152]{1,0:T(8,128)S(1)} collective-permute-done((f32[16,1152]{1,0:T(8,128)S(1)}, f32[16,1152]{1,0:T(8,128)S(1)}, u32[]{:S(2)}, u32[]{:S(2)}) %collective-permute-start.10) | collective-permute-done | bytes 73760 | tf_op jit(solution)/shard_map/ppermute | solution.py:285
  33.2 0.9 collective-permute-done.9.refs_0_
  34.1 0.7 collective-permute-start.15
  34.8 0.7 collective-permute-start.14
  35.4 0.7 collective-permute-start.13
  36.1 0.0 collective-permute-done.15.refs_5_
  36.1 0.0 collective-permute-done.13.refs_3_
  36.2 1.8 %collective-permute-start.17 = (f32[16,1152]{1,0:T(8,128)S(1)}, f32[16,1152]{1,0:T(8,128)S(1)}, u32[]{:S(2)}, u32[]{:S(2)}) collective-permute-start(f32[16,1152]{1,0:T(8,128)S(1)} %get-tuple-element.44.refs_1_), channel_id=1, source_target_pairs={{0,32},{1,0},{2,1},{3,2},{4,3},{5,4},{6,5},{7,6},{8,7},{9,8},{10,9... | collective-permute-start | bytes 221192 | tf_op jit(solution)/shard_map/ppermute | solution.py:285
  38.0 2.7 %collective-permute-start.16 = (f32[16,1152]{1,0:T(8,128)S(1)}, f32[16,1152]{1,0:T(8,128)S(1)}, u32[]{:S(2)}, u32[]{:S(2)}) collective-permute-start(f32[16,1152]{1,0:T(8,128)S(1)} %get-tuple-element.44.refs_1_), channel_id=1, source_target_pairs={{0,1},{1,2},{2,3},{3,4},{4,5},{5,6},{6,7},{7,8},{8,9},{9,10},{10,1... | collective-permute-start | bytes 221192 | tf_op jit(solution)/shard_map/ppermute | solution.py:283
  40.7 1.6 %collective-permute-done.17.refs_2_ = f32[16,1152]{1,0:T(8,128)S(1)} collective-permute-done((f32[16,1152]{1,0:T(8,128)S(1)}, f32[16,1152]{1,0:T(8,128)S(1)}, u32[]{:S(2)}, u32[]{:S(2)}) %collective-permute-start.17) | collective-permute-done | bytes 73760 | tf_op jit(solution)/shard_map/ppermute | solution.py:285
  42.3 0.7 collective-permute-start.20
  43.0 0.7 collective-permute-start.19
  43.7 0.7 collective-permute-start.18
  44.3 0.0 collective-permute-done.20.refs_5_
  44.4 0.0 collective-permute-done.18.refs_3_
  44.4 1.8 %collective-permute-start.22 = (f32[16,1152]{1,0:T(8,128)S(1)}, f32[16,1152]{1,0:T(8,128)S(1)}, u32[]{:S(2)}, u32[]{:S(2)}) collective-permute-start(f32[16,1152]{1,0:T(8,128)S(1)} %get-tuple-element.49.refs_1_), channel_id=1, source_target_pairs={{0,32},{1,0},{2,1},{3,2},{4,3},{5,4},{6,5},{7,6},{8,7},{9,8},{10,9... | collective-permute-start | bytes 221192 | tf_op jit(solution)/shard_map/ppermute | solution.py:285
  46.2 2.0 %collective-permute-start.21 = (f32[16,1152]{1,0:T(8,128)S(1)}, f32[16,1152]{1,0:T(8,128)S(1)}, u32[]{:S(2)}, u32[]{:S(2)}) collective-permute-start(f32[16,1152]{1,0:T(8,128)S(1)} %get-tuple-element.49.refs_1_), channel_id=1, source_target_pairs={{0,1},{1,2},{2,3},{3,4},{4,5},{5,6},{6,7},{7,8},{8,9},{9,10},{10,1... | collective-permute-start | bytes 221192 | tf_op jit(solution)/shard_map/ppermute | solution.py:283
  48.2 2.0 %collective-permute-done.22.refs_2_ = f32[16,1152]{1,0:T(8,128)S(1)} collective-permute-done((f32[16,1152]{1,0:T(8,128)S(1)}, f32[16,1152]{1,0:T(8,128)S(1)}, u32[]{:S(2)}, u32[]{:S(2)}) %collective-permute-start.22) | collective-permute-done | bytes 73760 | tf_op jit(solution)/shard_map/ppermute | solution.py:285
  50.2 1.3 %collective-permute-start.25 = (f32[16,1152]{1,0:T(8,128)S(1)}, f32[16,1152]{1,0:T(8,128)S(1)}, u32[]{:S(2)}, u32[]{:S(2)}) collective-permute-start(f32[16,1152]{1,0:T(8,128)S(1)} %get-tuple-element.52), channel_id=1, source_target_pairs={{129,192},{130,193},{131,194},{132,195},{133,196},{134,197},{135,1... | collective-permute-start | bytes 221192 | tf_op jit(solution)/shard_map/ppermute | solution.py:346
  51.5 1.3 %collective-permute-start.24 = (f32[16,1152]{1,0:T(8,128)S(1)}, f32[16,1152]{1,0:T(8,128)S(1)}, u32[]{:S(2)}, u32[]{:S(2)}) collective-permute-start(f32[16,1152]{1,0:T(8,128)S(1)} %get-tuple-element.52), channel_id=1, source_target_pairs={{128,192},{129,193},{130,194},{131,195},{132,196},{133,197},{134,1... | collective-permute-start | bytes 221192 | tf_op jit(solution)/shard_map/ppermute | solution.py:346
  52.8 1.3 %collective-permute-start.23 = (f32[16,1152]{1,0:T(8,128)S(1)}, f32[16,1152]{1,0:T(8,128)S(1)}, u32[]{:S(2)}, u32[]{:S(2)}) collective-permute-start(f32[16,1152]{1,0:T(8,128)S(1)} %get-tuple-element.52), channel_id=1, source_target_pairs={{128,193},{129,194},{130,195},{131,196},{132,197},{133,198},{134,1... | collective-permute-start | bytes 221192 | tf_op jit(solution)/shard_map/ppermute | solution.py:346
  54.1 24.3 %collective-permute-done.25.refs_5_ = f32[16,1152]{1,0:T(8,128)S(1)} collective-permute-done((f32[16,1152]{1,0:T(8,128)S(1)}, f32[16,1152]{1,0:T(8,128)S(1)}, u32[]{:S(2)}, u32[]{:S(2)}) %collective-permute-start.25) | collective-permute-done | bytes 73760 | tf_op jit(solution)/shard_map/ppermute | solution.py:346
  78.4 0.0 collective-permute-done.23.refs_3_
  78.4 2.0 %shard_map.84 = (f32[2,16,1152]{2,1,0:T(8,128)S(1)}, f32[16,1152]{1,0:T(8,128)S(1)}, f32[16,1152]{1,0:T(8,128)S(1)}) custom-call(f32[16,1152]{1,0:T(8,128)S(1)} %collective-permute-done.4.refs_0_, f32[16,1152]{1,0:T(8,128)S(1)} %get-tuple-element.32.refs_1_, f32[16,1152]{1,0:T(8,128)S(1)} %collective-permute-done.5.refs_2_, ...), custom_call_target="tpu_custom_call" | custom-call | tf_op jit(solution)/shard_map/pallas_call | solution.py:172
  80.5 0.1 collective-permute-start.27
  80.6 3.6 %collective-permute-start.26 = (f32[16,1152]{1,0:T(8,128)S(1)}, f32[16,1152]{1,0:T(8,128)S(1)}, u32[]{:S(2)}, u32[]{:S(2)}) collective-permute-start(f32[16,1152]{1,0:T(8,128)S(1)} %get-tuple-element.54.refs_1_), channel_id=1, source_target_pairs={{0,1},{1,2},{2,3},{3,4},{4,5},{5,6},{6,7},{7,8},{8,9},{9,10},{10,1... | collective-permute-start | bytes 221192 | tf_op jit(solution)/shard_map/ppermute | solution.py:283
  84.2 1.7 %collective-permute-done.27.refs_2_ = f32[16,1152]{1,0:T(8,128)S(1)} collective-permute-done((f32[16,1152]{1,0:T(8,128)S(1)}, f32[16,1152]{1,0:T(8,128)S(1)}, u32[]{:S(2)}, u32[]{:S(2)}) %collective-permute-start.27) | collective-permute-done | bytes 73760 | tf_op jit(solution)/shard_map/ppermute | solution.py:285
  85.9 0.0 collective-permute-done.26.refs_0_
  85.9 2.7 %shard_map.85 = (f32[2,16,1152]{2,1,0:T(8,128)S(1)}, f32[16,1152]{1,0:T(8,128)}) custom-call(f32[16,1152]{1,0:T(8,128)S(1)} %collective-permute-done.26.refs_0_, f32[16,1152]{1,0:T(8,128)S(1)} %get-tuple-element.54.refs_1_, f32[16,1152]{1,0:T(8,128)S(1)} %collective-permute-done.27.refs_2_, f32[64,1152]{1,0:T(8,128)S(1)} %collective-permute-done.11.refs_3_, ...), custom_call_target="tpu_custom_call" | custom-call | tf_op jit(solution)/shard_map/pallas_call | solution.py:172
  88.6 0.7 shard_map.86
  89.2 13.3 %collective-permute-start.28 = (f32[2,16,1024]{2,1,0:T(8,128)S(1)}, f32[2,16,1024]{2,1,0:T(8,128)S(1)}, u32[]{:S(2)}, u32[]{:S(2)}) collective-permute-start(f32[2,16,1024]{2,1,0:T(8,128)S(1)} %get-tuple-element.58), channel_id=1, source_target_pairs={{0,32},{32,0},{64,96},{96,64},{128,160},{160,128},{192,224},{224,1... | collective-permute-start | bytes 393224 | tf_op jit(solution)/shard_map/ppermute | solution.py:355
  102.5 1.0 collective-permute-done.28
  103.5 0.7 maximum_select_fusion
  (31 shorter events, 0.2 us)
Async XLA Ops:
  0.0 2.5 %copy-start.4 = (s32[256]{0:T(256)S(1)}, s32[256]{0:T(256)}, u32[]{:S(2)}) copy-start(s32[256]{0:T(256)} %param.10) | copy-start | bytes 3076
  0.0 2.5 %copy-start.3 = (f32[1,2,256]{2,1,0:T(2,128)S(1)}, f32[1,2,256]{2,1,0:T(2,128)}, u32[]{:S(2)}) copy-start(f32[1,2,256]{2,1,0:T(2,128)} %param.9) | copy-start | bytes 6148
  0.0 2.5 %copy-start.5 = (f32[1,2,16,2048]{3,2,1,0:T(8,128)S(1)}, f32[1,2,16,2048]{3,2,1,0:T(8,128)}, u32[]{:S(2)}) copy-start(f32[1,2,16,2048]{3,2,1,0:T(8,128)} %param.8) | copy-start | bytes 786436
  1.1 3.4 %collective-permute-start = (f32[2,16,1152]{2,1,0:T(8,128)S(1)}, f32[2,16,1152]{2,1,0:T(8,128)S(1)}, u32[]{:S(2)}, u32[]{:S(2)}) collective-permute-start(f32[2,16,1152]{2,1,0:T(8,128)S(1)} %slice_select_fusion), channel_id=1, source_target_pairs={{0,32},{32,0},{64,96},{96,64},{128,160},{160,128},{192,224},{224,1... | collective-permute-start | bytes 442376 | tf_op jit(solution)/shard_map/ppermute | solution.py:304
  3.5 0.9 copy-start.1
  3.5 1.0 copy-start
  3.5 4.4 %collective-permute-start.6 = (f32[40,1152]{1,0:T(8,128)S(1)}, f32[40,1152]{1,0:T(8,128)S(1)}, u32[]{:S(2)}, u32[]{:S(2)}) collective-permute-start(f32[40,1152]{1,0:T(8,128)S(1)} %broadcast_select_fusion), channel_id=1, source_target_pairs={{0,32},{32,0},{64,96},{96,64},{128,160},{160,128},{192,224},{224,1... | collective-permute-start | bytes 552968 | tf_op jit(solution)/shard_map/ppermute | solution.py:304
  4.6 10.1 %collective-permute-start.3 = (f32[16,1152]{1,0:T(8,128)S(1)}, f32[16,1152]{1,0:T(8,128)S(1)}, u32[]{:S(2)}, u32[]{:S(2)}) collective-permute-start(f32[16,1152]{1,0:T(8,128)S(1)} %fusion.5), channel_id=1, source_target_pairs={{0,192},{32,224},{64,128},{96,160},{128,64},{160,96},{192,0},{224,... | collective-permute-start | bytes 221192 | tf_op jit(solution)/shard_map/ppermute | solution.py:313
  4.9 9.9 %collective-permute-start.2 = (f32[16,1152]{1,0:T(8,128)S(1)}, f32[16,1152]{1,0:T(8,128)S(1)}, u32[]{:S(2)}, u32[]{:S(2)}) collective-permute-start(f32[16,1152]{1,0:T(8,128)S(1)} %fusion.5), channel_id=1, source_target_pairs={{0,128},{32,160},{64,192},{96,224},{128,0},{160,32},{192,64},{224,... | collective-permute-start | bytes 221192 | tf_op jit(solution)/shard_map/ppermute | solution.py:313
  7.0 7.7 %collective-permute-start.1 = (f32[16,1152]{1,0:T(8,128)S(1)}, f32[16,1152]{1,0:T(8,128)S(1)}, u32[]{:S(2)}, u32[]{:S(2)}) collective-permute-start(f32[16,1152]{1,0:T(8,128)S(1)} %fusion.5), channel_id=1, source_target_pairs={{0,64},{32,96},{64,0},{96,32},{128,192},{160,224},{192,128},{224,1... | collective-permute-start | bytes 221192 | tf_op jit(solution)/shard_map/ppermute | solution.py:313
  8.0 6.8 %copy-start.2 = (f32[16,2048]{1,0:T(8,128)S(1)}, f32[16,2048]{1,0:T(8,128)}, u32[]{:S(2)}) copy-start(f32[16,2048]{1,0:T(8,128)} %param.12) | copy-start | bytes 393220
  8.8 14.7 %collective-permute-start.8 = (f32[80,1152]{1,0:T(8,128)S(1)}, f32[80,1152]{1,0:T(8,128)S(1)}, u32[]{:S(2)}, u32[]{:S(2)}) collective-permute-start(f32[80,1152]{1,0:T(8,128)S(1)} %get-tuple-element.34.refs_4_.refs_7_.refs_10_), channel_id=1, source_target_pairs={{0,32},{1,0},{2,1},{3,2},{4,3},{5,4},{6,5},{7,6},{8,7},{9,8},{10,9... | collective-permute-start | bytes 1105928 | tf_op jit(solution)/shard_map/ppermute | solution.py:285
  10.5 13.0 %collective-permute-start.7 = (f32[80,1152]{1,0:T(8,128)S(1)}, f32[80,1152]{1,0:T(8,128)S(1)}, u32[]{:S(2)}, u32[]{:S(2)}) collective-permute-start(f32[80,1152]{1,0:T(8,128)S(1)} %get-tuple-element.34.refs_4_.refs_7_.refs_10_), channel_id=1, source_target_pairs={{0,1},{1,2},{2,3},{3,4},{4,5},{5,6},{6,7},{7,8},{8,9},{9,10},{10,1... | collective-permute-start | bytes 1105928 | tf_op jit(solution)/shard_map/ppermute | solution.py:283
  15.6 6.0 %collective-permute-start.5 = (f32[16,1152]{1,0:T(8,128)S(1)}, f32[16,1152]{1,0:T(8,128)S(1)}, u32[]{:S(2)}, u32[]{:S(2)}) collective-permute-start(f32[16,1152]{1,0:T(8,128)S(1)} %get-tuple-element.32.refs_1_), channel_id=1, source_target_pairs={{0,32},{1,0},{2,1},{3,2},{4,3},{5,4},{6,5},{7,6},{8,7},{9,8},{10,9... | collective-permute-start | bytes 221192 | tf_op jit(solution)/shard_map/ppermute | solution.py:285
  15.6 7.8 %collective-permute-start.4 = (f32[16,1152]{1,0:T(8,128)S(1)}, f32[16,1152]{1,0:T(8,128)S(1)}, u32[]{:S(2)}, u32[]{:S(2)}) collective-permute-start(f32[16,1152]{1,0:T(8,128)S(1)} %get-tuple-element.32.refs_1_), channel_id=1, source_target_pairs={{0,1},{1,2},{2,3},{3,4},{4,5},{5,6},{6,7},{7,8},{8,9},{9,10},{10,1... | collective-permute-start | bytes 221192 | tf_op jit(solution)/shard_map/ppermute | solution.py:283
  23.5 10.6 %collective-permute-start.12 = (f32[64,1152]{1,0:T(8,128)S(1)}, f32[64,1152]{1,0:T(8,128)S(1)}, u32[]{:S(2)}, u32[]{:S(2)}) collective-permute-start(f32[64,1152]{1,0:T(8,128)S(1)} %get-tuple-element.39.refs_4_), channel_id=1, source_target_pairs={{0,32},{1,0},{2,1},{3,2},{4,3},{5,4},{6,5},{7,6},{8,7},{9,8},{10,9... | collective-permute-start | bytes 884744 | tf_op jit(solution)/shard_map/ppermute | solution.py:285
  24.0 10.1 %collective-permute-start.11 = (f32[64,1152]{1,0:T(8,128)S(1)}, f32[64,1152]{1,0:T(8,128)S(1)}, u32[]{:S(2)}, u32[]{:S(2)}) collective-permute-start(f32[64,1152]{1,0:T(8,128)S(1)} %get-tuple-element.39.refs_4_), channel_id=1, source_target_pairs={{0,1},{1,2},{2,3},{3,4},{4,5},{5,6},{6,7},{7,8},{8,9},{9,10},{10,1... | collective-permute-start | bytes 884744 | tf_op jit(solution)/shard_map/ppermute | solution.py:283
  27.9 5.3 %collective-permute-start.10 = (f32[16,1152]{1,0:T(8,128)S(1)}, f32[16,1152]{1,0:T(8,128)S(1)}, u32[]{:S(2)}, u32[]{:S(2)}) collective-permute-start(f32[16,1152]{1,0:T(8,128)S(1)} %get-tuple-element.37.refs_1_), channel_id=1, source_target_pairs={{0,32},{1,0},{2,1},{3,2},{4,3},{5,4},{6,5},{7,6},{8,7},{9,8},{10,9... | collective-permute-start | bytes 221192 | tf_op jit(solution)/shard_map/ppermute | solution.py:285
  27.9 6.2 %collective-permute-start.9 = (f32[16,1152]{1,0:T(8,128)S(1)}, f32[16,1152]{1,0:T(8,128)S(1)}, u32[]{:S(2)}, u32[]{:S(2)}) collective-permute-start(f32[16,1152]{1,0:T(8,128)S(1)} %get-tuple-element.37.refs_1_), channel_id=1, source_target_pairs={{0,1},{1,2},{2,3},{3,4},{4,5},{5,6},{6,7},{7,8},{8,9},{9,10},{10,1... | collective-permute-start | bytes 221192 | tf_op jit(solution)/shard_map/ppermute | solution.py:283
  34.1 2.0 %collective-permute-start.15 = (f32[16,1152]{1,0:T(8,128)S(1)}, f32[16,1152]{1,0:T(8,128)S(1)}, u32[]{:S(2)}, u32[]{:S(2)}) collective-permute-start(f32[16,1152]{1,0:T(8,128)S(1)} %get-tuple-element.42), channel_id=1, source_target_pairs={{1,64},{2,65},{3,66},{4,67},{5,68},{6,69},{7,70},{8,71},{9,72},{10... | collective-permute-start | bytes 221192 | tf_op jit(solution)/shard_map/ppermute | solution.py:346
  34.8 1.4 %collective-permute-start.14 = (f32[16,1152]{1,0:T(8,128)S(1)}, f32[16,1152]{1,0:T(8,128)S(1)}, u32[]{:S(2)}, u32[]{:S(2)}) collective-permute-start(f32[16,1152]{1,0:T(8,128)S(1)} %get-tuple-element.42), channel_id=1, source_target_pairs={{0,64},{1,65},{2,66},{3,67},{4,68},{5,69},{6,70},{7,71},{8,72},{9,... | collective-permute-start | bytes 221192 | tf_op jit(solution)/shard_map/ppermute | solution.py:346
  35.4 0.7 collective-permute-start.13
  36.2 6.1 %collective-permute-start.17 = (f32[16,1152]{1,0:T(8,128)S(1)}, f32[16,1152]{1,0:T(8,128)S(1)}, u32[]{:S(2)}, u32[]{:S(2)}) collective-permute-start(f32[16,1152]{1,0:T(8,128)S(1)} %get-tuple-element.44.refs_1_), channel_id=1, source_target_pairs={{0,32},{1,0},{2,1},{3,2},{4,3},{5,4},{6,5},{7,6},{8,7},{9,8},{10,9... | collective-permute-start | bytes 221192 | tf_op jit(solution)/shard_map/ppermute | solution.py:285
  38.0 4.3 %collective-permute-start.16 = (f32[16,1152]{1,0:T(8,128)S(1)}, f32[16,1152]{1,0:T(8,128)S(1)}, u32[]{:S(2)}, u32[]{:S(2)}) collective-permute-start(f32[16,1152]{1,0:T(8,128)S(1)} %get-tuple-element.44.refs_1_), channel_id=1, source_target_pairs={{0,1},{1,2},{2,3},{3,4},{4,5},{5,6},{6,7},{7,8},{8,9},{9,10},{10,1... | collective-permute-start | bytes 221192 | tf_op jit(solution)/shard_map/ppermute | solution.py:283
  42.3 2.0 %collective-permute-start.20 = (f32[16,1152]{1,0:T(8,128)S(1)}, f32[16,1152]{1,0:T(8,128)S(1)}, u32[]{:S(2)}, u32[]{:S(2)}) collective-permute-start(f32[16,1152]{1,0:T(8,128)S(1)} %get-tuple-element.47), channel_id=1, source_target_pairs={{65,128},{66,129},{67,130},{68,131},{69,132},{70,133},{71,134},{72... | collective-permute-start | bytes 221192 | tf_op jit(solution)/shard_map/ppermute | solution.py:346
  43.0 1.4 %collective-permute-start.19 = (f32[16,1152]{1,0:T(8,128)S(1)}, f32[16,1152]{1,0:T(8,128)S(1)}, u32[]{:S(2)}, u32[]{:S(2)}) collective-permute-start(f32[16,1152]{1,0:T(8,128)S(1)} %get-tuple-element.47), channel_id=1, source_target_pairs={{64,128},{65,129},{66,130},{67,131},{68,132},{69,133},{70,134},{71... | collective-permute-start | bytes 221192 | tf_op jit(solution)/shard_map/ppermute | solution.py:346
  43.7 0.7 collective-permute-start.18
  44.4 5.8 %collective-permute-start.22 = (f32[16,1152]{1,0:T(8,128)S(1)}, f32[16,1152]{1,0:T(8,128)S(1)}, u32[]{:S(2)}, u32[]{:S(2)}) collective-permute-start(f32[16,1152]{1,0:T(8,128)S(1)} %get-tuple-element.49.refs_1_), channel_id=1, source_target_pairs={{0,32},{1,0},{2,1},{3,2},{4,3},{5,4},{6,5},{7,6},{8,7},{9,8},{10,9... | collective-permute-start | bytes 221192 | tf_op jit(solution)/shard_map/ppermute | solution.py:285
  46.2 4.0 %collective-permute-start.21 = (f32[16,1152]{1,0:T(8,128)S(1)}, f32[16,1152]{1,0:T(8,128)S(1)}, u32[]{:S(2)}, u32[]{:S(2)}) collective-permute-start(f32[16,1152]{1,0:T(8,128)S(1)} %get-tuple-element.49.refs_1_), channel_id=1, source_target_pairs={{0,1},{1,2},{2,3},{3,4},{4,5},{5,6},{6,7},{7,8},{8,9},{9,10},{10,1... | collective-permute-start | bytes 221192 | tf_op jit(solution)/shard_map/ppermute | solution.py:283
  50.2 28.2 %collective-permute-start.25 = (f32[16,1152]{1,0:T(8,128)S(1)}, f32[16,1152]{1,0:T(8,128)S(1)}, u32[]{:S(2)}, u32[]{:S(2)}) collective-permute-start(f32[16,1152]{1,0:T(8,128)S(1)} %get-tuple-element.52), channel_id=1, source_target_pairs={{129,192},{130,193},{131,194},{132,195},{133,196},{134,197},{135,1... | collective-permute-start | bytes 221192 | tf_op jit(solution)/shard_map/ppermute | solution.py:346
  51.5 26.9 %collective-permute-start.24 = (f32[16,1152]{1,0:T(8,128)S(1)}, f32[16,1152]{1,0:T(8,128)S(1)}, u32[]{:S(2)}, u32[]{:S(2)}) collective-permute-start(f32[16,1152]{1,0:T(8,128)S(1)} %get-tuple-element.52), channel_id=1, source_target_pairs={{128,192},{129,193},{130,194},{131,195},{132,196},{133,197},{134,1... | collective-permute-start | bytes 221192 | tf_op jit(solution)/shard_map/ppermute | solution.py:346
  52.8 25.6 %collective-permute-start.23 = (f32[16,1152]{1,0:T(8,128)S(1)}, f32[16,1152]{1,0:T(8,128)S(1)}, u32[]{:S(2)}, u32[]{:S(2)}) collective-permute-start(f32[16,1152]{1,0:T(8,128)S(1)} %get-tuple-element.52), channel_id=1, source_target_pairs={{128,193},{129,194},{130,195},{131,196},{132,197},{133,198},{134,1... | collective-permute-start | bytes 221192 | tf_op jit(solution)/shard_map/ppermute | solution.py:346
  80.5 5.4 %collective-permute-start.27 = (f32[16,1152]{1,0:T(8,128)S(1)}, f32[16,1152]{1,0:T(8,128)S(1)}, u32[]{:S(2)}, u32[]{:S(2)}) collective-permute-start(f32[16,1152]{1,0:T(8,128)S(1)} %get-tuple-element.54.refs_1_), channel_id=1, source_target_pairs={{0,32},{1,0},{2,1},{3,2},{4,3},{5,4},{6,5},{7,6},{8,7},{9,8},{10,9... | collective-permute-start | bytes 221192 | tf_op jit(solution)/shard_map/ppermute | solution.py:285
  80.6 5.3 %collective-permute-start.26 = (f32[16,1152]{1,0:T(8,128)S(1)}, f32[16,1152]{1,0:T(8,128)S(1)}, u32[]{:S(2)}, u32[]{:S(2)}) collective-permute-start(f32[16,1152]{1,0:T(8,128)S(1)} %get-tuple-element.54.refs_1_), channel_id=1, source_target_pairs={{0,1},{1,2},{2,3},{3,4},{4,5},{5,6},{6,7},{7,8},{8,9},{9,10},{10,1... | collective-permute-start | bytes 221192 | tf_op jit(solution)/shard_map/ppermute | solution.py:283
  89.2 14.3 %collective-permute-start.28 = (f32[2,16,1024]{2,1,0:T(8,128)S(1)}, f32[2,16,1024]{2,1,0:T(8,128)S(1)}, u32[]{:S(2)}, u32[]{:S(2)}) collective-permute-start(f32[2,16,1024]{2,1,0:T(8,128)S(1)} %get-tuple-element.58), channel_id=1, source_target_pairs={{0,32},{32,0},{64,96},{96,64},{128,160},{160,128},{192,224},{224,1... | collective-permute-start | bytes 393224 | tf_op jit(solution)/shard_map/ppermute | solution.py:355

commit v4 on v3

--- a/solution.py
+++ b/solution.py
@@ -22,7 +22,7 @@
     tiles = lax.axis_size("tile")
     return [
         (con * tiles + tile, (con + 2) * tiles + tile + step)
-        for con, step in ((2 * chip, shift), (2 * chip + 1, -shift))
+        for con, step in ((2 * chip, -shift), (2 * chip + 1, shift))
         for tile in range(tiles)
         if 0 <= tile + step < tiles
     ]
@@ -57,11 +57,11 @@
             )
 
 
-def section_kernel(chip, speeds, carried, more, *refs):
+def section_kernel(chip, speeds, carried, more, first, *refs):
     refs = list(refs)
     take = lambda count: [refs.pop(0) for _ in range(count)]
     speed_refs = [take(3) for _ in range(speeds)]
-    field_refs, deep_refs = take(3), take(3)
+    field_refs, force_refs = take(3), take(3)
     (tone_ref,) = take(1)
     passed_ref = take(1)[0] if carried else None
     later_ref = take(1)[0] if more else None
@@ -78,12 +78,12 @@
         lane2 = lax.broadcasted_iota(jnp.int32, (ROWS, 128), 1)
         nothing = jnp.zeros((8, 128), jnp.float32)
         angular = jnp.broadcast_to(tone_ref[0:1, 0:128], (ROWS, 128))
-        first_row = pl.multiple_of(2 * ROWS * core, ROWS)
+        first_row = pl.multiple_of(2 * ROWS * (1 - core), ROWS)
         places = (first_row, ROWS, pl.multiple_of(2 * ROWS - first_row, ROWS))
         above, below = tile > 0, tile < tiles - 1
         inner = [
             jnp.logical_or(
-                jnp.logical_and(core == turn, above), jnp.logical_and(core != turn, below)
+                jnp.logical_and(core != turn, above), jnp.logical_and(core == turn, below)
             )
             for turn in range(2)
         ]
@@ -97,7 +97,7 @@
                 speed_sq = speed_refs[0][piece][:, lanes]
                 if speeds == 2:
                     speed_sq = speed_sq + speed_refs[1][piece][:, lanes]
-                deep = deep_refs[piece][pl.ds(4 * ROWS, ROWS), lanes]
+                deep = force_refs[piece][pl.ds(4 * ROWS, ROWS), lanes]
                 drag = DRAG_COEF * jnp.sqrt(speed_sq)
                 scaled = deep / (drag * drag + angular * angular)
                 gain_real = scaled * drag
@@ -108,7 +108,9 @@
                 inv_real = diag_real * inverse
                 inv_imag = -diag_imag * inverse
                 field_real, field_imag, force_real, force_imag = (
-                    field_refs[piece][pl.ds(ROWS * part, ROWS), lanes] for part in range(4)
+                    part[piece][pl.ds(first + ROWS * plane, ROWS), lanes]
+                    for part in (field_refs, force_refs)
+                    for plane in range(2)
                 )
                 values = [
                     gain_real * inv_real - gain_imag * inv_imag,
@@ -161,17 +163,17 @@
                 speed_out[:, lanes] = total + later_ref[:, lanes]
 
 
-def section(chip, speeds, fields, deeps, tone, passed=None, later=None):
+def section(chip, speeds, fields, forces, first, tone, passed=None, later=None):
     tile_shape = jax.ShapeDtypeStruct((ROWS, WINDOW), jnp.float32)
     pair_shape = jax.ShapeDtypeStruct((2, ROWS, WINDOW), jnp.float32)
-    operands = [piece for term in speeds for piece in term] + [*fields, *deeps, tone]
+    operands = [piece for term in speeds for piece in term] + [*fields, *forces, tone]
     operands += [value for value in (passed, later) if value is not None]
     outs = [pair_shape, tile_shape] + ([tile_shape] if later is not None else [])
     whole = pl.BlockSpec(memory_space=pltpu.VMEM)
     vmem = lambda rows: pltpu.VMEM((2, COLS, rows, 128), jnp.float32)
     return pl.pallas_call(
         functools.partial(
-            section_kernel, chip, len(speeds), passed is not None, later is not None
+            section_kernel, chip, len(speeds), passed is not None, later is not None, first
         ),
         out_shape=outs,
         in_specs=[whole] * len(operands),
@@ -272,7 +274,7 @@
     pairs = []
     for con in range(cons):
         for tile in range(tiles):
-            there = tile + (1 if con % 2 == turn else -1)
+            there = tile + (1 if con % 2 != turn else -1)
             other = (con, there) if 0 <= there < tiles else (con ^ 1, tile)
             pairs.append((con * tiles + tile, other[0] * tiles + other[1]))
     return pairs
@@ -305,6 +307,7 @@
         return jnp.where(core == 0, mine, got), jnp.where(core == 0, got, mine), sent
 
     field_even, field_odd, sent = shared(first_guess[0])
+    raw_first, _, raw_last = beside(after(first_guess, sent)[0])
     square_odd = squared(field_odd)
     square_pair = squared(field_even) + square_odd
     later = window(base_speed, 0)
@@ -331,12 +334,26 @@
     force_even, force_odd, _ = shared(jnp.concatenate([forcing, tones]))
     tone_even, tone_odd = force_even[2 * ROWS :], force_odd[2 * ROWS :]
     flat = lambda field: field.reshape(2 * ROWS, WINDOW)
-    even_bundle, odd_bundle = woven(
-        [(flat(field_even), 2 * ROWS), (force_even, 2 * ROWS), (window(depth, 0), ROWS)],
-        [(flat(field_odd), 2 * ROWS), (force_odd, 2 * ROWS)],
-    )
-    evens = beside(even_bundle)
-    odds = beside(after(odd_bundle, starts[0], starts[2], evens[0], evens[2]))
+    forces, fields = woven(
+        [(force_even, 2 * ROWS), (force_odd, 2 * ROWS), (window(depth, 0), ROWS)],
+        [(flat(field_even), 2 * ROWS), (flat(field_odd), 2 * ROWS)],
+    )
+    forces = beside(forces)
+    given = [window(value, 1) for value in (raw_first, raw_last)]
+    got = lax.ppermute(
+        jnp.where(core == 0, jnp.stack(given), jnp.stack(given[::-1])), "con", swap
+    )
+    sides = []
+    for value, pair in ((raw_first, (got[0], got[1])), (raw_last, (got[1], got[0]))):
+        mine = window(value, 0)
+        sides.append(
+            [
+                (flat(jnp.where(core == 0, mine, pair[1])), 2 * ROWS),
+                (flat(jnp.where(core == 0, pair[0], mine)), 2 * ROWS),
+            ]
+        )
+    field_first, field_last = woven(*sides)
+    fields = (field_first, fields, field_last)
 
     passed, results = None, []
     for now in range(chips):
@@ -346,9 +363,9 @@
                 lax.ppermute(passed, BOTH, hop_pairs(now - 1, shift)) for shift in (1, -1, 0)
             ]
             speeds.append([up, passed, down])
-        solved, passed, speed = section(now, speeds, evens, evens, tone_even, passed, later)
+        solved, passed, speed = section(now, speeds, fields, forces, 0, tone_even, passed, later)
         results.append(solved)
-        solved, passed = section(now, [beside(speed)], odds, evens, tone_odd, passed)
+        solved, passed = section(now, [beside(speed)], fields, forces, 2 * ROWS, tone_odd, passed)
         results.append(solved)
 
     kept, sent = unwoven(results)

time: 105 us -> 99.9 us (0.951)
  the two profiles are of different devices: /device:TPU:31 before, /device:TPU:7 now
where the time goes in v4:
time: 99.9 us; the launch traced here: 98.6 us
  starting transfers between devices  43.2 us (43%)
  waiting for transfers between devices  43.1 us (43%)
  Pallas kernels  7.85 us (8%)
  other arithmetic  2.1 us (2%)
  between operations  1.03 us (1%)
    ppermute x9, waiting for transfers between devices, body(): lax.ppermute(passed, BOTH, hop_pairs(now - 1, shift))  25 us
    ppermute x7, starting transfers between devices, beside(): lax.ppermute(value, BOTH, snake(1))  21.3 us
    ppermute x7, waiting for transfers between devices, beside(): lax.ppermute(value, BOTH, snake(0))  11.3 us
    ppermute x9, starting transfers between devices, body(): lax.ppermute(passed, BOTH, hop_pairs(now - 1, shift))  7.21 us
    ppermute x7, waiting for transfers between devices, beside(): lax.ppermute(value, BOTH, snake(1))  5.76 us
    ppermute x1, starting transfers between devices, body(): got = lax.ppermute(sent, 'con', swap)  5.31 us
    pallas_call x8, Pallas kernels, section(): pl.pallas_call(functools.partial(section_kernel, chip, len(speeds), passe...  4.76 us
    ppermute x3, starting transfers between devices, body(): got = lax.ppermute(square_pair, 'con', pairs)  3.34 us
  transfers between devices with their start and end apart: 30, of which 12 were waited for; matrix products, arithmetic and copies ran while one was open for 1% of the time, Pallas kernels for 2%

profile of v4, /device:TPU:7, one launch (start us, length us, event | category | flops | bytes accessed | tf_op | source)
XLA Modules:
  0.0 98.6 jit_solution(12226069015016343127)
XLA Ops:
  0.0 1.1 %slice_select_fusion.2 = f32[2,16,1152]{2,1,0:T(8,128)S(1)} fusion(f32[2,16,2048]{2,1,0:T(8,128)} %bitcast.50, pred[]{:T(512)S(6)} %eq.25), kind=kLoop, calls=%fused_computation.17 | loop fusion | flops 36864 | bytes 442369 | tf_op jit(solution)/shard_map/jit(_where)/select_n | solution.py:302
  1.1 0.8 collective-permute-start
  1.9 0.1 collective-permute-start.7
  2.0 1.6 %collective-permute-start.6 = (f32[2,16,2048]{2,1,0:T(8,128)S(1)}, f32[2,16,2048]{2,1,0:T(8,128)S(1)}, u32[]{:S(2)}, u32[]{:S(2)}) collective-permute-start(f32[2,16,2048]{2,1,0:T(8,128)S(1)} %bitcast.52), channel_id=1, source_target_pairs={{0,32},{1,0},{2,1},{3,2},{4,3},{5,4},{6,5},{7,6},{8,7},{9,8},{10,9... | collective-permute-start | bytes 786440 | tf_op jit(solution)/shard_map/ppermute | solution.py:285
  4.2 0.9 convolution_add_fusion
  5.2 0.0 copy-start.1
  5.2 0.4 collective-permute-start.9
  5.6 0.4 copy-done.1
  6.1 0.0 collective-permute-done
  6.2 1.8 %collective-permute-start.3 = (f32[16,1152]{1,0:T(8,128)S(1)}, f32[16,1152]{1,0:T(8,128)S(1)}, u32[]{:S(2)}, u32[]{:S(2)}) collective-permute-start(f32[16,1152]{1,0:T(8,128)S(1)} %fusion.9), channel_id=1, source_target_pairs={{0,192},{32,224},{64,128},{96,160},{128,64},{160,96},{192,0},{224,... | collective-permute-start | bytes 221192 | tf_op jit(solution)/shard_map/ppermute | solution.py:316
  8.0 0.6 collective-permute-start.2
  8.6 0.0 collective-permute-done.9
  8.6 0.9 collective-permute-start.1
  9.6 0.8 shard_map.78
  10.4 0.0 collective-permute-done.7
  10.4 1.3 %collective-permute-start.11 = (f32[80,1152]{1,0:T(8,128)S(1)}, f32[80,1152]{1,0:T(8,128)S(1)}, u32[]{:S(2)}, u32[]{:S(2)}) collective-permute-start(f32[80,1152]{1,0:T(8,128)S(1)} %get-tuple-element.40.refs_7_.refs_10_), channel_id=1, source_target_pairs={{0,1},{1,2},{2,3},{3,4},{4,5},{5,6},{6,7},{7,8},{8,9},{9,10},{10,1... | collective-permute-start | bytes 1105928 | tf_op jit(solution)/shard_map/ppermute | solution.py:287
  11.7 0.0 collective-permute-done.6
  11.7 0.5 collective-permute-start.10
  12.3 0.0 copy-start.2
  12.3 0.0 collective-permute-done.3
  12.3 1.7 %collective-permute-start.8 = (f32[2,2,16,1152]{3,2,1,0:T(8,128)S(1)}, f32[2,2,16,1152]{3,2,1,0:T(8,128)S(1)}, u32[]{:S(2)}, u32[]{:S(2)}) collective-permute-start(f32[2,2,16,1152]{3,2,1,0:T(8,128)S(1)} %maximum_select_fusion), channel_id=1, source_target_pairs={{0,32},{32,0},{64,96},{96,64},{128,160},{160,128},{192,224},{224,1... | collective-permute-start | bytes 884744 | tf_op jit(solution)/shard_map/ppermute | solution.py:343
  14.0 0.1 fusion.11
  14.1 0.8 shard_map.76
  14.8 0.8 collective-permute-start.5
  15.7 1.1 %collective-permute-start.4 = (f32[16,1152]{1,0:T(8,128)S(1)}, f32[16,1152]{1,0:T(8,128)S(1)}, u32[]{:S(2)}, u32[]{:S(2)}) collective-permute-start(f32[16,1152]{1,0:T(8,128)S(1)} %get-tuple-element.34.refs_1_), channel_id=1, source_target_pairs={{0,32},{1,0},{2,1},{3,2},{4,3},{5,4},{6,5},{7,6},{8,7},{9,8},{10,9... | collective-permute-start | bytes 221192 | tf_op jit(solution)/shard_map/ppermute | solution.py:285
  16.7 0.0 collective-permute-done.8
  16.7 0.1 fusion.1
  16.8 0.8 shard_map.77
  17.6 1.8 %collective-permute-done.5.refs_2_ = f32[16,1152]{1,0:T(8,128)S(1)} collective-permute-done((f32[16,1152]{1,0:T(8,128)S(1)}, f32[16,1152]{1,0:T(8,128)S(1)}, u32[]{:S(2)}, u32[]{:S(2)}) %collective-permute-start.5) | collective-permute-done | bytes 73760 | tf_op jit(solution)/shard_map/ppermute | solution.py:287
  19.4 1.1 %collective-permute-done.4.refs_0_ = f32[16,1152]{1,0:T(8,128)S(1)} collective-permute-done((f32[16,1152]{1,0:T(8,128)S(1)}, f32[16,1152]{1,0:T(8,128)S(1)}, u32[]{:S(2)}, u32[]{:S(2)}) %collective-permute-start.4) | collective-permute-done | bytes 73760 | tf_op jit(solution)/shard_map/ppermute | solution.py:285
  20.5 3.0 %collective-permute-start.13 = (f32[16,1152]{1,0:T(8,128)S(1)}, f32[16,1152]{1,0:T(8,128)S(1)}, u32[]{:S(2)}, u32[]{:S(2)}) collective-permute-start(f32[16,1152]{1,0:T(8,128)S(1)} %get-tuple-element.43.refs_1_), channel_id=1, source_target_pairs={{0,1},{1,2},{2,3},{3,4},{4,5},{5,6},{6,7},{7,8},{8,9},{9,10},{10,1... | collective-permute-start | bytes 221192 | tf_op jit(solution)/shard_map/ppermute | solution.py:287
  23.5 1.2 %collective-permute-done.13.refs_2_ = f32[16,1152]{1,0:T(8,128)S(1)} collective-permute-done((f32[16,1152]{1,0:T(8,128)S(1)}, f32[16,1152]{1,0:T(8,128)S(1)}, u32[]{:S(2)}, u32[]{:S(2)}) %collective-permute-start.13) | collective-permute-done | bytes 73760 | tf_op jit(solution)/shard_map/ppermute | solution.py:287
  24.7 2.5 %collective-permute-done.12.refs_0_ = f32[16,1152]{1,0:T(8,128)S(1)} collective-permute-done((f32[16,1152]{1,0:T(8,128)S(1)}, f32[16,1152]{1,0:T(8,128)S(1)}, u32[]{:S(2)}, u32[]{:S(2)}) %collective-permute-start.12) | collective-permute-done | bytes 73760 | tf_op jit(solution)/shard_map/ppermute | solution.py:285
  27.2 0.7 collective-permute-start.16
  27.8 0.7 collective-permute-start.15
  28.5 0.7 collective-permute-start.14
  29.2 0.0 collective-permute-done.16.refs_5_
  29.2 0.0 collective-permute-done.15.refs_4_.refs_13_
  29.2 4.9 %collective-permute-start.18 = (f32[16,1152]{1,0:T(8,128)S(1)}, f32[16,1152]{1,0:T(8,128)S(1)}, u32[]{:S(2)}, u32[]{:S(2)}) collective-permute-start(f32[16,1152]{1,0:T(8,128)S(1)} %get-tuple-element.48.refs_1_), channel_id=1, source_target_pairs={{0,1},{1,2},{2,3},{3,4},{4,5},{5,6},{6,7},{7,8},{8,9},{9,10},{10,1... | collective-permute-start | bytes 221192 | tf_op jit(solution)/shard_map/ppermute | solution.py:287
  34.1 0.9 collective-permute-done.18.refs_2_
  35.0 3.6 %collective-permute-done.17.refs_0_ = f32[16,1152]{1,0:T(8,128)S(1)} collective-permute-done((f32[16,1152]{1,0:T(8,128)S(1)}, f32[16,1152]{1,0:T(8,128)S(1)}, u32[]{:S(2)}, u32[]{:S(2)}) %collective-permute-start.17) | collective-permute-done | bytes 73760 | tf_op jit(solution)/shard_map/ppermute | solution.py:285
  38.6 0.7 collective-permute-start.21
  39.3 0.7 collective-permute-start.20
  39.9 0.7 collective-permute-start.19
  40.6 0.0 collective-permute-done.20.refs_4_.refs_13_
  40.7 3.7 %collective-permute-start.23 = (f32[16,1152]{1,0:T(8,128)S(1)}, f32[16,1152]{1,0:T(8,128)S(1)}, u32[]{:S(2)}, u32[]{:S(2)}) collective-permute-start(f32[16,1152]{1,0:T(8,128)S(1)} %get-tuple-element.53.refs_1_), channel_id=1, source_target_pairs={{0,1},{1,2},{2,3},{3,4},{4,5},{5,6},{6,7},{7,8},{8,9},{9,10},{10,1... | collective-permute-start | bytes 221192 | tf_op jit(solution)/shard_map/ppermute | solution.py:287
  44.4 0.0 collective-permute-start.22
  44.4 0.9 collective-permute-done.23.refs_2_
  45.3 2.3 %collective-permute-done.22.refs_0_ = f32[16,1152]{1,0:T(8,128)S(1)} collective-permute-done((f32[16,1152]{1,0:T(8,128)S(1)}, f32[16,1152]{1,0:T(8,128)S(1)}, u32[]{:S(2)}, u32[]{:S(2)}) %collective-permute-start.22) | collective-permute-done | bytes 73760 | tf_op jit(solution)/shard_map/ppermute | solution.py:285
  47.6 1.3 %collective-permute-start.26 = (f32[16,1152]{1,0:T(8,128)S(1)}, f32[16,1152]{1,0:T(8,128)S(1)}, u32[]{:S(2)}, u32[]{:S(2)}) collective-permute-start(f32[16,1152]{1,0:T(8,128)S(1)} %get-tuple-element.56), channel_id=1, source_target_pairs={{128,193},{129,194},{130,195},{131,196},{132,197},{133,198},{134,1... | collective-permute-start | bytes 221192 | tf_op jit(solution)/shard_map/ppermute | solution.py:363
  48.8 1.3 %collective-permute-start.25 = (f32[16,1152]{1,0:T(8,128)S(1)}, f32[16,1152]{1,0:T(8,128)S(1)}, u32[]{:S(2)}, u32[]{:S(2)}) collective-permute-start(f32[16,1152]{1,0:T(8,128)S(1)} %get-tuple-element.56), channel_id=1, source_target_pairs={{128,192},{129,193},{130,194},{131,195},{132,196},{133,197},{134,1... | collective-permute-start | bytes 221192 | tf_op jit(solution)/shard_map/ppermute | solution.py:363
  50.1 0.7 collective-permute-start.24
  50.8 25.0 %collective-permute-done.26.refs_5_ = f32[16,1152]{1,0:T(8,128)S(1)} collective-permute-done((f32[16,1152]{1,0:T(8,128)S(1)}, f32[16,1152]{1,0:T(8,128)S(1)}, u32[]{:S(2)}, u32[]{:S(2)}) %collective-permute-start.26) | collective-permute-done | bytes 73760 | tf_op jit(solution)/shard_map/ppermute | solution.py:363
  75.8 0.0 collective-permute-done.24.refs_3_
  75.8 2.0 %shard_map.85 = (f32[2,16,1152]{2,1,0:T(8,128)S(1)}, f32[16,1152]{1,0:T(8,128)S(1)}, f32[16,1152]{1,0:T(8,128)S(1)}) custom-call(f32[16,1152]{1,0:T(8,128)S(1)} %collective-permute-done.4.refs_0_, f32[16,1152]{1,0:T(8,128)S(1)} %get-tuple-element.34.refs_1_, f32[16,1152]{1,0:T(8,128)S(1)} %collective-permute-done.5.refs_2_, ...), custom_call_target="tpu_custom_call" | custom-call | tf_op jit(solution)/shard_map/pallas_call | solution.py:174
  77.8 7.5 %collective-permute-start.28 = (f32[16,1152]{1,0:T(8,128)S(1)}, f32[16,1152]{1,0:T(8,128)S(1)}, u32[]{:S(2)}, u32[]{:S(2)}) collective-permute-start(f32[16,1152]{1,0:T(8,128)S(1)} %get-tuple-element.58.refs_1_), channel_id=1, source_target_pairs={{0,1},{1,2},{2,3},{3,4},{4,5},{5,6},{6,7},{7,8},{8,9},{9,10},{10,1... | collective-permute-start | bytes 221192 | tf_op jit(solution)/shard_map/ppermute | solution.py:287
  85.4 0.0 collective-permute-start.27
  85.4 0.9 collective-permute-done.28.refs_2_
  86.3 1.9 %collective-permute-done.27.refs_0_ = f32[16,1152]{1,0:T(8,128)S(1)} collective-permute-done((f32[16,1152]{1,0:T(8,128)S(1)}, f32[16,1152]{1,0:T(8,128)S(1)}, u32[]{:S(2)}, u32[]{:S(2)}) %collective-permute-start.27) | collective-permute-done | bytes 73760 | tf_op jit(solution)/shard_map/ppermute | solution.py:285
  88.2 2.7 %shard_map.86 = (f32[2,16,1152]{2,1,0:T(8,128)S(1)}, f32[16,1152]{1,0:T(8,128)}) custom-call(f32[16,1152]{1,0:T(8,128)S(1)} %collective-permute-done.27.refs_0_, f32[16,1152]{1,0:T(8,128)S(1)} %get-tuple-element.58.refs_1_, f32[16,1152]{1,0:T(8,128)S(1)} %collective-permute-done.28.refs_2_, f32[64,1152]{1,0:T(8,128)S(1)} %get-tuple-element.36.refs_3_.refs_6_, ...), custom_call_target="tpu_custom_call" | custom-call | tf_op jit(solution)/shard_map/pallas_call | solution.py:174
  90.9 0.7 shard_map.87
  91.5 5.3 %collective-permute-start.29 = (f32[2,16,1024]{2,1,0:T(8,128)S(1)}, f32[2,16,1024]{2,1,0:T(8,128)S(1)}, u32[]{:S(2)}, u32[]{:S(2)}) collective-permute-start(f32[2,16,1024]{2,1,0:T(8,128)S(1)} %get-tuple-element.62), channel_id=1, source_target_pairs={{0,32},{32,0},{64,96},{96,64},{128,160},{160,128},{192,224},{224,1... | collective-permute-start | bytes 393224 | tf_op jit(solution)/shard_map/ppermute | solution.py:372
  96.8 1.0 %collective-permute-done.29 = f32[2,16,1024]{2,1,0:T(8,128)S(1)} collective-permute-done((f32[2,16,1024]{2,1,0:T(8,128)S(1)}, f32[2,16,1024]{2,1,0:T(8,128)S(1)}, u32[]{:S(2)}, u32[]{:S(2)}) %collective-permute-start.29) | collective-permute-done | bytes 131104 | tf_op jit(solution)/shard_map/ppermute | solution.py:372
  97.8 0.7 maximum_select_fusion.1
  (38 shorter events, 0.3 us)
Async XLA Ops:
  0.0 1.9 %copy-start = (f32[1,2,16,2048]{3,2,1,0:T(8,128)S(1)}, f32[1,2,16,2048]{3,2,1,0:T(8,128)}, u32[]{:S(2)}) copy-start(f32[1,2,16,2048]{3,2,1,0:T(8,128)} %param.7) | copy-start | bytes 786436
  0.0 4.2 %copy-start.4 = (s32[256]{0:T(256)S(1)}, s32[256]{0:T(256)}, u32[]{:S(2)}) copy-start(s32[256]{0:T(256)} %param.10) | copy-start | bytes 3076
  0.0 4.2 %copy-start.3 = (f32[1,2,256]{2,1,0:T(2,128)S(1)}, f32[1,2,256]{2,1,0:T(2,128)}, u32[]{:S(2)}) copy-start(f32[1,2,256]{2,1,0:T(2,128)} %param.9) | copy-start | bytes 6148
  0.0 4.2 %copy-start.5 = (f32[1,2,16,2048]{3,2,1,0:T(8,128)S(1)}, f32[1,2,16,2048]{3,2,1,0:T(8,128)}, u32[]{:S(2)}) copy-start(f32[1,2,16,2048]{3,2,1,0:T(8,128)} %param.8) | copy-start | bytes 786436
  1.1 5.0 %collective-permute-start = (f32[2,16,1152]{2,1,0:T(8,128)S(1)}, f32[2,16,1152]{2,1,0:T(8,128)S(1)}, u32[]{:S(2)}, u32[]{:S(2)}) collective-permute-start(f32[2,16,1152]{2,1,0:T(8,128)S(1)} %slice_select_fusion.2), channel_id=1, source_target_pairs={{0,32},{32,0},{64,96},{96,64},{128,160},{160,128},{192,224},{224,1... | collective-permute-start | bytes 442376 | tf_op jit(solution)/shard_map/ppermute | solution.py:306
  1.9 8.5 %collective-permute-start.7 = (f32[2,16,2048]{2,1,0:T(8,128)S(1)}, f32[2,16,2048]{2,1,0:T(8,128)S(1)}, u32[]{:S(2)}, u32[]{:S(2)}) collective-permute-start(f32[2,16,2048]{2,1,0:T(8,128)S(1)} %bitcast.51), channel_id=1, source_target_pairs={{0,1},{1,2},{2,3},{3,4},{4,5},{5,6},{6,7},{7,8},{8,9},{9,10},{10,1... | collective-permute-start | bytes 786440 | tf_op jit(solution)/shard_map/ppermute | solution.py:287
  2.0 9.7 %collective-permute-start.6 = (f32[2,16,2048]{2,1,0:T(8,128)S(1)}, f32[2,16,2048]{2,1,0:T(8,128)S(1)}, u32[]{:S(2)}, u32[]{:S(2)}) collective-permute-start(f32[2,16,2048]{2,1,0:T(8,128)S(1)} %bitcast.52), channel_id=1, source_target_pairs={{0,32},{1,0},{2,1},{3,2},{4,3},{5,4},{6,5},{7,6},{8,7},{9,8},{10,9... | collective-permute-start | bytes 786440 | tf_op jit(solution)/shard_map/ppermute | solution.py:285
  5.2 0.9 copy-start.1
  5.2 3.4 %collective-permute-start.9 = (f32[40,1152]{1,0:T(8,128)S(1)}, f32[40,1152]{1,0:T(8,128)S(1)}, u32[]{:S(2)}, u32[]{:S(2)}) collective-permute-start(f32[40,1152]{1,0:T(8,128)S(1)} %broadcast_select_fusion), channel_id=1, source_target_pairs={{0,32},{32,0},{64,96},{96,64},{128,160},{160,128},{192,224},{224,1... | collective-permute-start | bytes 552968 | tf_op jit(solution)/shard_map/ppermute | solution.py:306
  6.2 6.1 %collective-permute-start.3 = (f32[16,1152]{1,0:T(8,128)S(1)}, f32[16,1152]{1,0:T(8,128)S(1)}, u32[]{:S(2)}, u32[]{:S(2)}) collective-permute-start(f32[16,1152]{1,0:T(8,128)S(1)} %fusion.9), channel_id=1, source_target_pairs={{0,192},{32,224},{64,128},{96,160},{128,64},{160,96},{192,0},{224,... | collective-permute-start | bytes 221192 | tf_op jit(solution)/shard_map/ppermute | solution.py:316
  8.0 6.0 %collective-permute-start.2 = (f32[16,1152]{1,0:T(8,128)S(1)}, f32[16,1152]{1,0:T(8,128)S(1)}, u32[]{:S(2)}, u32[]{:S(2)}) collective-permute-start(f32[16,1152]{1,0:T(8,128)S(1)} %fusion.9), channel_id=1, source_target_pairs={{0,128},{32,160},{64,192},{96,224},{128,0},{160,32},{192,64},{224,... | collective-permute-start | bytes 221192 | tf_op jit(solution)/shard_map/ppermute | solution.py:316
  8.6 5.4 %collective-permute-start.1 = (f32[16,1152]{1,0:T(8,128)S(1)}, f32[16,1152]{1,0:T(8,128)S(1)}, u32[]{:S(2)}, u32[]{:S(2)}) collective-permute-start(f32[16,1152]{1,0:T(8,128)S(1)} %fusion.9), channel_id=1, source_target_pairs={{0,64},{32,96},{64,0},{96,32},{128,192},{160,224},{192,128},{224,1... | collective-permute-start | bytes 221192 | tf_op jit(solution)/shard_map/ppermute | solution.py:316
  10.4 10.1 %collective-permute-start.11 = (f32[80,1152]{1,0:T(8,128)S(1)}, f32[80,1152]{1,0:T(8,128)S(1)}, u32[]{:S(2)}, u32[]{:S(2)}) collective-permute-start(f32[80,1152]{1,0:T(8,128)S(1)} %get-tuple-element.40.refs_7_.refs_10_), channel_id=1, source_target_pairs={{0,1},{1,2},{2,3},{3,4},{4,5},{5,6},{6,7},{7,8},{8,9},{9,10},{10,1... | collective-permute-start | bytes 1105928 | tf_op jit(solution)/shard_map/ppermute | solution.py:287
  11.7 8.8 %collective-permute-start.10 = (f32[80,1152]{1,0:T(8,128)S(1)}, f32[80,1152]{1,0:T(8,128)S(1)}, u32[]{:S(2)}, u32[]{:S(2)}) collective-permute-start(f32[80,1152]{1,0:T(8,128)S(1)} %get-tuple-element.40.refs_7_.refs_10_), channel_id=1, source_target_pairs={{0,32},{1,0},{2,1},{3,2},{4,3},{5,4},{6,5},{7,6},{8,7},{9,8},{10,9... | collective-permute-start | bytes 1105928 | tf_op jit(solution)/shard_map/ppermute | solution.py:285
  12.3 1.7 %copy-start.2 = (f32[16,2048]{1,0:T(8,128)S(1)}, f32[16,2048]{1,0:T(8,128)}, u32[]{:S(2)}) copy-start(f32[16,2048]{1,0:T(8,128)} %param.12) | copy-start | bytes 393220
  12.3 4.4 %collective-permute-start.8 = (f32[2,2,16,1152]{3,2,1,0:T(8,128)S(1)}, f32[2,2,16,1152]{3,2,1,0:T(8,128)S(1)}, u32[]{:S(2)}, u32[]{:S(2)}) collective-permute-start(f32[2,2,16,1152]{3,2,1,0:T(8,128)S(1)} %maximum_select_fusion), channel_id=1, source_target_pairs={{0,32},{32,0},{64,96},{96,64},{128,160},{160,128},{192,224},{224,1... | collective-permute-start | bytes 884744 | tf_op jit(solution)/shard_map/ppermute | solution.py:343
  14.8 4.6 %collective-permute-start.5 = (f32[16,1152]{1,0:T(8,128)S(1)}, f32[16,1152]{1,0:T(8,128)S(1)}, u32[]{:S(2)}, u32[]{:S(2)}) collective-permute-start(f32[16,1152]{1,0:T(8,128)S(1)} %get-tuple-element.34.refs_1_), channel_id=1, source_target_pairs={{0,1},{1,2},{2,3},{3,4},{4,5},{5,6},{6,7},{7,8},{8,9},{9,10},{10,1... | collective-permute-start | bytes 221192 | tf_op jit(solution)/shard_map/ppermute | solution.py:287
  15.7 4.9 %collective-permute-start.4 = (f32[16,1152]{1,0:T(8,128)S(1)}, f32[16,1152]{1,0:T(8,128)S(1)}, u32[]{:S(2)}, u32[]{:S(2)}) collective-permute-start(f32[16,1152]{1,0:T(8,128)S(1)} %get-tuple-element.34.refs_1_), channel_id=1, source_target_pairs={{0,32},{1,0},{2,1},{3,2},{4,3},{5,4},{6,5},{7,6},{8,7},{9,8},{10,9... | collective-permute-start | bytes 221192 | tf_op jit(solution)/shard_map/ppermute | solution.py:285
  20.5 4.2 %collective-permute-start.13 = (f32[16,1152]{1,0:T(8,128)S(1)}, f32[16,1152]{1,0:T(8,128)S(1)}, u32[]{:S(2)}, u32[]{:S(2)}) collective-permute-start(f32[16,1152]{1,0:T(8,128)S(1)} %get-tuple-element.43.refs_1_), channel_id=1, source_target_pairs={{0,1},{1,2},{2,3},{3,4},{4,5},{5,6},{6,7},{7,8},{8,9},{9,10},{10,1... | collective-permute-start | bytes 221192 | tf_op jit(solution)/shard_map/ppermute | solution.py:287
  23.5 3.7 %collective-permute-start.12 = (f32[16,1152]{1,0:T(8,128)S(1)}, f32[16,1152]{1,0:T(8,128)S(1)}, u32[]{:S(2)}, u32[]{:S(2)}) collective-permute-start(f32[16,1152]{1,0:T(8,128)S(1)} %get-tuple-element.43.refs_1_), channel_id=1, source_target_pairs={{0,32},{1,0},{2,1},{3,2},{4,3},{5,4},{6,5},{7,6},{8,7},{9,8},{10,9... | collective-permute-start | bytes 221192 | tf_op jit(solution)/shard_map/ppermute | solution.py:285
  27.2 2.0 %collective-permute-start.16 = (f32[16,1152]{1,0:T(8,128)S(1)}, f32[16,1152]{1,0:T(8,128)S(1)}, u32[]{:S(2)}, u32[]{:S(2)}) collective-permute-start(f32[16,1152]{1,0:T(8,128)S(1)} %get-tuple-element.46), channel_id=1, source_target_pairs={{0,65},{1,66},{2,67},{3,68},{4,69},{5,70},{6,71},{7,72},{8,73},{9,... | collective-permute-start | bytes 221192 | tf_op jit(solution)/shard_map/ppermute | solution.py:363
  27.8 1.4 %collective-permute-start.15 = (f32[16,1152]{1,0:T(8,128)S(1)}, f32[16,1152]{1,0:T(8,128)S(1)}, u32[]{:S(2)}, u32[]{:S(2)}) collective-permute-start(f32[16,1152]{1,0:T(8,128)S(1)} %get-tuple-element.46), channel_id=1, source_target_pairs={{0,64},{1,65},{2,66},{3,67},{4,68},{5,69},{6,70},{7,71},{8,72},{9,... | collective-permute-start | bytes 221192 | tf_op jit(solution)/shard_map/ppermute | solution.py:363
  28.5 0.7 collective-permute-start.14
  29.2 5.8 %collective-permute-start.18 = (f32[16,1152]{1,0:T(8,128)S(1)}, f32[16,1152]{1,0:T(8,128)S(1)}, u32[]{:S(2)}, u32[]{:S(2)}) collective-permute-start(f32[16,1152]{1,0:T(8,128)S(1)} %get-tuple-element.48.refs_1_), channel_id=1, source_target_pairs={{0,1},{1,2},{2,3},{3,4},{4,5},{5,6},{6,7},{7,8},{8,9},{9,10},{10,1... | collective-permute-start | bytes 221192 | tf_op jit(solution)/shard_map/ppermute | solution.py:287
  34.1 4.5 %collective-permute-start.17 = (f32[16,1152]{1,0:T(8,128)S(1)}, f32[16,1152]{1,0:T(8,128)S(1)}, u32[]{:S(2)}, u32[]{:S(2)}) collective-permute-start(f32[16,1152]{1,0:T(8,128)S(1)} %get-tuple-element.48.refs_1_), channel_id=1, source_target_pairs={{0,32},{1,0},{2,1},{3,2},{4,3},{5,4},{6,5},{7,6},{8,7},{9,8},{10,9... | collective-permute-start | bytes 221192 | tf_op jit(solution)/shard_map/ppermute | solution.py:285
  38.6 2.0 %collective-permute-start.21 = (f32[16,1152]{1,0:T(8,128)S(1)}, f32[16,1152]{1,0:T(8,128)S(1)}, u32[]{:S(2)}, u32[]{:S(2)}) collective-permute-start(f32[16,1152]{1,0:T(8,128)S(1)} %get-tuple-element.51), channel_id=1, source_target_pairs={{64,129},{65,130},{66,131},{67,132},{68,133},{69,134},{70,135},{71... | collective-permute-start | bytes 221192 | tf_op jit(solution)/shard_map/ppermute | solution.py:363
  39.3 1.4 %collective-permute-start.20 = (f32[16,1152]{1,0:T(8,128)S(1)}, f32[16,1152]{1,0:T(8,128)S(1)}, u32[]{:S(2)}, u32[]{:S(2)}) collective-permute-start(f32[16,1152]{1,0:T(8,128)S(1)} %get-tuple-element.51), channel_id=1, source_target_pairs={{64,128},{65,129},{66,130},{67,131},{68,132},{69,133},{70,134},{71... | collective-permute-start | bytes 221192 | tf_op jit(solution)/shard_map/ppermute | solution.py:363
  39.9 0.7 collective-permute-start.19
  40.7 4.6 %collective-permute-start.23 = (f32[16,1152]{1,0:T(8,128)S(1)}, f32[16,1152]{1,0:T(8,128)S(1)}, u32[]{:S(2)}, u32[]{:S(2)}) collective-permute-start(f32[16,1152]{1,0:T(8,128)S(1)} %get-tuple-element.53.refs_1_), channel_id=1, source_target_pairs={{0,1},{1,2},{2,3},{3,4},{4,5},{5,6},{6,7},{7,8},{8,9},{9,10},{10,1... | collective-permute-start | bytes 221192 | tf_op jit(solution)/shard_map/ppermute | solution.py:287
  44.4 3.2 %collective-permute-start.22 = (f32[16,1152]{1,0:T(8,128)S(1)}, f32[16,1152]{1,0:T(8,128)S(1)}, u32[]{:S(2)}, u32[]{:S(2)}) collective-permute-start(f32[16,1152]{1,0:T(8,128)S(1)} %get-tuple-element.53.refs_1_), channel_id=1, source_target_pairs={{0,32},{1,0},{2,1},{3,2},{4,3},{5,4},{6,5},{7,6},{8,7},{9,8},{10,9... | collective-permute-start | bytes 221192 | tf_op jit(solution)/shard_map/ppermute | solution.py:285
  47.6 28.2 %collective-permute-start.26 = (f32[16,1152]{1,0:T(8,128)S(1)}, f32[16,1152]{1,0:T(8,128)S(1)}, u32[]{:S(2)}, u32[]{:S(2)}) collective-permute-start(f32[16,1152]{1,0:T(8,128)S(1)} %get-tuple-element.56), channel_id=1, source_target_pairs={{128,193},{129,194},{130,195},{131,196},{132,197},{133,198},{134,1... | collective-permute-start | bytes 221192 | tf_op jit(solution)/shard_map/ppermute | solution.py:363
  48.8 26.9 %collective-permute-start.25 = (f32[16,1152]{1,0:T(8,128)S(1)}, f32[16,1152]{1,0:T(8,128)S(1)}, u32[]{:S(2)}, u32[]{:S(2)}) collective-permute-start(f32[16,1152]{1,0:T(8,128)S(1)} %get-tuple-element.56), channel_id=1, source_target_pairs={{128,192},{129,193},{130,194},{131,195},{132,196},{133,197},{134,1... | collective-permute-start | bytes 221192 | tf_op jit(solution)/shard_map/ppermute | solution.py:363
  50.1 25.6 %collective-permute-start.24 = (f32[16,1152]{1,0:T(8,128)S(1)}, f32[16,1152]{1,0:T(8,128)S(1)}, u32[]{:S(2)}, u32[]{:S(2)}) collective-permute-start(f32[16,1152]{1,0:T(8,128)S(1)} %get-tuple-element.56), channel_id=1, source_target_pairs={{129,192},{130,193},{131,194},{132,195},{133,196},{134,197},{135,1... | collective-permute-start | bytes 221192 | tf_op jit(solution)/shard_map/ppermute | solution.py:363
  77.8 8.4 %collective-permute-start.28 = (f32[16,1152]{1,0:T(8,128)S(1)}, f32[16,1152]{1,0:T(8,128)S(1)}, u32[]{:S(2)}, u32[]{:S(2)}) collective-permute-start(f32[16,1152]{1,0:T(8,128)S(1)} %get-tuple-element.58.refs_1_), channel_id=1, source_target_pairs={{0,1},{1,2},{2,3},{3,4},{4,5},{5,6},{6,7},{7,8},{8,9},{9,10},{10,1... | collective-permute-start | bytes 221192 | tf_op jit(solution)/shard_map/ppermute | solution.py:287
  85.4 2.8 %collective-permute-start.27 = (f32[16,1152]{1,0:T(8,128)S(1)}, f32[16,1152]{1,0:T(8,128)S(1)}, u32[]{:S(2)}, u32[]{:S(2)}) collective-permute-start(f32[16,1152]{1,0:T(8,128)S(1)} %get-tuple-element.58.refs_1_), channel_id=1, source_target_pairs={{0,32},{1,0},{2,1},{3,2},{4,3},{5,4},{6,5},{7,6},{8,7},{9,8},{10,9... | collective-permute-start | bytes 221192 | tf_op jit(solution)/shard_map/ppermute | solution.py:285
  91.5 6.3 %collective-permute-start.29 = (f32[2,16,1024]{2,1,0:T(8,128)S(1)}, f32[2,16,1024]{2,1,0:T(8,128)S(1)}, u32[]{:S(2)}, u32[]{:S(2)}) collective-permute-start(f32[2,16,1024]{2,1,0:T(8,128)S(1)} %get-tuple-element.62), channel_id=1, source_target_pairs={{0,32},{32,0},{64,96},{96,64},{128,160},{160,128},{192,224},{224,1... | collective-permute-start | bytes 393224 | tf_op jit(solution)/shard_map/ppermute | solution.py:372

commit v5 on v4

--- a/solution.py
+++ b/solution.py
@@ -315,7 +315,7 @@
         pairs = [(i, i ^ (2 * step)) for i in range(2 * chips)]
         got = lax.ppermute(square_pair, "con", pairs)
         later = later + jnp.where(chip ^ step > chip, got, 0.0)
-    start, later = woven([(later + square_odd, ROWS)], [(later, ROWS)])
+    (start,) = woven([(later + square_odd, ROWS)])
     starts = beside(start)
 
     innovations = after(innovations, sent)
@@ -352,7 +352,7 @@
                 (flat(jnp.where(core == 0, pair[0], mine)), 2 * ROWS),
             ]
         )
-    field_first, field_last = woven(*sides)
+    field_first, field_last, later = woven(*sides, [(later, ROWS)])
     fields = (field_first, fields, field_last)
 
     passed, results = None, []

time: 99.9 us -> 100 us (level)
  no operation moved by 1% of the time
where the time goes in v5:
time: 100 us; the launch traced here: 98.7 us
  starting transfers between devices  43.5 us (44%)
  waiting for transfers between devices  42.9 us (43%)
  Pallas kernels  7.82 us (8%)
  other arithmetic  2.1 us (2%)
  between operations  1.02 us (1%)
    ppermute x9, waiting for transfers between devices, body(): lax.ppermute(passed, BOTH, hop_pairs(now - 1, shift))  25 us
    ppermute x7, starting transfers between devices, beside(): lax.ppermute(value, BOTH, snake(1))  21.3 us
    ppermute x7, waiting for transfers between devices, beside(): lax.ppermute(value, BOTH, snake(0))  11.4 us
    ppermute x9, starting transfers between devices, body(): lax.ppermute(passed, BOTH, hop_pairs(now - 1, shift))  7.21 us
    ppermute x1, starting transfers between devices, body(): got = lax.ppermute(sent, 'con', swap)  5.65 us
    ppermute x7, waiting for transfers between devices, beside(): lax.ppermute(value, BOTH, snake(1))  5.49 us
    pallas_call x8, Pallas kernels, section(): pl.pallas_call(functools.partial(section_kernel, chip, len(speeds), passe...  4.76 us
    ppermute x3, starting transfers between devices, body(): got = lax.ppermute(square_pair, 'con', pairs)  3.34 us
  transfers between devices with their start and end apart: 30, of which 12 were waited for; matrix products, arithmetic and copies ran while one was open for 1% of the time, Pallas kernels for 2%

profile of v5, /device:TPU:7, one launch (start us, length us, event | category | flops | bytes accessed | tf_op | source)
XLA Modules:
  0.0 98.7 jit_solution(4255781550238152169)
XLA Ops:
  0.0 1.1 %slice_select_fusion.2 = f32[2,16,1152]{2,1,0:T(8,128)S(1)} fusion(f32[2,16,2048]{2,1,0:T(8,128)} %bitcast.50, pred[]{:T(512)S(6)} %eq.25), kind=kLoop, calls=%fused_computation.17 | loop fusion | flops 36864 | bytes 442369 | tf_op jit(solution)/shard_map/jit(_where)/select_n | solution.py:302
  1.1 0.8 collective-permute-start
  1.9 0.1 collective-permute-start.7
  2.0 1.6 %collective-permute-start.6 = (f32[2,16,2048]{2,1,0:T(8,128)S(1)}, f32[2,16,2048]{2,1,0:T(8,128)S(1)}, u32[]{:S(2)}, u32[]{:S(2)}) collective-permute-start(f32[2,16,2048]{2,1,0:T(8,128)S(1)} %bitcast.52), channel_id=1, source_target_pairs={{0,32},{1,0},{2,1},{3,2},{4,3},{5,4},{6,5},{7,6},{8,7},{9,8},{10,9... | collective-permute-start | bytes 786440 | tf_op jit(solution)/shard_map/ppermute | solution.py:285
  4.2 0.9 convolution_add_fusion
  5.2 0.0 copy-start.1
  5.2 0.4 collective-permute-start.9
  5.6 0.4 copy-done.1
  6.1 0.0 collective-permute-done
  6.2 1.8 %collective-permute-start.3 = (f32[16,1152]{1,0:T(8,128)S(1)}, f32[16,1152]{1,0:T(8,128)S(1)}, u32[]{:S(2)}, u32[]{:S(2)}) collective-permute-start(f32[16,1152]{1,0:T(8,128)S(1)} %fusion.9), channel_id=1, source_target_pairs={{0,192},{32,224},{64,128},{96,160},{128,64},{160,96},{192,0},{224,... | collective-permute-start | bytes 221192 | tf_op jit(solution)/shard_map/ppermute | solution.py:316
  8.0 0.6 collective-permute-start.2
  8.6 0.0 collective-permute-done.9
  8.6 0.9 collective-permute-start.1
  9.6 0.8 shard_map.78
  10.4 0.0 collective-permute-done.7
  10.4 1.3 %collective-permute-start.11 = (f32[80,1152]{1,0:T(8,128)S(1)}, f32[80,1152]{1,0:T(8,128)S(1)}, u32[]{:S(2)}, u32[]{:S(2)}) collective-permute-start(f32[80,1152]{1,0:T(8,128)S(1)} %get-tuple-element.38.refs_7_.refs_10_), channel_id=1, source_target_pairs={{0,1},{1,2},{2,3},{3,4},{4,5},{5,6},{6,7},{7,8},{8,9},{9,10},{10,1... | collective-permute-start | bytes 1105928 | tf_op jit(solution)/shard_map/ppermute | solution.py:287
  11.7 0.0 collective-permute-done.6
  11.7 0.5 collective-permute-start.10
  12.3 0.0 copy-start.2
  12.3 0.0 collective-permute-done.3
  12.3 1.7 %collective-permute-start.8 = (f32[2,2,16,1152]{3,2,1,0:T(8,128)S(1)}, f32[2,2,16,1152]{3,2,1,0:T(8,128)S(1)}, u32[]{:S(2)}, u32[]{:S(2)}) collective-permute-start(f32[2,2,16,1152]{3,2,1,0:T(8,128)S(1)} %maximum_select_fusion), channel_id=1, source_target_pairs={{0,32},{32,0},{64,96},{96,64},{128,160},{160,128},{192,224},{224,1... | collective-permute-start | bytes 884744 | tf_op jit(solution)/shard_map/ppermute | solution.py:343
  14.0 0.0 collective-permute-done.2
  14.0 0.1 fusion.11
  14.1 0.4 shard_map.76.refs_1_
  14.5 0.8 collective-permute-start.5
  15.3 1.1 %collective-permute-start.4 = (f32[16,1152]{1,0:T(8,128)S(1)}, f32[16,1152]{1,0:T(8,128)S(1)}, u32[]{:S(2)}, u32[]{:S(2)}) collective-permute-start(f32[16,1152]{1,0:T(8,128)S(1)} %shard_map.76.refs_1_), channel_id=1, source_target_pairs={{0,32},{1,0},{2,1},{3,2},{4,3},{5,4},{6,5},{7,6},{8,7},{9,8},{10,9... | collective-permute-start | bytes 221192 | tf_op jit(solution)/shard_map/ppermute | solution.py:285
  16.4 0.0 collective-permute-done.8
  16.4 0.1 fusion.1
  16.4 1.2 %shard_map.77 = (f32[64,1152]{1,0:T(8,128)S(1)}, f32[64,1152]{1,0:T(8,128)S(1)}, f32[16,1152]{1,0:T(8,128)S(1)}) custom-call(f32[32,1152]{1,0:T(8,128)S(1)} %bitcast.47, f32[32,1152]{1,0:T(8,128)S(1)} %bitcast.48, f32[32,1152]{1,0:T(8,128)S(1)} %bitcast.46, f32[32,1152]{1,0:T(8,128)S(1)} %bitcast.45, f32[16,1152]{1,0:T(8,128)S(1)} %get-tuple-element.62.refs_4_), custom_call_target="tpu_custom_call" | custom-call | tf_op jit(solution)/shard_map/pallas_call | solution.py:217
  17.6 1.6 %collective-permute-done.5.refs_2_ = f32[16,1152]{1,0:T(8,128)S(1)} collective-permute-done((f32[16,1152]{1,0:T(8,128)S(1)}, f32[16,1152]{1,0:T(8,128)S(1)}, u32[]{:S(2)}, u32[]{:S(2)}) %collective-permute-start.5) | collective-permute-done | bytes 73760 | tf_op jit(solution)/shard_map/ppermute | solution.py:287
  19.1 1.4 %collective-permute-done.4.refs_0_ = f32[16,1152]{1,0:T(8,128)S(1)} collective-permute-done((f32[16,1152]{1,0:T(8,128)S(1)}, f32[16,1152]{1,0:T(8,128)S(1)}, u32[]{:S(2)}, u32[]{:S(2)}) %collective-permute-start.4) | collective-permute-done | bytes 73760 | tf_op jit(solution)/shard_map/ppermute | solution.py:285
  20.5 0.0 collective-permute-done.11.refs_8_.refs_11_
  20.5 3.0 %collective-permute-start.13 = (f32[16,1152]{1,0:T(8,128)S(1)}, f32[16,1152]{1,0:T(8,128)S(1)}, u32[]{:S(2)}, u32[]{:S(2)}) collective-permute-start(f32[16,1152]{1,0:T(8,128)S(1)} %get-tuple-element.41.refs_1_), channel_id=1, source_target_pairs={{0,1},{1,2},{2,3},{3,4},{4,5},{5,6},{6,7},{7,8},{8,9},{9,10},{10,1... | collective-permute-start | bytes 221192 | tf_op jit(solution)/shard_map/ppermute | solution.py:287
  23.5 1.2 %collective-permute-done.13.refs_2_ = f32[16,1152]{1,0:T(8,128)S(1)} collective-permute-done((f32[16,1152]{1,0:T(8,128)S(1)}, f32[16,1152]{1,0:T(8,128)S(1)}, u32[]{:S(2)}, u32[]{:S(2)}) %collective-permute-start.13) | collective-permute-done | bytes 73760 | tf_op jit(solution)/shard_map/ppermute | solution.py:287
  24.7 2.1 %collective-permute-done.12.refs_0_ = f32[16,1152]{1,0:T(8,128)S(1)} collective-permute-done((f32[16,1152]{1,0:T(8,128)S(1)}, f32[16,1152]{1,0:T(8,128)S(1)}, u32[]{:S(2)}, u32[]{:S(2)}) %collective-permute-start.12) | collective-permute-done | bytes 73760 | tf_op jit(solution)/shard_map/ppermute | solution.py:285
  26.8 0.7 collective-permute-start.16
  27.5 0.7 collective-permute-start.15
  28.2 0.7 collective-permute-start.14
  28.8 0.0 collective-permute-done.16.refs_5_
  28.9 0.0 collective-permute-done.14.refs_3_
  28.9 4.9 %collective-permute-start.18 = (f32[16,1152]{1,0:T(8,128)S(1)}, f32[16,1152]{1,0:T(8,128)S(1)}, u32[]{:S(2)}, u32[]{:S(2)}) collective-permute-start(f32[16,1152]{1,0:T(8,128)S(1)} %get-tuple-element.46.refs_1_), channel_id=1, source_target_pairs={{0,1},{1,2},{2,3},{3,4},{4,5},{5,6},{6,7},{7,8},{8,9},{9,10},{10,1... | collective-permute-start | bytes 221192 | tf_op jit(solution)/shard_map/ppermute | solution.py:287
  33.8 0.0 collective-permute-start.17
  33.8 0.9 collective-permute-done.18.refs_2_
  34.7 3.5 %collective-permute-done.17.refs_0_ = f32[16,1152]{1,0:T(8,128)S(1)} collective-permute-done((f32[16,1152]{1,0:T(8,128)S(1)}, f32[16,1152]{1,0:T(8,128)S(1)}, u32[]{:S(2)}, u32[]{:S(2)}) %collective-permute-start.17) | collective-permute-done | bytes 73760 | tf_op jit(solution)/shard_map/ppermute | solution.py:285
  38.2 0.7 collective-permute-start.21
  38.8 0.7 collective-permute-start.20
  39.5 0.7 collective-permute-start.19
  40.2 0.0 collective-permute-done.21.refs_5_
  40.3 3.7 %collective-permute-start.23 = (f32[16,1152]{1,0:T(8,128)S(1)}, f32[16,1152]{1,0:T(8,128)S(1)}, u32[]{:S(2)}, u32[]{:S(2)}) collective-permute-start(f32[16,1152]{1,0:T(8,128)S(1)} %get-tuple-element.51.refs_1_), channel_id=1, source_target_pairs={{0,1},{1,2},{2,3},{3,4},{4,5},{5,6},{6,7},{7,8},{8,9},{9,10},{10,1... | collective-permute-start | bytes 221192 | tf_op jit(solution)/shard_map/ppermute | solution.py:287
  43.9 0.9 collective-permute-done.23.refs_2_
  44.8 2.7 %collective-permute-done.22.refs_0_ = f32[16,1152]{1,0:T(8,128)S(1)} collective-permute-done((f32[16,1152]{1,0:T(8,128)S(1)}, f32[16,1152]{1,0:T(8,128)S(1)}, u32[]{:S(2)}, u32[]{:S(2)}) %collective-permute-start.22) | collective-permute-done | bytes 73760 | tf_op jit(solution)/shard_map/ppermute | solution.py:285
  47.6 1.3 %collective-permute-start.26 = (f32[16,1152]{1,0:T(8,128)S(1)}, f32[16,1152]{1,0:T(8,128)S(1)}, u32[]{:S(2)}, u32[]{:S(2)}) collective-permute-start(f32[16,1152]{1,0:T(8,128)S(1)} %get-tuple-element.54), channel_id=1, source_target_pairs={{128,193},{129,194},{130,195},{131,196},{132,197},{133,198},{134,1... | collective-permute-start | bytes 221192 | tf_op jit(solution)/shard_map/ppermute | solution.py:363
  48.8 1.3 %collective-permute-start.25 = (f32[16,1152]{1,0:T(8,128)S(1)}, f32[16,1152]{1,0:T(8,128)S(1)}, u32[]{:S(2)}, u32[]{:S(2)}) collective-permute-start(f32[16,1152]{1,0:T(8,128)S(1)} %get-tuple-element.54), channel_id=1, source_target_pairs={{128,192},{129,193},{130,194},{131,195},{132,196},{133,197},{134,1... | collective-permute-start | bytes 221192 | tf_op jit(solution)/shard_map/ppermute | solution.py:363
  50.1 0.7 collective-permute-start.24
  50.8 25.0 %collective-permute-done.26.refs_5_ = f32[16,1152]{1,0:T(8,128)S(1)} collective-permute-done((f32[16,1152]{1,0:T(8,128)S(1)}, f32[16,1152]{1,0:T(8,128)S(1)}, u32[]{:S(2)}, u32[]{:S(2)}) %collective-permute-start.26) | collective-permute-done | bytes 73760 | tf_op jit(solution)/shard_map/ppermute | solution.py:363
  75.8 2.0 %shard_map.85 = (f32[2,16,1152]{2,1,0:T(8,128)S(1)}, f32[16,1152]{1,0:T(8,128)S(1)}, f32[16,1152]{1,0:T(8,128)S(1)}) custom-call(f32[16,1152]{1,0:T(8,128)S(1)} %collective-permute-done.4.refs_0_, f32[16,1152]{1,0:T(8,128)S(1)} %shard_map.76.refs_1_, f32[16,1152]{1,0:T(8,128)S(1)} %collective-permute-done.5.refs_2_, ...), custom_call_target="tpu_custom_call" | custom-call | tf_op jit(solution)/shard_map/pallas_call | solution.py:174
  77.8 7.5 %collective-permute-start.28 = (f32[16,1152]{1,0:T(8,128)S(1)}, f32[16,1152]{1,0:T(8,128)S(1)}, u32[]{:S(2)}, u32[]{:S(2)}) collective-permute-start(f32[16,1152]{1,0:T(8,128)S(1)} %get-tuple-element.56.refs_1_), channel_id=1, source_target_pairs={{0,1},{1,2},{2,3},{3,4},{4,5},{5,6},{6,7},{7,8},{8,9},{9,10},{10,1... | collective-permute-start | bytes 221192 | tf_op jit(solution)/shard_map/ppermute | solution.py:287
  85.4 0.9 collective-permute-done.28.refs_2_
  86.3 1.7 %collective-permute-done.27.refs_0_ = f32[16,1152]{1,0:T(8,128)S(1)} collective-permute-done((f32[16,1152]{1,0:T(8,128)S(1)}, f32[16,1152]{1,0:T(8,128)S(1)}, u32[]{:S(2)}, u32[]{:S(2)}) %collective-permute-start.27) | collective-permute-done | bytes 73760 | tf_op jit(solution)/shard_map/ppermute | solution.py:285
  88.0 2.7 %shard_map.86 = (f32[2,16,1152]{2,1,0:T(8,128)S(1)}, f32[16,1152]{1,0:T(8,128)}) custom-call(f32[16,1152]{1,0:T(8,128)S(1)} %collective-permute-done.27.refs_0_, f32[16,1152]{1,0:T(8,128)S(1)} %get-tuple-element.56.refs_1_, f32[16,1152]{1,0:T(8,128)S(1)} %collective-permute-done.28.refs_2_, f32[64,1152]{1,0:T(8,128)S(1)} %get-tuple-element.34.refs_3_.refs_6_, ...), custom_call_target="tpu_custom_call" | custom-call | tf_op jit(solution)/shard_map/pallas_call | solution.py:174
  90.7 0.7 shard_map.87
  91.3 5.6 %collective-permute-start.29 = (f32[2,16,1024]{2,1,0:T(8,128)S(1)}, f32[2,16,1024]{2,1,0:T(8,128)S(1)}, u32[]{:S(2)}, u32[]{:S(2)}) collective-permute-start(f32[2,16,1024]{2,1,0:T(8,128)S(1)} %get-tuple-element.60), channel_id=1, source_target_pairs={{0,32},{32,0},{64,96},{96,64},{128,160},{160,128},{192,224},{224,1... | collective-permute-start | bytes 393224 | tf_op jit(solution)/shard_map/ppermute | solution.py:372
  97.0 1.0 collective-permute-done.29
  98.0 0.7 maximum_select_fusion.1
  (38 shorter events, 0.3 us)
Async XLA Ops:
  0.0 1.9 %copy-start = (f32[1,2,16,2048]{3,2,1,0:T(8,128)S(1)}, f32[1,2,16,2048]{3,2,1,0:T(8,128)}, u32[]{:S(2)}) copy-start(f32[1,2,16,2048]{3,2,1,0:T(8,128)} %param.7) | copy-start | bytes 786436
  0.0 4.2 %copy-start.4 = (s32[256]{0:T(256)S(1)}, s32[256]{0:T(256)}, u32[]{:S(2)}) copy-start(s32[256]{0:T(256)} %param.10) | copy-start | bytes 3076
  0.0 4.2 %copy-start.3 = (f32[1,2,256]{2,1,0:T(2,128)S(1)}, f32[1,2,256]{2,1,0:T(2,128)}, u32[]{:S(2)}) copy-start(f32[1,2,256]{2,1,0:T(2,128)} %param.9) | copy-start | bytes 6148
  0.0 4.2 %copy-start.5 = (f32[1,2,16,2048]{3,2,1,0:T(8,128)S(1)}, f32[1,2,16,2048]{3,2,1,0:T(8,128)}, u32[]{:S(2)}) copy-start(f32[1,2,16,2048]{3,2,1,0:T(8,128)} %param.8) | copy-start | bytes 786436
  1.1 5.0 %collective-permute-start = (f32[2,16,1152]{2,1,0:T(8,128)S(1)}, f32[2,16,1152]{2,1,0:T(8,128)S(1)}, u32[]{:S(2)}, u32[]{:S(2)}) collective-permute-start(f32[2,16,1152]{2,1,0:T(8,128)S(1)} %slice_select_fusion.2), channel_id=1, source_target_pairs={{0,32},{32,0},{64,96},{96,64},{128,160},{160,128},{192,224},{224,1... | collective-permute-start | bytes 442376 | tf_op jit(solution)/shard_map/ppermute | solution.py:306
  1.9 8.5 %collective-permute-start.7 = (f32[2,16,2048]{2,1,0:T(8,128)S(1)}, f32[2,16,2048]{2,1,0:T(8,128)S(1)}, u32[]{:S(2)}, u32[]{:S(2)}) collective-permute-start(f32[2,16,2048]{2,1,0:T(8,128)S(1)} %bitcast.51), channel_id=1, source_target_pairs={{0,1},{1,2},{2,3},{3,4},{4,5},{5,6},{6,7},{7,8},{8,9},{9,10},{10,1... | collective-permute-start | bytes 786440 | tf_op jit(solution)/shard_map/ppermute | solution.py:287
  2.0 9.7 %collective-permute-start.6 = (f32[2,16,2048]{2,1,0:T(8,128)S(1)}, f32[2,16,2048]{2,1,0:T(8,128)S(1)}, u32[]{:S(2)}, u32[]{:S(2)}) collective-permute-start(f32[2,16,2048]{2,1,0:T(8,128)S(1)} %bitcast.52), channel_id=1, source_target_pairs={{0,32},{1,0},{2,1},{3,2},{4,3},{5,4},{6,5},{7,6},{8,7},{9,8},{10,9... | collective-permute-start | bytes 786440 | tf_op jit(solution)/shard_map/ppermute | solution.py:285
  5.2 0.9 copy-start.1
  5.2 3.4 %collective-permute-start.9 = (f32[40,1152]{1,0:T(8,128)S(1)}, f32[40,1152]{1,0:T(8,128)S(1)}, u32[]{:S(2)}, u32[]{:S(2)}) collective-permute-start(f32[40,1152]{1,0:T(8,128)S(1)} %broadcast_select_fusion), channel_id=1, source_target_pairs={{0,32},{32,0},{64,96},{96,64},{128,160},{160,128},{192,224},{224,1... | collective-permute-start | bytes 552968 | tf_op jit(solution)/shard_map/ppermute | solution.py:306
  6.2 6.1 %collective-permute-start.3 = (f32[16,1152]{1,0:T(8,128)S(1)}, f32[16,1152]{1,0:T(8,128)S(1)}, u32[]{:S(2)}, u32[]{:S(2)}) collective-permute-start(f32[16,1152]{1,0:T(8,128)S(1)} %fusion.9), channel_id=1, source_target_pairs={{0,192},{32,224},{64,128},{96,160},{128,64},{160,96},{192,0},{224,... | collective-permute-start | bytes 221192 | tf_op jit(solution)/shard_map/ppermute | solution.py:316
  8.0 6.0 %collective-permute-start.2 = (f32[16,1152]{1,0:T(8,128)S(1)}, f32[16,1152]{1,0:T(8,128)S(1)}, u32[]{:S(2)}, u32[]{:S(2)}) collective-permute-start(f32[16,1152]{1,0:T(8,128)S(1)} %fusion.9), channel_id=1, source_target_pairs={{0,128},{32,160},{64,192},{96,224},{128,0},{160,32},{192,64},{224,... | collective-permute-start | bytes 221192 | tf_op jit(solution)/shard_map/ppermute | solution.py:316
  8.6 5.4 %collective-permute-start.1 = (f32[16,1152]{1,0:T(8,128)S(1)}, f32[16,1152]{1,0:T(8,128)S(1)}, u32[]{:S(2)}, u32[]{:S(2)}) collective-permute-start(f32[16,1152]{1,0:T(8,128)S(1)} %fusion.9), channel_id=1, source_target_pairs={{0,64},{32,96},{64,0},{96,32},{128,192},{160,224},{192,128},{224,1... | collective-permute-start | bytes 221192 | tf_op jit(solution)/shard_map/ppermute | solution.py:316
  10.4 10.1 %collective-permute-start.11 = (f32[80,1152]{1,0:T(8,128)S(1)}, f32[80,1152]{1,0:T(8,128)S(1)}, u32[]{:S(2)}, u32[]{:S(2)}) collective-permute-start(f32[80,1152]{1,0:T(8,128)S(1)} %get-tuple-element.38.refs_7_.refs_10_), channel_id=1, source_target_pairs={{0,1},{1,2},{2,3},{3,4},{4,5},{5,6},{6,7},{7,8},{8,9},{9,10},{10,1... | collective-permute-start | bytes 1105928 | tf_op jit(solution)/shard_map/ppermute | solution.py:287
  11.7 8.8 %collective-permute-start.10 = (f32[80,1152]{1,0:T(8,128)S(1)}, f32[80,1152]{1,0:T(8,128)S(1)}, u32[]{:S(2)}, u32[]{:S(2)}) collective-permute-start(f32[80,1152]{1,0:T(8,128)S(1)} %get-tuple-element.38.refs_7_.refs_10_), channel_id=1, source_target_pairs={{0,32},{1,0},{2,1},{3,2},{4,3},{5,4},{6,5},{7,6},{8,7},{9,8},{10,9... | collective-permute-start | bytes 1105928 | tf_op jit(solution)/shard_map/ppermute | solution.py:285
  12.3 1.7 %copy-start.2 = (f32[16,2048]{1,0:T(8,128)S(1)}, f32[16,2048]{1,0:T(8,128)}, u32[]{:S(2)}) copy-start(f32[16,2048]{1,0:T(8,128)} %param.12) | copy-start | bytes 393220
  12.3 4.0 %collective-permute-start.8 = (f32[2,2,16,1152]{3,2,1,0:T(8,128)S(1)}, f32[2,2,16,1152]{3,2,1,0:T(8,128)S(1)}, u32[]{:S(2)}, u32[]{:S(2)}) collective-permute-start(f32[2,2,16,1152]{3,2,1,0:T(8,128)S(1)} %maximum_select_fusion), channel_id=1, source_target_pairs={{0,32},{32,0},{64,96},{96,64},{128,160},{160,128},{192,224},{224,1... | collective-permute-start | bytes 884744 | tf_op jit(solution)/shard_map/ppermute | solution.py:343
  14.5 4.7 %collective-permute-start.5 = (f32[16,1152]{1,0:T(8,128)S(1)}, f32[16,1152]{1,0:T(8,128)S(1)}, u32[]{:S(2)}, u32[]{:S(2)}) collective-permute-start(f32[16,1152]{1,0:T(8,128)S(1)} %shard_map.76.refs_1_), channel_id=1, source_target_pairs={{0,1},{1,2},{2,3},{3,4},{4,5},{5,6},{6,7},{7,8},{8,9},{9,10},{10,1... | collective-permute-start | bytes 221192 | tf_op jit(solution)/shard_map/ppermute | solution.py:287
  15.3 5.2 %collective-permute-start.4 = (f32[16,1152]{1,0:T(8,128)S(1)}, f32[16,1152]{1,0:T(8,128)S(1)}, u32[]{:S(2)}, u32[]{:S(2)}) collective-permute-start(f32[16,1152]{1,0:T(8,128)S(1)} %shard_map.76.refs_1_), channel_id=1, source_target_pairs={{0,32},{1,0},{2,1},{3,2},{4,3},{5,4},{6,5},{7,6},{8,7},{9,8},{10,9... | collective-permute-start | bytes 221192 | tf_op jit(solution)/shard_map/ppermute | solution.py:285
  20.5 4.2 %collective-permute-start.13 = (f32[16,1152]{1,0:T(8,128)S(1)}, f32[16,1152]{1,0:T(8,128)S(1)}, u32[]{:S(2)}, u32[]{:S(2)}) collective-permute-start(f32[16,1152]{1,0:T(8,128)S(1)} %get-tuple-element.41.refs_1_), channel_id=1, source_target_pairs={{0,1},{1,2},{2,3},{3,4},{4,5},{5,6},{6,7},{7,8},{8,9},{9,10},{10,1... | collective-permute-start | bytes 221192 | tf_op jit(solution)/shard_map/ppermute | solution.py:287
  23.5 3.3 %collective-permute-start.12 = (f32[16,1152]{1,0:T(8,128)S(1)}, f32[16,1152]{1,0:T(8,128)S(1)}, u32[]{:S(2)}, u32[]{:S(2)}) collective-permute-start(f32[16,1152]{1,0:T(8,128)S(1)} %get-tuple-element.41.refs_1_), channel_id=1, source_target_pairs={{0,32},{1,0},{2,1},{3,2},{4,3},{5,4},{6,5},{7,6},{8,7},{9,8},{10,9... | collective-permute-start | bytes 221192 | tf_op jit(solution)/shard_map/ppermute | solution.py:285
  26.8 2.0 %collective-permute-start.16 = (f32[16,1152]{1,0:T(8,128)S(1)}, f32[16,1152]{1,0:T(8,128)S(1)}, u32[]{:S(2)}, u32[]{:S(2)}) collective-permute-start(f32[16,1152]{1,0:T(8,128)S(1)} %get-tuple-element.44), channel_id=1, source_target_pairs={{0,65},{1,66},{2,67},{3,68},{4,69},{5,70},{6,71},{7,72},{8,73},{9,... | collective-permute-start | bytes 221192 | tf_op jit(solution)/shard_map/ppermute | solution.py:363
  27.5 1.4 %collective-permute-start.15 = (f32[16,1152]{1,0:T(8,128)S(1)}, f32[16,1152]{1,0:T(8,128)S(1)}, u32[]{:S(2)}, u32[]{:S(2)}) collective-permute-start(f32[16,1152]{1,0:T(8,128)S(1)} %get-tuple-element.44), channel_id=1, source_target_pairs={{0,64},{1,65},{2,66},{3,67},{4,68},{5,69},{6,70},{7,71},{8,72},{9,... | collective-permute-start | bytes 221192 | tf_op jit(solution)/shard_map/ppermute | solution.py:363
  28.2 0.7 collective-permute-start.14
  28.9 5.8 %collective-permute-start.18 = (f32[16,1152]{1,0:T(8,128)S(1)}, f32[16,1152]{1,0:T(8,128)S(1)}, u32[]{:S(2)}, u32[]{:S(2)}) collective-permute-start(f32[16,1152]{1,0:T(8,128)S(1)} %get-tuple-element.46.refs_1_), channel_id=1, source_target_pairs={{0,1},{1,2},{2,3},{3,4},{4,5},{5,6},{6,7},{7,8},{8,9},{9,10},{10,1... | collective-permute-start | bytes 221192 | tf_op jit(solution)/shard_map/ppermute | solution.py:287
  33.8 4.4 %collective-permute-start.17 = (f32[16,1152]{1,0:T(8,128)S(1)}, f32[16,1152]{1,0:T(8,128)S(1)}, u32[]{:S(2)}, u32[]{:S(2)}) collective-permute-start(f32[16,1152]{1,0:T(8,128)S(1)} %get-tuple-element.46.refs_1_), channel_id=1, source_target_pairs={{0,32},{1,0},{2,1},{3,2},{4,3},{5,4},{6,5},{7,6},{8,7},{9,8},{10,9... | collective-permute-start | bytes 221192 | tf_op jit(solution)/shard_map/ppermute | solution.py:285
  38.2 2.0 %collective-permute-start.21 = (f32[16,1152]{1,0:T(8,128)S(1)}, f32[16,1152]{1,0:T(8,128)S(1)}, u32[]{:S(2)}, u32[]{:S(2)}) collective-permute-start(f32[16,1152]{1,0:T(8,128)S(1)} %get-tuple-element.49), channel_id=1, source_target_pairs={{64,129},{65,130},{66,131},{67,132},{68,133},{69,134},{70,135},{71... | collective-permute-start | bytes 221192 | tf_op jit(solution)/shard_map/ppermute | solution.py:363
  38.8 1.4 %collective-permute-start.20 = (f32[16,1152]{1,0:T(8,128)S(1)}, f32[16,1152]{1,0:T(8,128)S(1)}, u32[]{:S(2)}, u32[]{:S(2)}) collective-permute-start(f32[16,1152]{1,0:T(8,128)S(1)} %get-tuple-element.49), channel_id=1, source_target_pairs={{64,128},{65,129},{66,130},{67,131},{68,132},{69,133},{70,134},{71... | collective-permute-start | bytes 221192 | tf_op jit(solution)/shard_map/ppermute | solution.py:363
  39.5 0.7 collective-permute-start.19
  40.3 4.6 %collective-permute-start.23 = (f32[16,1152]{1,0:T(8,128)S(1)}, f32[16,1152]{1,0:T(8,128)S(1)}, u32[]{:S(2)}, u32[]{:S(2)}) collective-permute-start(f32[16,1152]{1,0:T(8,128)S(1)} %get-tuple-element.51.refs_1_), channel_id=1, source_target_pairs={{0,1},{1,2},{2,3},{3,4},{4,5},{5,6},{6,7},{7,8},{8,9},{9,10},{10,1... | collective-permute-start | bytes 221192 | tf_op jit(solution)/shard_map/ppermute | solution.py:287
  43.9 3.6 %collective-permute-start.22 = (f32[16,1152]{1,0:T(8,128)S(1)}, f32[16,1152]{1,0:T(8,128)S(1)}, u32[]{:S(2)}, u32[]{:S(2)}) collective-permute-start(f32[16,1152]{1,0:T(8,128)S(1)} %get-tuple-element.51.refs_1_), channel_id=1, source_target_pairs={{0,32},{1,0},{2,1},{3,2},{4,3},{5,4},{6,5},{7,6},{8,7},{9,8},{10,9... | collective-permute-start | bytes 221192 | tf_op jit(solution)/shard_map/ppermute | solution.py:285
  47.6 28.2 %collective-permute-start.26 = (f32[16,1152]{1,0:T(8,128)S(1)}, f32[16,1152]{1,0:T(8,128)S(1)}, u32[]{:S(2)}, u32[]{:S(2)}) collective-permute-start(f32[16,1152]{1,0:T(8,128)S(1)} %get-tuple-element.54), channel_id=1, source_target_pairs={{128,193},{129,194},{130,195},{131,196},{132,197},{133,198},{134,1... | collective-permute-start | bytes 221192 | tf_op jit(solution)/shard_map/ppermute | solution.py:363
  48.8 26.9 %collective-permute-start.25 = (f32[16,1152]{1,0:T(8,128)S(1)}, f32[16,1152]{1,0:T(8,128)S(1)}, u32[]{:S(2)}, u32[]{:S(2)}) collective-permute-start(f32[16,1152]{1,0:T(8,128)S(1)} %get-tuple-element.54), channel_id=1, source_target_pairs={{128,192},{129,193},{130,194},{131,195},{132,196},{133,197},{134,1... | collective-permute-start | bytes 221192 | tf_op jit(solution)/shard_map/ppermute | solution.py:363
  50.1 25.6 %collective-permute-start.24 = (f32[16,1152]{1,0:T(8,128)S(1)}, f32[16,1152]{1,0:T(8,128)S(1)}, u32[]{:S(2)}, u32[]{:S(2)}) collective-permute-start(f32[16,1152]{1,0:T(8,128)S(1)} %get-tuple-element.54), channel_id=1, source_target_pairs={{129,192},{130,193},{131,194},{132,195},{133,196},{134,197},{135,1... | collective-permute-start | bytes 221192 | tf_op jit(solution)/shard_map/ppermute | solution.py:363
  77.8 8.4 %collective-permute-start.28 = (f32[16,1152]{1,0:T(8,128)S(1)}, f32[16,1152]{1,0:T(8,128)S(1)}, u32[]{:S(2)}, u32[]{:S(2)}) collective-permute-start(f32[16,1152]{1,0:T(8,128)S(1)} %get-tuple-element.56.refs_1_), channel_id=1, source_target_pairs={{0,1},{1,2},{2,3},{3,4},{4,5},{5,6},{6,7},{7,8},{8,9},{9,10},{10,1... | collective-permute-start | bytes 221192 | tf_op jit(solution)/shard_map/ppermute | solution.py:287
  85.4 2.6 %collective-permute-start.27 = (f32[16,1152]{1,0:T(8,128)S(1)}, f32[16,1152]{1,0:T(8,128)S(1)}, u32[]{:S(2)}, u32[]{:S(2)}) collective-permute-start(f32[16,1152]{1,0:T(8,128)S(1)} %get-tuple-element.56.refs_1_), channel_id=1, source_target_pairs={{0,32},{1,0},{2,1},{3,2},{4,3},{5,4},{6,5},{7,6},{8,7},{9,8},{10,9... | collective-permute-start | bytes 221192 | tf_op jit(solution)/shard_map/ppermute | solution.py:285
  91.3 6.6 %collective-permute-start.29 = (f32[2,16,1024]{2,1,0:T(8,128)S(1)}, f32[2,16,1024]{2,1,0:T(8,128)S(1)}, u32[]{:S(2)}, u32[]{:S(2)}) collective-permute-start(f32[2,16,1024]{2,1,0:T(8,128)S(1)} %get-tuple-element.60), channel_id=1, source_target_pairs={{0,32},{32,0},{64,96},{96,64},{128,160},{160,128},{192,224},{224,1... | collective-permute-start | bytes 393224 | tf_op jit(solution)/shard_map/ppermute | solution.py:372
